TPU v7x, 256 devices: a whole 4x4x8 slice. The times are simulated.
256 devices in a mesh: section: 2 (over z_hi), dp: 32 (over x, z_lo, core), mp: 4 (over y).
Axes of the slice: x: 4, y: 4, z: 8 (z_hi: 2, z_lo: 4; z = z_hi * 4 + z_lo), core: 2. Of those that a mesh axis runs over, the one named last changes fastest.
Arguments:
- train_acts: bfloat16 [2, 4096, 4096], P('section', 'dp', 'mp'), may hold values from -6 to 6
- train_grads: bfloat16 [2, 4096, 14336], P('section', 'dp', 'mp'), may hold values from -6 to 6
- basis_in: bfloat16 [2, 4096, 512], P('section', 'mp'), may hold values from -0.25 to 0.25
- basis_out: bfloat16 [2, 14336, 512], P('section', 'mp'), may hold values from -0.25 to 0.25
- eigen_values: float32 [2, 4, 3584, 4096], P('section', None, 'dp', 'mp'), may hold values from 0.01 to 10
- query_acts: bfloat16 [2, 32, 32, 4096], P('section', 'dp', None, 'mp'), may hold values from -6 to 6
- query_grads: bfloat16 [2, 32, 32, 14336], P('section', 'dp', None, 'mp'), may hold values from -6 to 6
- query_owner: int32 [8], replicated, may hold values from 0 to 31, as said below
Outputs:
- influence: float32 [32, 8], P('dp')
Inputs may be any that keep to these rules, and one draw needn't show every extreme that they name: `query_owner`: distinct slot numbers; slot s lies on index s // 1 of dp; slots that no query names hold unused data.
All inputs are finite; a program needn't handle non-finite values.
Results may differ from a plain program's by a relative error of at most 0.0056.
Values may be sent and summed in bfloat16 or wider, within the bound.
No kernel may reach another device: no remote copies, remote signals or barrier semaphores. Data moves between devices by JAX's collectives and lax.ppermute only.
A program may use at most 128 MiB of HBM per device.

v0:
```python
import math

import jax
import jax.numpy as jnp
from jax import lax
from jax.sharding import PartitionSpec as P

SEQLEN = 128


DAMPING = 0.1


def broadcast(block, axis, owner):
    block = jnp.where(lax.axis_index(axis) == owner, block, jnp.zeros_like(block))
    return lax.psum(block, axis)


def rotate(values, eigen_basis, block_size):
    row_count = values.shape[0]
    blocks = eigen_basis.shape[0] // block_size
    shaped = values.reshape(row_count, blocks, block_size)
    factor = eigen_basis.reshape(blocks, block_size, block_size)
    turned = jnp.einsum("rbk,bkc->rbc", shaped, factor, preferred_element_type=jnp.float32)
    return turned.reshape(row_count, blocks * block_size).astype(jnp.bfloat16)


def per_device(
    train_acts, train_grads, basis_in, basis_out, eigen_values, query_acts, query_grads, query_owner
):
    block_size = basis_in.shape[2]
    tok_rows = train_acts.shape[1]
    act_cols = train_acts.shape[2]
    grad_cols = train_grads.shape[2]
    slot_count = query_acts.shape[1]
    query_len = query_acts.shape[2]
    query_total = query_owner.shape[0]
    data_size = lax.axis_size("dp")
    model_size = lax.axis_size("mp")
    data_index = lax.axis_index("dp")
    piece_cols = grad_cols // data_size
    total_seqs = tok_rows * data_size // SEQLEN
    seq_block = math.gcd(total_seqs, 8)
    block_count = total_seqs // seq_block
    turned_acts = rotate(train_acts[0], basis_in[0], block_size)
    turned_grads = rotate(train_grads[0], basis_out[0], block_size)
    slot_acts = rotate(
        query_acts[0].reshape(slot_count * query_len, act_cols), basis_in[0], block_size
    ).reshape(slot_count, query_len, act_cols)
    slot_grads = rotate(
        query_grads[0].reshape(slot_count * query_len, grad_cols), basis_out[0], block_size
    ).reshape(slot_count, query_len, grad_cols)
    packed_slots = jnp.concatenate([slot_acts, slot_grads], axis=2)

    def fetch(position):
        owner_slot = query_owner[position]
        root_index = owner_slot // slot_count
        local_slot = owner_slot % slot_count
        packed = lax.dynamic_index_in_dim(packed_slots, local_slot, 0, keepdims=False)
        return broadcast(packed, "dp", root_index)

    fetched = jnp.stack([fetch(position) for position in range(query_total)])
    chosen_acts = fetched[:, :, :act_cols]
    query_piece = lax.dynamic_slice_in_dim(
        fetched[:, :, act_cols:], data_index * piece_cols, piece_cols, 2
    )
    split_grads = turned_grads.reshape(tok_rows, data_size, piece_cols)
    moved_cols = lax.all_to_all(split_grads, "dp", split_axis=1, concat_axis=0, tiled=True)
    train_cols = lax.all_gather(
        moved_cols.reshape(tok_rows * data_size, piece_cols), "mp", axis=1, tiled=True
    )
    query_cols = lax.all_gather(query_piece, "mp", axis=2, tiled=True)
    all_acts = lax.all_gather(turned_acts, "dp", axis=0, tiled=True)
    local_values = eigen_values[0].reshape(model_size * piece_cols, act_cols)
    moments = jnp.einsum(
        "qsk,qsj->qkj", query_cols, chosen_acts, preferred_element_type=jnp.float32
    )
    weighted = (moments / (local_values + DAMPING)).astype(jnp.bfloat16)
    seq_acts = all_acts.reshape(total_seqs, SEQLEN, act_cols)
    seq_grads = train_cols.reshape(total_seqs, SEQLEN, model_size * piece_cols)

    def add_block(block_index, layer_acc):
        start = block_index * seq_block
        acts_block = lax.dynamic_slice_in_dim(seq_acts, start, seq_block, 0)
        grads_block = lax.dynamic_slice_in_dim(seq_grads, start, seq_block, 0)
        gram_block = jnp.einsum(
            "itk,itj->ikj", grads_block, acts_block, preferred_element_type=jnp.float32
        ).astype(jnp.bfloat16)
        block_scores = jnp.einsum(
            "ikj,qkj->iq", gram_block, weighted, preferred_element_type=jnp.float32
        )
        return lax.dynamic_update_slice_in_dim(layer_acc, block_scores, start, 0)

    layer_part = lax.fori_loop(
        0, block_count, add_block, jnp.zeros((total_seqs, query_total), jnp.float32)
    )
    summed = lax.psum(layer_part, ("section", "dp", "mp"))
    layer_total = train_acts.shape[0] * lax.axis_size("section")
    normalizer = math.sqrt(
        layer_total * act_cols * model_size * grad_cols * model_size * SEQLEN * query_len
    )
    own_count = total_seqs // data_size
    own_rows = lax.dynamic_slice_in_dim(summed, data_index * own_count, own_count, 0)
    return own_rows / normalizer


def solution(mesh):
    in_specs = (
        P("section", "dp", "mp"),
        P("section", "dp", "mp"),
        P("section", "mp", None),
        P("section", "mp", None),
        P("section", None, "dp", "mp"),
        P("section", "dp", None, "mp"),
        P("section", "dp", None, "mp"),
        P(),
    )
    out_specs = P("dp", None)
    return jax.shard_map(
        per_device, mesh=mesh, in_specs=in_specs, out_specs=out_specs, check_vma=False
    )
```

profile of v0, /device:TPU:1, one launch (start us, length us, event | category | flops | bytes accessed | tf_op | source)
XLA Modules:
  0.0 510.4 jit_solution(4394906761280477485)
XLA Ops:
  7.4 0.0 copy-start
  7.4 0.0 all-reduce.3.cloned.1.call-start
  7.4 1.6 fusion.18
  14.0 0.9 reshape_reshape_squeeze.6
  14.9 0.0 copy-done
  14.9 0.3 fusion.12
  15.2 0.1 copy.41
  15.3 1.2 reshape_reshape_squeeze.7
  16.6 2.6 fusion.11
  19.2 0.1 copy.43
  19.3 0.3 convert_element_type.72
  19.7 0.0 copy-start.3
  19.7 1.4 broadcast_select_fusion
  21.1 0.0 all-reduce.3.cloned.1.call-update
  21.2 0.0 all-gather.3.cloned.1.call-start
  21.2 0.2 copy-done.3
  21.4 0.6 copy.33
  22.0 3.3 convolution_convert_fusion.1
  25.3 40.3 %all_to_all.15 = bf16[128,32,112]{0,2,1:T(8,128)(2,1)S(1)} all-to-all(bf16[128,32,112]{0,2,1:T(8,128)(2,1)S(1)} %bitcast.66), channel_id=1, replica_groups=mesh['section'=2,'dp'=32,'mp'=4] {'dp'}, dimensions={1} | all-to-all | bytes 1835008 | tf_op jit(solution)/shard_map/all_to_all | solution.py:68
  65.6 0.0 copy-start.8
  65.6 0.2 copy.36
  65.8 0.0 copy-start.2
  65.9 1.3 copy.74
  67.2 0.0 all-gather.3.cloned.1.call-update
  67.2 0.0 all-gather.5.cloned.1.call-start
  67.3 0.0 copy-done.8
  67.3 0.2 reshape_squeeze.18
  67.4 1.2 convolution_convert_fusion.2
  68.7 0.0 all-gather.5.cloned.1.call-update
  68.7 0.0 copy-done.2
  68.7 1.5 broadcast_add_fusion
  70.2 250.0 %all-reduce.3.cloned.1.call-done = (bf16[1,32,4608]{2,1,0:T(8,128)(2,1)}, bf16[1,32,4608]{2,1,0:T(8,128)(2,1)}, bf16[1,32,4608]{2,1,0:T(8,128)(2,1)}, bf16[1,32,...) async-done(((bf16[1,32,4608]{2,1,0:T(8,128)(2,1)}, ...) | async-done | bytes 2359312 | tf_op jit(solution)/shard_map/psum | solution.py:16
  320.2 1.1 constant_dynamic-update-slice_fusion.9
  321.3 1.0 constant_dynamic-update-slice_fusion.8
  322.3 1.0 constant_dynamic-update-slice_fusion.7
  323.3 1.0 constant_dynamic-update-slice_fusion.6
  324.2 0.0 copy-done.7
  324.3 0.0 copy-done.6
  324.3 0.0 copy-done.5
  324.4 0.0 copy-done.4
  324.4 0.2 slice.40
  324.6 0.1 constant_dynamic-slice_fusion.1
  324.7 0.9 copy.44
  325.5 13.7 %all_gather.11 = bf16[8,32,448]{1,0,2:T(8,128)(2,1)S(1)} all-gather(bf16[8,32,112]{1,0,2:T(8,128)(2,1)} %copy.44), channel_id=1, replica_groups=mesh['section'=2,'dp'=32,'mp'=4] {'mp'}, dimensions={2}, use_global_device_ids=true | all-gather | bytes 286720 | tf_op jit(solution)/shard_map/all_gather | solution.py:72
  339.2 3.4 divide_convert_fusion
  342.6 7.1 %copy.47 = bf16[8,448,1024]{2,0,1:T(8,128)(2,1)} copy(bf16[8,448,1024]{2,1,0:T(8,128)(2,1)S(1)} %divide_convert_fusion) | data formatting | bytes 14680064 | tf_op jit(solution)/shard_map/while | solution.py:94
  349.7 5.0 copy.56
  354.7 11.9 %copy.39 = bf16[4096,1024]{1,0:T(8,128)(2,1)} copy(bf16[4096,1024]{0,1:T(8,128)(2,1)} %all-gather.5.cloned.1.call-done) | data formatting | bytes 16777216 | tf_op jit(solution)/shard_map/all_gather | solution.py:73
  366.7 57.0 %while.13 = (s32[]{:T(128)}, f32[32,8]{1,0:T(8,128)S(1)}, bf16[32,128,448]{1,0,2:T(8,128)(2,1)}, bf16[32,128,1024]{2,1,0:T(8,128)(2,1)}, bf16[8,448,1024]{2,0,1:...) while((s32[]{:T(128)}, f32[32,8]{1,0:T(8,128)S(1)}, bf16[32,128,448]{1,0,2:T(8,128)(2,1)}, ...), condition=%wide.region_9.10_spmd, body=%wide.region_8.9_spmd.sunk | while | flops 1001914368 | bytes 26874008 | solution.py:94
  366.7 1.2 constant_dynamic-slice_fusion.3
  367.9 3.7 convolution_convert_fusion.6
  371.6 9.3 %fusion.34 = f32[32,8]{1,0:T(8,128)S(1)} fusion(f32[32,8]{1,0:T(8,128)S(1)} %get-tuple-element.190, s32[]{:T(128)S(6)} %select_n.169, bf16[8,448,1024]{2,0,1:T(8,128)(2,1)} %get-tuple-element.202, bf16[8,448,1024]{2,1,0:T(8,128)(2,1)S(1)} %convolution_convert_fusion.6), kind=kOutput, calls=%fused_computation.5.clone.1 | convolution fusion | flops 58720256 | bytes 14684164 | tf_op jit(solution)/shard_map/while/body/eval_jaxpr/ikj,qkj->iq/dot_general | solution.py:89
  380.9 1.3 constant_dynamic-slice_fusion.3
  382.1 3.7 convolution_convert_fusion.6
  385.8 9.3 %fusion.34 = f32[32,8]{1,0:T(8,128)S(1)} fusion(f32[32,8]{1,0:T(8,128)S(1)} %get-tuple-element.190, s32[]{:T(128)S(6)} %select_n.169, bf16[8,448,1024]{2,0,1:T(8,128)(2,1)} %get-tuple-element.202, bf16[8,448,1024]{2,1,0:T(8,128)(2,1)S(1)} %convolution_convert_fusion.6), kind=kOutput, calls=%fused_computation.5.clone.1 | convolution fusion | flops 58720256 | bytes 14684164 | tf_op jit(solution)/shard_map/while/body/eval_jaxpr/ikj,qkj->iq/dot_general | solution.py:89
  395.1 1.3 constant_dynamic-slice_fusion.3
  396.4 3.7 convolution_convert_fusion.6
  400.1 9.3 %fusion.34 = f32[32,8]{1,0:T(8,128)S(1)} fusion(f32[32,8]{1,0:T(8,128)S(1)} %get-tuple-element.190, s32[]{:T(128)S(6)} %select_n.169, bf16[8,448,1024]{2,0,1:T(8,128)(2,1)} %get-tuple-element.202, bf16[8,448,1024]{2,1,0:T(8,128)(2,1)S(1)} %convolution_convert_fusion.6), kind=kOutput, calls=%fused_computation.5.clone.1 | convolution fusion | flops 58720256 | bytes 14684164 | tf_op jit(solution)/shard_map/while/body/eval_jaxpr/ikj,qkj->iq/dot_general | solution.py:89
  409.4 1.3 constant_dynamic-slice_fusion.3
  410.6 3.7 convolution_convert_fusion.6
  414.3 9.3 %fusion.34 = f32[32,8]{1,0:T(8,128)S(1)} fusion(f32[32,8]{1,0:T(8,128)S(1)} %get-tuple-element.190, s32[]{:T(128)S(6)} %select_n.169, bf16[8,448,1024]{2,0,1:T(8,128)(2,1)} %get-tuple-element.202, bf16[8,448,1024]{2,1,0:T(8,128)(2,1)S(1)} %convolution_convert_fusion.6), kind=kOutput, calls=%fused_computation.5.clone.1 | convolution fusion | flops 58720256 | bytes 14684164 | tf_op jit(solution)/shard_map/while/body/eval_jaxpr/ikj,qkj->iq/dot_general | solution.py:89
  423.6 78.8 %psum.71 = f32[32,8]{1,0:T(8,128)S(1)} all-reduce(f32[32,8]{1,0:T(8,128)S(1)} %get-tuple-element.99), channel_id=1, replica_groups=mesh['section'=2,'dp'=32,'mp'=4] {'section','dp','mp'}, use_global_device_ids=true, to_apply=%region_10.11 | all-reduce | flops 256 | bytes 2048 | tf_op jit(solution)/shard_map/psum | solution.py:97
  502.4 0.5 dynamic-slice_multiply_fusion
  503.0 0.0 copy-done.1
  (15 shorter events, 0.2 us)
Async XLA Ops:
  7.4 7.5 %copy-start = (bf16[1,1024,512]{2,1,0:T(8,128)(2,1)S(1)}, bf16[1,1024,512]{2,1,0:T(8,128)(2,1)}, u32[]{:S(2)}) copy-start(bf16[1,1024,512]{2,1,0:T(8,128)(2,1)} %param.12) | copy-start | bytes 3145732
  7.4 312.8 %all-reduce.3.cloned.1.call-start = ((), (), s32[]{:S(2)}) async-start(), calls=%async_computation.3 | async-start | bytes 4718592 | tf_op jit(solution)/shard_map/psum | solution.py:16
  19.7 1.7 copy-start.3
  21.2 328.6 %all-gather.3.cloned.1.call-start = ((), (), s32[]{:S(2)}) async-start(), calls=%async_computation.1 | async-start | bytes 4587520 | tf_op jit(solution)/shard_map/all_gather | solution.py:69
  65.6 1.7 copy-start.8
  65.8 2.9 copy-start.2
  67.2 287.5 %all-gather.5.cloned.1.call-start = ((), (), s32[]{:S(2)}) async-start(), calls=%async_computation.2 | async-start | bytes 8650752 | tf_op jit(solution)/shard_map/all_gather | solution.py:73
  320.2 4.0 copy-start.7
  320.2 4.1 copy-start.6
  320.2 4.1 copy-start.5
  320.2 4.2 copy-start.4
  423.6 79.3 %copy-start.1 = (bf16[1,1024,512]{2,1,0:T(8,128)(2,1)S(1)}, bf16[1,1024,512]{2,1,0:T(8,128)(2,1)}, u32[]{:S(2)}) copy-start(bf16[1,1024,512]{2,1,0:T(8,128)(2,1)} %param.12) | copy-start | bytes 3145732
Sparse Core Ops, SparseCore 0:
  21.3 298.8 all-reduce.2
Sparse Core Ops, SparseCore 1:
  67.3 44.8 all-gather.2
  113.8 90.5 all-gather.4
where the time goes:
time: 512 us; the launch traced here: 510 us
  waiting for transfers between devices  250 us (49%)
  blocking collectives  133 us (26%)
  matrix products  62.8 us (12%)
  local copies, waits for them, and re-layouts  41.1 us (8%)
  between operations  20.1 us (4%)
    psum x1, waiting for transfers between devices, broadcast(): return lax.psum(block, axis)  250 us
    psum x1, blocking collectives, per_device(): summed = lax.psum(layer_part, ('section', 'dp', 'mp'))  78.8 us
    all_to_all x1, blocking collectives, per_device(): lax.all_to_all(split_grads, 'dp', split_axis=1, concat_axis=0, tiled=True)  40.3 us
    dot_general x4, matrix products, add_block(): jnp.einsum('ikj,qkj->iq', gram_block, weighted, preferred_element_type=jn...  37.3 us
    dot_general x4, matrix products, add_block(): jnp.einsum('itk,itj->ikj', grads_block, acts_block, preferred_element_typ...  14.6 us
    all_gather x1, blocking collectives, per_device(): query_cols = lax.all_gather(query_piece, 'mp', axis=2, tiled=True)  13.7 us
    all_gather x1, local copies, waits for them, and re-layouts, per_device(): all_acts = lax.all_gather(turned_acts, 'dp', axis=0, tiled=True)  11.9 us
    unnamed x29, local copies, waits for them, and re-layouts  11.2 us
  transfers between devices with their start and end apart: 3, of which 1 were waited for; matrix products, arithmetic and copies ran while one was open for 6% of the time, Pallas kernels for 0%

commit v1 on v0

v1 whole, which is shorter than its diff:
```python
import functools
import math

import jax
import jax.numpy as jnp
from jax import lax
from jax.experimental import pallas as pl
from jax.experimental.pallas import tpu as pltpu
from jax.sharding import PartitionSpec as P

SEQLEN = 128
DAMPING = 0.1
ROWS = 16
CHUNK = 4
MIB = 1 << 20


def turn_acts_kernel(train_ref, query_ref, basis_ref, out_ref):
    size = basis_ref.shape[1]
    for b in range(train_ref.shape[1] // size):
        cols = slice(b * size, (b + 1) * size)
        rows = jnp.concatenate([train_ref[:, cols], query_ref[:, cols]], axis=0)
        out_ref[:, cols] = jnp.dot(
            rows, basis_ref[cols, :], preferred_element_type=jnp.float32
        ).astype(jnp.bfloat16)


def turn_grads_kernel(train_ref, query_ref, basis_ref, out_ref, turned, slots):
    step = pl.program_id(0)
    steps = pl.num_programs(0)
    size = basis_ref.shape[1]
    tokens = train_ref.shape[0]
    rows = jnp.concatenate([train_ref[...], query_ref[...]], axis=0)
    product = jnp.dot(rows, basis_ref[...], preferred_element_type=jnp.float32)
    turned[step] = product[:tokens].T.astype(jnp.bfloat16)
    slots[step] = product[tokens:]

    @pl.when(step == steps - 1)
    def _():
        pieces, _, lanes = out_ref.shape
        total = turned.shape[0] * size
        piece = total // pieces
        for d in range(pieces):
            start = d * piece
            parts = []
            at = start
            while at < start + piece:
                block = at // size
                end = min(start + piece, (block + 1) * size)
                parts.append(turned[block, at - block * size : end - block * size, :])
                at = end
            out_ref[d, :piece, :] = parts[0] if len(parts) == 1 else jnp.concatenate(parts, axis=0)
            first = start // lanes
            tiles = []
            for tile in range(first, min(first + 2, total // lanes)):
                col = tile * lanes
                block = col // size
                tiles.append(slots[block, :, col - block * size : col - block * size + lanes])
            window = jnp.concatenate(tiles, axis=1) if len(tiles) > 1 else tiles[0]
            shift = start - first * lanes
            if shift:
                window = pltpu.roll(window, window.shape[1] - shift, 1)
            out_ref[d, piece:, :] = window[:, :lanes].astype(jnp.bfloat16)


def weigh_kernel(order_ref, owner_ref, grads_ref, *refs):
    queries = owner_ref.shape[0]
    slot_refs = refs[:queries]
    lambda_ref, out_ref, acts = refs[queries:]
    length = slot_refs[0].shape[1]

    @pl.when(pl.program_id(0) == 0)
    def _():
        for q in range(queries):
            acts[q * length : (q + 1) * length, :] = slot_refs[q][0]

    turned = grads_ref[0].astype(jnp.float32).T.astype(jnp.bfloat16)
    shape = (queries * ROWS, queries * length)
    own = (
        lax.broadcasted_iota(jnp.int32, shape, 0) // ROWS
        == lax.broadcasted_iota(jnp.int32, shape, 1) // length
    )
    for b in range(lambda_ref.shape[1] // ROWS):
        rows = slice(b * ROWS, (b + 1) * ROWS)
        spread = jnp.concatenate([turned[rows].astype(jnp.float32)] * queries, axis=0)
        spread = jnp.where(own, spread, 0.0).astype(jnp.bfloat16)
        moments = jnp.dot(spread, acts[...], preferred_element_type=jnp.float32)
        inverse = 1.0 / (lambda_ref[0, rows, :] + DAMPING)
        moments = moments.reshape(queries, ROWS, moments.shape[1]) * inverse[None]
        out_ref[0, b] = moments.reshape(queries * ROWS, moments.shape[2]).astype(jnp.bfloat16)


def score_kernel(grads_ref, acts_ref, weighted_ref, out_ref, grams):
    step = pl.program_id(0)
    steps = pl.num_programs(0)
    blocks = weighted_ref.shape[1]
    for i in range(CHUNK):
        gram = jnp.dot(grads_ref[i], acts_ref[i], preferred_element_type=jnp.float32)
        gram = gram.astype(jnp.bfloat16)
        start = pl.multiple_of((step * CHUNK + i) * ROWS, ROWS)
        for b in range(blocks):
            grams[b, pl.ds(start, ROWS), :] = gram[b * ROWS : (b + 1) * ROWS]

    @pl.when(step == steps - 1)
    def _():
        total = jnp.zeros((grams.shape[1], weighted_ref.shape[2]), jnp.float32)
        for b in range(blocks):
            total += lax.dot_general(
                grams[b],
                weighted_ref[0, b],
                (((1,), (1,)), ((), ())),
                preferred_element_type=jnp.float32,
            )
        same = (
            lax.broadcasted_iota(jnp.int32, total.shape, 0) % ROWS
            == lax.broadcasted_iota(jnp.int32, total.shape, 1) % ROWS
        )
        total = jnp.where(same, total, 0.0)
        out_ref[...] = jnp.sum(total.reshape(-1, ROWS, total.shape[1]), axis=1)


def per_device(
    train_acts, train_grads, basis_in, basis_out, eigen_values, query_acts, query_grads, query_owner
):
    block_size = basis_in.shape[2]
    tokens, act_cols = train_acts.shape[1:]
    grad_cols = train_grads.shape[2]
    length = query_acts.shape[2]
    queries = query_owner.shape[0]
    data_size = lax.axis_size("dp")
    model_size = lax.axis_size("mp")
    piece = grad_cols // data_size
    sequences = data_size * tokens // SEQLEN
    bf16 = jnp.bfloat16

    turned_acts = pl.pallas_call(
        turn_acts_kernel,
        out_shape=jax.ShapeDtypeStruct((tokens + length, act_cols), bf16),
        compiler_params=pltpu.CompilerParams(vmem_limit_bytes=24 * MIB),
        name="turn_acts",
    )(train_acts[0], query_acts[0, 0], basis_in[0])
    all_acts = lax.all_gather(turned_acts, "dp", axis=0)

    steps = grad_cols // block_size
    pieces = pl.pallas_call(
        turn_grads_kernel,
        grid=(steps,),
        in_specs=[
            pl.BlockSpec((tokens, block_size), lambda s: (0, s)),
            pl.BlockSpec((length, block_size), lambda s: (0, s)),
            pl.BlockSpec((block_size, block_size), lambda s: (s, 0)),
        ],
        out_specs=pl.BlockSpec((data_size, piece + length, tokens), lambda s: (0, 0, 0)),
        out_shape=jax.ShapeDtypeStruct((data_size, piece + length, tokens), bf16),
        scratch_shapes=[
            pltpu.VMEM((steps, block_size, tokens), bf16),
            pltpu.VMEM((steps, length, block_size), jnp.float32),
        ],
        compiler_params=pltpu.CompilerParams(vmem_limit_bytes=24 * MIB),
        name="turn_grads",
    )(train_grads[0], query_grads[0, 0], basis_out[0])
    moved = lax.all_to_all(pieces, "dp", split_axis=0, concat_axis=0, tiled=True)
    own_grads = moved[:, :piece]
    own_query = jnp.take(moved[:, piece:], query_owner, axis=0).reshape(queries * length, tokens)

    ring = range(model_size)
    shifts = [[(i, (i + s) % model_size) for i in ring] for s in (1, model_size - 1, 2)]
    query_parts = [own_query] + [lax.ppermute(own_query, "mp", pairs) for pairs in shifts]
    grad_parts = [own_grads] + [lax.ppermute(own_grads, "mp", pairs) for pairs in shifts]
    model_index = lax.axis_index("mp")
    order = jnp.stack([(model_index + s) % model_size for s in (0, model_size - 1, 1, 2)])
    order = order.astype(jnp.int32)

    blocks = piece // ROWS
    slot_specs = [
        pl.BlockSpec((1, length, act_cols), functools.partial(
            lambda q, s, order, owner: (owner[q], tokens // length, 0), q))
        for q in range(queries)
    ]
    weighted = pl.pallas_call(
        weigh_kernel,
        grid_spec=pltpu.PrefetchScalarGridSpec(
            num_scalar_prefetch=2,
            grid=(model_size,),
            in_specs=[
                pl.BlockSpec((1, queries * length, tokens), lambda s, order, owner: (s, 0, 0)),
                *slot_specs,
                pl.BlockSpec((1, piece, act_cols), lambda s, order, owner: (order[s], 0, 0)),
            ],
            out_specs=pl.BlockSpec(
                (1, blocks, queries * ROWS, act_cols), lambda s, order, owner: (s, 0, 0, 0)
            ),
            scratch_shapes=[pltpu.VMEM((queries * length, act_cols), bf16)],
        ),
        out_shape=jax.ShapeDtypeStruct((model_size, blocks, queries * ROWS, act_cols), bf16),
        compiler_params=pltpu.CompilerParams(vmem_limit_bytes=32 * MIB),
        name="weigh",
    )(order, query_owner, jnp.stack(query_parts), *([all_acts] * queries), eigen_values[0])

    def score(part, grads):
        return pl.pallas_call(
            score_kernel,
            grid=(sequences // CHUNK,),
            in_specs=[
                pl.BlockSpec((CHUNK, piece, tokens), lambda s: (s, 0, 0)),
                pl.BlockSpec((CHUNK, tokens, act_cols), lambda s: (s, 0, 0)),
                pl.BlockSpec(
                    (1, blocks, queries * ROWS, act_cols), lambda s: (part, 0, 0, 0)
                ),
            ],
            out_specs=pl.BlockSpec((sequences, queries * ROWS), lambda s: (0, 0)),
            out_shape=jax.ShapeDtypeStruct((sequences, queries * ROWS), jnp.float32),
            scratch_shapes=[pltpu.VMEM((blocks, sequences * ROWS, act_cols), bf16)],
            compiler_params=pltpu.CompilerParams(vmem_limit_bytes=40 * MIB),
            name="score",
        )(grads, all_acts, weighted)

    scores = sum(score(part, grads) for part, grads in enumerate(grad_parts))
    partial = scores.reshape(sequences, queries, ROWS).sum(axis=2)

    mine = lax.all_to_all(partial, "dp", split_axis=0, concat_axis=0, tiled=True).sum(axis=0)
    others = model_size * lax.axis_size("section")
    spread = jnp.broadcast_to(mine[None], (others, queries))
    gathered = lax.all_to_all(spread, ("section", "mp"), split_axis=0, concat_axis=0, tiled=True)
    layers = train_acts.shape[0] * lax.axis_size("section")
    normalizer = math.sqrt(
        layers * act_cols * model_size * grad_cols * model_size * SEQLEN * length
    )
    return gathered.sum(axis=0, keepdims=True) / normalizer


def solution(mesh):
    in_specs = (
        P("section", "dp", "mp"),
        P("section", "dp", "mp"),
        P("section", "mp", None),
        P("section", "mp", None),
        P("section", None, "dp", "mp"),
        P("section", "dp", None, "mp"),
        P("section", "dp", None, "mp"),
        P(),
    )
    return jax.shard_map(
        per_device, mesh=mesh, in_specs=in_specs, out_specs=P("dp", None), check_vma=False
    )
```

time: 512 us -> 202 us (0.39)
  waiting for transfers between devices: 250 us -> 72.7 us
  blocking collectives: 133 us -> 33.2 us
  matrix products: 62.8 us -> 0 us
  Pallas kernels: 0 us -> 45.6 us
  local copies, waits for them, and re-layouts: 41.1 us -> 14.3 us
  starting transfers between devices: 0.09 us -> 21 us
  between operations: 20.1 us -> 13.6 us
    psum x1 -> x0, waiting for transfers between devices: 250 us -> none  [broadcast(): return lax.psum(block, axis)]
    psum x1 -> x0, blocking collectives: 78.8 us -> none  [per_device(): summed = lax.psum(layer_part, ('section', 'dp', 'mp'))]
    dot_general x13 -> x0, matrix products: 62.8 us -> none  [the longest x4 37.3 us: add_block(): jnp.einsum('ikj,qkj->iq', gram_block, weighted, preferred_element_type=jn...]
    pallas_call x0 -> x7, Pallas kernels: none -> 45.6 us  [the longest x4 37.4 us: score(): pl.pallas_call(score_kernel, grid=(sequences // CHUNK,), in_specs=[pl.Blo...]
    all_to_all x0 -> x1, waiting for transfers between devices: none -> 42.3 us  [per_device(): lax.all_to_all(pieces, 'dp', split_axis=0, concat_axis=0, tiled=True)]
    ppermute x0 -> x6, waiting for transfers between devices: none -> 30.3 us  [the longest x3 30.3 us: per_device(): lax.ppermute(own_query, 'mp', pairs)]
    all_gather x1 -> x0, blocking collectives: 13.7 us -> none  [per_device(): query_cols = lax.all_gather(query_piece, 'mp', axis=2, tiled=True)]
    all_gather x1 -> x0, local copies, waits for them, and re-layouts: 11.9 us -> none  [per_device(): all_acts = lax.all_gather(turned_acts, 'dp', axis=0, tiled=True)]
  transfers between devices with their start and end apart: 3 -> 8, of which waited for: 1 -> 3; matrix products, arithmetic and copies ran while one was open for 6% -> 2% of each run, Pallas kernels for 0% -> 17%
where the time goes in v1:
time: 202 us; the launch traced here: 201 us
  waiting for transfers between devices  72.7 us (36%)
  Pallas kernels  45.6 us (23%)
  blocking collectives  33.2 us (16%)
  starting transfers between devices  21 us (10%)
  local copies, waits for them, and re-layouts  14.3 us (7%)
  between operations  13.6 us (7%)
    all_to_all x1, waiting for transfers between devices, per_device(): lax.all_to_all(pieces, 'dp', split_axis=0, concat_axis=0, tiled=True)  42.3 us
    pallas_call x4, Pallas kernels, score(): pl.pallas_call(score_kernel, grid=(sequences // CHUNK,), in_specs=[pl.Blo...  37.4 us
    ppermute x3, waiting for transfers between devices, per_device(): lax.ppermute(own_query, 'mp', pairs)  30.3 us
    all_to_all x1, blocking collectives, per_device(): lax.all_to_all(partial, 'dp', split_axis=0, concat_axis=0, tiled=True)  17 us
    all_to_all x1, blocking collectives, per_device(): lax.all_to_all(spread, ('section', 'mp'), split_axis=0, concat_axis=0, ti...  16.2 us
    unnamed x18, local copies, waits for them, and re-layouts  11.1 us
    all_to_all x1, starting transfers between devices, per_device(): lax.all_to_all(pieces, 'dp', split_axis=0, concat_axis=0, tiled=True)  10.2 us
    ppermute x3, starting transfers between devices, per_device(): lax.ppermute(own_query, 'mp', pairs)  6.31 us
  transfers between devices with their start and end apart: 8, of which 3 were waited for; matrix products, arithmetic and copies ran while one was open for 2% of the time, Pallas kernels for 17%

profile of v1, /device:TPU:1, one launch (start us, length us, event | category | flops | bytes accessed | tf_op | source)
XLA Modules:
  0.0 201.3 jit_solution(8740166293309895054)
XLA Ops:
  6.5 0.0 all-gather.3.cloned.1.call-start
  6.5 0.0 copy-start.3
  6.5 1.2 copy-done.3
  7.8 0.0 copy-start.5
  7.8 0.9 copy-done.5
  8.7 0.0 copy-start.7
  8.7 0.8 copy-done.7
  9.6 1.1 turn_acts.1
  10.6 0.0 all-gather.3.cloned.1.call-update
  10.7 0.0 copy-start.1
  10.7 2.0 %copy-done.1 = bf16[1,3584,512]{2,1,0:T(8,128)(2,1)S(1)} copy-done((bf16[1,3584,512]{2,1,0:T(8,128)(2,1)S(1)}, bf16[1,3584,512]{2,1,0:T(8,128)(2,1)}, u32[]{:S(2)}) %copy-start.1) | copy-done | bytes 3670040
  12.7 0.0 copy-start.4
  12.7 1.2 copy-done.4
  13.9 0.0 copy-start.6
  13.9 0.9 copy-done.6
  14.8 0.0 copy-start.8
  14.8 3.6 %turn_grads.1 = bf16[32,144,128]{2,1,0:T(8,128)(2,1)} custom-call(bf16[128,3584]{1,0:T(8,128)(2,1)S(1)} %bitcast.41, bf16[32,3584]{1,0:T(8,128)(2,1)S(1)} %bitcast.43, bf16[3584,512]{1,0:T(8,128)(2,1)S(1)} %bitcast.38), custom_call_target="tpu_custom_call" | custom-call | tf_op jit(solution)/shard_map/turn_grads/pallas_call | solution.py:145
  18.4 0.0 copy-start.2
  18.4 10.2 %all-to-all-start = ((bf16[32,144,128]{2,1,0:T(8,128)(2,1)}), bf16[32,144,128]{2,1,0:T(8,128)(2,1)}, u32[]{:S(2)}, u32[]{:S(2)}) async-start(bf16[32,144,128]{2,1,0:T(8,128)(2,1)} %turn_grads.1), calls=%async_computation | async-start | bytes 2359296 | tf_op jit(solution)/shard_map/all_to_all | solution.py:162
  28.7 0.0 copy-done.8
  28.7 0.1 broadcast_in_dim.27
  28.8 0.1 broadcast_in_dim.28
  28.9 42.3 %all-to-all-done = bf16[32,144,128]{2,1,0:T(8,128)(2,1)} async-done(((bf16[32,144,128]{2,1,0:T(8,128)(2,1)}), bf16[32,144,128]{2,1,0:T(8,128)(2,1)}, u32[]{:S(2)}, u32[]{:S(2)}) %all-to-all-start) | async-done | bytes 1179680 | tf_op jit(solution)/shard_map/all_to_all | solution.py:162
  71.2 1.2 slice.10.grads_ref
  72.4 1.4 collective-permute-start.3
  73.8 1.6 collective-permute-start.4
  75.4 1.6 collective-permute-start.5
  76.9 1.0 slice.11
  77.9 0.6 gather_fusion
  78.5 0.1 bitcast_select_fusion
  78.6 0.5 collective-permute-start
  79.1 0.1 pad_add_fusion.order_ref
  79.1 2.3 %collective-permute-start.1 = (bf16[256,128]{1,0:T(8,128)(2,1)S(1)}, bf16[256,128]{1,0:T(8,128)(2,1)S(1)}, u32[]{:S(2)}, u32[]{:S(2)}) collective-permute-start(bf16[256,128]{1,0:T(8,128)(2,1)S(1)} %bitcast_select_fusion), channel_id=1, source_target_pairs={{0,3},{1,0},{2,1},{3,2},{4,7},{5,4},{6,5},{7,6},{8,11},{9,8},{10,9... | collective-permute-start | bytes 196616 | tf_op jit(solution)/shard_map/ppermute | solution.py:168
  81.4 28.8 %collective-permute-done = bf16[256,128]{1,0:T(8,128)(2,1)S(1)} collective-permute-done((bf16[256,128]{1,0:T(8,128)(2,1)S(1)}, bf16[256,128]{1,0:T(8,128)(2,1)S(1)}, u32[]{:S(2)}, u32[]{:S(2)}) %collective-permute-start) | collective-permute-done | bytes 65568 | tf_op jit(solution)/shard_map/ppermute | solution.py:168
  110.2 3.5 %collective-permute-start.2 = (bf16[256,128]{1,0:T(8,128)(2,1)S(1)}, bf16[256,128]{1,0:T(8,128)(2,1)S(1)}, u32[]{:S(2)}, u32[]{:S(2)}) collective-permute-start(bf16[256,128]{1,0:T(8,128)(2,1)S(1)} %bitcast_select_fusion), channel_id=1, source_target_pairs={{0,2},{1,3},{2,0},{3,1},{4,6},{5,7},{6,4},{7,5},{8,10},{9,11},{10,... | collective-permute-start | bytes 196616 | tf_op jit(solution)/shard_map/ppermute | solution.py:168
  113.7 0.1 bitcast_select_fusion.1
  113.9 0.0 collective-permute-done.1
  113.9 1.5 collective-permute-done.2
  115.4 0.0 all-gather.3.cloned.1.call-done
  115.5 0.0 copy-done.2
  115.5 0.0 copy-start
  115.5 4.0 %copy-done = bf16[5120,1024]{1,0:T(8,128)(2,1)S(1)} copy-done((bf16[5120,1024]{1,0:T(8,128)(2,1)S(1)}, bf16[5120,1024]{1,0:T(8,128)(2,1)}, u32[]{:S(2)}) %copy-start) | copy-done | bytes 10485784
  119.5 3.5 %weigh.1.weighted_ref = bf16[4,7,128,1024]{3,2,1,0:T(8,128)(2,1)S(1)} custom-call(s32[4]{0:T(128)S(1)} %pad_add_fusion.order_ref, s32[8]{0:T(128)S(1)} %copy-done.8, bf16[4,256,128]{2,1,0:T(8,128)(2,1)S(1)} %pad_maximum_fusion.grads_ref, bf16[32,160,1024]{2,1,0:T(8,128)(2,1)S(1)} %bitcast.30, bf16[32,160,1024]{2,1,0:T(8,128)(2,1)S(1)} %bitcast.31, ...), custom_call_target="tpu_custom_call" | custom-call | tf_op jit(solution)/shard_map/weigh/pallas_call | solution.py:180
  122.9 9.2 %score.4 = f32[32,128]{1,0:T(8,128)S(1)} custom-call(bf16[32,112,128]{2,1,0:T(8,128)(2,1)S(1)} %slice.10.grads_ref, bf16[32,160,1024]{2,1,0:T(8,128)(2,1)} %bitcast.26, bf16[4,7,128,1024]{3,2,1,0:T(8,128)(2,1)S(1)} %weigh.1.weighted_ref), custom_call_target="tpu_custom_call" | custom-call | tf_op jit(solution)/shard_map/score/pallas_call | solution.py:201
  132.2 0.0 collective-permute-done.3.grads_ref
  132.2 9.4 %score.5 = f32[32,128]{1,0:T(8,128)S(1)} custom-call(bf16[32,112,128]{2,1,0:T(8,128)(2,1)} %collective-permute-done.3.grads_ref, bf16[32,160,1024]{2,1,0:T(8,128)(2,1)} %bitcast.27, bf16[4,7,128,1024]{3,2,1,0:T(8,128)(2,1)S(1)} %weigh.1.weighted_ref), custom_call_target="tpu_custom_call" | custom-call | tf_op jit(solution)/shard_map/score/pallas_call | solution.py:201
  141.6 0.0 collective-permute-done.4.grads_ref
  141.6 9.4 %score.6 = f32[32,128]{1,0:T(8,128)S(1)} custom-call(bf16[32,112,128]{2,1,0:T(8,128)(2,1)} %collective-permute-done.4.grads_ref, bf16[32,160,1024]{2,1,0:T(8,128)(2,1)} %bitcast.28, bf16[4,7,128,1024]{3,2,1,0:T(8,128)(2,1)S(1)} %weigh.1.weighted_ref), custom_call_target="tpu_custom_call" | custom-call | tf_op jit(solution)/shard_map/score/pallas_call | solution.py:201
  151.0 0.0 collective-permute-done.5.grads_ref
  151.0 9.4 %score.7 = f32[32,128]{1,0:T(8,128)S(1)} custom-call(bf16[32,112,128]{2,1,0:T(8,128)(2,1)} %collective-permute-done.5.grads_ref, bf16[32,160,1024]{2,1,0:T(8,128)(2,1)} %bitcast.29, bf16[4,7,128,1024]{3,2,1,0:T(8,128)(2,1)S(1)} %weigh.1.weighted_ref), custom_call_target="tpu_custom_call" | custom-call | tf_op jit(solution)/shard_map/score/pallas_call | solution.py:201
  160.4 0.1 copy.14
  160.6 0.1 copy.15
  160.6 17.0 %all_to_all.20 = f32[32,1,8]{2,1,0:T(1,128)S(1)} all-to-all(f32[32,1,8]{2,1,0:T(1,128)S(1)} %copy.15), channel_id=1, replica_groups=mesh['section'=2,'dp'=32,'mp'=4] {'dp'}, dimensions={0} | all-to-all | bytes 2048 | tf_op jit(solution)/shard_map/all_to_all | solution.py:221
  177.6 0.1 reduce_sum.28
  177.7 16.2 %all_to_all.21 = f32[8,1,8]{2,1,0:T(1,128)S(1)} all-to-all(f32[8,1,8]{2,1,0:T(1,128)S(1)} %broadcast_in_dim.34), channel_id=1, replica_groups=mesh['section'=2,'dp'=32,'mp'=4] {'section','mp'}, dimensions={0} | all-to-all | bytes 512 | tf_op jit(solution)/shard_map/all_to_all | solution.py:224
  193.9 0.5 multiply_bitcast_fusion
  (8 shorter events, 0.1 us)
Async XLA Ops:
  6.5 108.9 %all-gather.3.cloned.1.call-start = ((), (), s32[]{:S(2)}) async-start(), calls=%async_computation.3 | async-start | bytes 10813440 | tf_op jit(solution)/shard_map/all_gather | solution.py:142
  6.5 1.2 copy-start.3
  7.8 0.9 copy-start.5
  8.7 0.8 copy-start.7
  10.7 2.0 %copy-start.1 = (bf16[1,3584,512]{2,1,0:T(8,128)(2,1)S(1)}, bf16[1,3584,512]{2,1,0:T(8,128)(2,1)}, u32[]{:S(2)}) copy-start(bf16[1,3584,512]{2,1,0:T(8,128)(2,1)} %param.11) | copy-start | bytes 11010052
  12.7 1.2 copy-start.4
  13.9 0.9 copy-start.6
  14.8 13.9 %copy-start.8 = (s32[8]{0:T(128)S(1)}, s32[8]{0:T(128)}, u32[]{:S(2)}) copy-start(s32[8]{0:T(128)} %owner_ref.1) | copy-start | bytes 100
  18.4 97.0 %copy-start.2 = (f32[1,4,112,1024]{3,2,1,0:T(8,128)S(1)}, f32[1,4,112,1024]{3,2,1,0:T(8,128)}, u32[]{:S(2)}) copy-start(f32[1,4,112,1024]{3,2,1,0:T(8,128)} %param.12) | copy-start | bytes 5505028
  18.4 52.7 %all-to-all-start = ((bf16[32,144,128]{2,1,0:T(8,128)(2,1)}), bf16[32,144,128]{2,1,0:T(8,128)(2,1)}, u32[]{:S(2)}, u32[]{:S(2)}) async-start(bf16[32,144,128]{2,1,0:T(8,128)(2,1)} %turn_grads.1), calls=%async_computation | async-start | bytes 2359296 | tf_op jit(solution)/shard_map/all_to_all | solution.py:162
  72.4 59.7 %collective-permute-start.3 = (bf16[32,112,128]{2,1,0:T(8,128)(2,1)S(1)}, bf16[32,112,128]{2,1,0:T(8,128)(2,1)}, u32[]{:S(2)}, u32[]{:S(2)}) collective-permute-start(bf16[32,112,128]{2,1,0:T(8,128)(2,1)S(1)} %slice.10.grads_ref), channel_id=1, source_target_pairs={{0,1},{1,2},{2,3},{3,0},{4,5},{5,6},{6,7},{7,4},{8,9},{9,10},{10,1... | collective-permute-start | bytes 2752520 | tf_op jit(solution)/shard_map/ppermute | solution.py:169
  73.8 67.8 %collective-permute-start.4 = (bf16[32,112,128]{2,1,0:T(8,128)(2,1)S(1)}, bf16[32,112,128]{2,1,0:T(8,128)(2,1)}, u32[]{:S(2)}, u32[]{:S(2)}) collective-permute-start(bf16[32,112,128]{2,1,0:T(8,128)(2,1)S(1)} %slice.10.grads_ref), channel_id=1, source_target_pairs={{0,3},{1,0},{2,1},{3,2},{4,7},{5,4},{6,5},{7,6},{8,11},{9,8},{10,9... | collective-permute-start | bytes 2752520 | tf_op jit(solution)/shard_map/ppermute | solution.py:169
  75.4 75.6 %collective-permute-start.5 = (bf16[32,112,128]{2,1,0:T(8,128)(2,1)S(1)}, bf16[32,112,128]{2,1,0:T(8,128)(2,1)}, u32[]{:S(2)}, u32[]{:S(2)}) collective-permute-start(bf16[32,112,128]{2,1,0:T(8,128)(2,1)S(1)} %slice.10.grads_ref), channel_id=1, source_target_pairs={{0,2},{1,3},{2,0},{3,1},{4,6},{5,7},{6,4},{7,5},{8,10},{9,11},{10,... | collective-permute-start | bytes 2752520 | tf_op jit(solution)/shard_map/ppermute | solution.py:169
  78.6 31.6 %collective-permute-start = (bf16[256,128]{1,0:T(8,128)(2,1)S(1)}, bf16[256,128]{1,0:T(8,128)(2,1)S(1)}, u32[]{:S(2)}, u32[]{:S(2)}) collective-permute-start(bf16[256,128]{1,0:T(8,128)(2,1)S(1)} %bitcast_select_fusion), channel_id=1, source_target_pairs={{0,1},{1,2},{2,3},{3,0},{4,5},{5,6},{6,7},{7,4},{8,9},{9,10},{10,1... | collective-permute-start | bytes 196616 | tf_op jit(solution)/shard_map/ppermute | solution.py:168
  79.1 34.7 %collective-permute-start.1 = (bf16[256,128]{1,0:T(8,128)(2,1)S(1)}, bf16[256,128]{1,0:T(8,128)(2,1)S(1)}, u32[]{:S(2)}, u32[]{:S(2)}) collective-permute-start(bf16[256,128]{1,0:T(8,128)(2,1)S(1)} %bitcast_select_fusion), channel_id=1, source_target_pairs={{0,3},{1,0},{2,1},{3,2},{4,7},{5,4},{6,5},{7,6},{8,11},{9,8},{10,9... | collective-permute-start | bytes 196616 | tf_op jit(solution)/shard_map/ppermute | solution.py:168
  110.2 5.2 %collective-permute-start.2 = (bf16[256,128]{1,0:T(8,128)(2,1)S(1)}, bf16[256,128]{1,0:T(8,128)(2,1)S(1)}, u32[]{:S(2)}, u32[]{:S(2)}) collective-permute-start(bf16[256,128]{1,0:T(8,128)(2,1)S(1)} %bitcast_select_fusion), channel_id=1, source_target_pairs={{0,2},{1,3},{2,0},{3,1},{4,6},{5,7},{6,4},{7,5},{8,10},{9,11},{10,... | collective-permute-start | bytes 196616 | tf_op jit(solution)/shard_map/ppermute | solution.py:168
  115.5 4.0 %copy-start = (bf16[5120,1024]{1,0:T(8,128)(2,1)S(1)}, bf16[5120,1024]{1,0:T(8,128)(2,1)}, u32[]{:S(2)}) copy-start(bf16[5120,1024]{1,0:T(8,128)(2,1)} %all-gather.3.cloned.1.call-done) | copy-start | bytes 31457284
Sparse Core Ops, SparseCore 0:
  10.8 99.8 all-gather.2

commit v2 on v1

--- a/solution.py
+++ b/solution.py
@@ -16,13 +16,10 @@
 
 
 def turn_acts_kernel(train_ref, query_ref, basis_ref, out_ref):
-    size = basis_ref.shape[1]
-    for b in range(train_ref.shape[1] // size):
-        cols = slice(b * size, (b + 1) * size)
-        rows = jnp.concatenate([train_ref[:, cols], query_ref[:, cols]], axis=0)
-        out_ref[:, cols] = jnp.dot(
-            rows, basis_ref[cols, :], preferred_element_type=jnp.float32
-        ).astype(jnp.bfloat16)
+    rows = jnp.concatenate([train_ref[...], query_ref[...]], axis=0)
+    out_ref[...] = jnp.dot(
+        rows, basis_ref[...], preferred_element_type=jnp.float32
+    ).astype(jnp.bfloat16)
 
 
 def turn_grads_kernel(train_ref, query_ref, basis_ref, out_ref, turned, slots):
@@ -90,12 +87,22 @@
         out_ref[0, b] = moments.reshape(queries * ROWS, moments.shape[2]).astype(jnp.bfloat16)
 
 
-def score_kernel(grads_ref, acts_ref, weighted_ref, out_ref, grams):
+def score_kernel(*refs):
+    parts = len(refs) - 7
+    part_refs = refs[:parts]
+    acts_ref, weighted_ref, out_ref, grams, weighted, totals, arrived = refs[parts:]
     step = pl.program_id(0)
     steps = pl.num_programs(0)
-    blocks = weighted_ref.shape[1]
+    blocks = weighted.shape[0]
+    load = pltpu.make_async_copy(weighted_ref, weighted, arrived)
+
+    @pl.when(step == 0)
+    def _():
+        load.start()
+
     for i in range(CHUNK):
-        gram = jnp.dot(grads_ref[i], acts_ref[i], preferred_element_type=jnp.float32)
+        grads = jnp.concatenate([part[i] for part in part_refs], axis=0)
+        gram = jnp.dot(grads, acts_ref[i], preferred_element_type=jnp.float32)
         gram = gram.astype(jnp.bfloat16)
         start = pl.multiple_of((step * CHUNK + i) * ROWS, ROWS)
         for b in range(blocks):
@@ -103,20 +110,27 @@
 
     @pl.when(step == steps - 1)
     def _():
-        total = jnp.zeros((grams.shape[1], weighted_ref.shape[2]), jnp.float32)
-        for b in range(blocks):
-            total += lax.dot_general(
-                grams[b],
-                weighted_ref[0, b],
-                (((1,), (1,)), ((), ())),
-                preferred_element_type=jnp.float32,
-            )
+        load.wait()
+        totals[...] = jnp.zeros_like(totals)
+        group = 7
+
+        @pl.loop(0, blocks // group)
+        def _(g):
+            for b in range(group):
+                totals[...] += lax.dot_general(
+                    grams[g * group + b],
+                    weighted[g * group + b],
+                    (((1,), (1,)), ((), ())),
+                    preferred_element_type=jnp.float32,
+                )
+
+        shape = totals.shape
         same = (
-            lax.broadcasted_iota(jnp.int32, total.shape, 0) % ROWS
-            == lax.broadcasted_iota(jnp.int32, total.shape, 1) % ROWS
+            lax.broadcasted_iota(jnp.int32, shape, 0) % ROWS
+            == lax.broadcasted_iota(jnp.int32, shape, 1) % ROWS
         )
-        total = jnp.where(same, total, 0.0)
-        out_ref[...] = jnp.sum(total.reshape(-1, ROWS, total.shape[1]), axis=1)
+        kept = jnp.where(same, totals[...], 0.0)
+        out_ref[...] = jnp.sum(kept.reshape(-1, ROWS, shape[1]), axis=1)
 
 
 def per_device(
@@ -135,8 +149,15 @@
 
     turned_acts = pl.pallas_call(
         turn_acts_kernel,
+        grid=(act_cols // block_size,),
+        in_specs=[
+            pl.BlockSpec((tokens, block_size), lambda s: (0, s)),
+            pl.BlockSpec((length, block_size), lambda s: (0, s)),
+            pl.BlockSpec((block_size, block_size), lambda s: (s, 0)),
+        ],
+        out_specs=pl.BlockSpec((tokens + length, block_size), lambda s: (0, s)),
         out_shape=jax.ShapeDtypeStruct((tokens + length, act_cols), bf16),
-        compiler_params=pltpu.CompilerParams(vmem_limit_bytes=24 * MIB),
+        compiler_params=pltpu.CompilerParams(vmem_limit_bytes=60 * MIB),
         name="turn_acts",
     )(train_acts[0], query_acts[0, 0], basis_in[0])
     all_acts = lax.all_gather(turned_acts, "dp", axis=0)
@@ -156,7 +177,7 @@
             pltpu.VMEM((steps, block_size, tokens), bf16),
             pltpu.VMEM((steps, length, block_size), jnp.float32),
         ],
-        compiler_params=pltpu.CompilerParams(vmem_limit_bytes=24 * MIB),
+        compiler_params=pltpu.CompilerParams(vmem_limit_bytes=60 * MIB),
         name="turn_grads",
     )(train_grads[0], query_grads[0, 0], basis_out[0])
     moved = lax.all_to_all(pieces, "dp", split_axis=0, concat_axis=0, tiled=True)
@@ -193,29 +214,31 @@
             scratch_shapes=[pltpu.VMEM((queries * length, act_cols), bf16)],
         ),
         out_shape=jax.ShapeDtypeStruct((model_size, blocks, queries * ROWS, act_cols), bf16),
-        compiler_params=pltpu.CompilerParams(vmem_limit_bytes=32 * MIB),
+        compiler_params=pltpu.CompilerParams(vmem_limit_bytes=60 * MIB),
         name="weigh",
     )(order, query_owner, jnp.stack(query_parts), *([all_acts] * queries), eigen_values[0])
 
-    def score(part, grads):
-        return pl.pallas_call(
-            score_kernel,
-            grid=(sequences // CHUNK,),
-            in_specs=[
-                pl.BlockSpec((CHUNK, piece, tokens), lambda s: (s, 0, 0)),
-                pl.BlockSpec((CHUNK, tokens, act_cols), lambda s: (s, 0, 0)),
-                pl.BlockSpec(
-                    (1, blocks, queries * ROWS, act_cols), lambda s: (part, 0, 0, 0)
-                ),
-            ],
-            out_specs=pl.BlockSpec((sequences, queries * ROWS), lambda s: (0, 0)),
-            out_shape=jax.ShapeDtypeStruct((sequences, queries * ROWS), jnp.float32),
-            scratch_shapes=[pltpu.VMEM((blocks, sequences * ROWS, act_cols), bf16)],
-            compiler_params=pltpu.CompilerParams(vmem_limit_bytes=40 * MIB),
-            name="score",
-        )(grads, all_acts, weighted)
-
-    scores = sum(score(part, grads) for part, grads in enumerate(grad_parts))
+    weighted = weighted.reshape(model_size * blocks, queries * ROWS, act_cols)
+    part_spec = pl.BlockSpec((CHUNK, piece, tokens), lambda s: (s, 0, 0))
+    scores = pl.pallas_call(
+        score_kernel,
+        grid=(sequences // CHUNK,),
+        in_specs=[part_spec] * model_size
+        + [
+            pl.BlockSpec((CHUNK, tokens, act_cols), lambda s: (s, 0, 0)),
+            pl.BlockSpec(memory_space=pl.ANY),
+        ],
+        out_specs=pl.BlockSpec((sequences, queries * ROWS), lambda s: (0, 0)),
+        out_shape=jax.ShapeDtypeStruct((sequences, queries * ROWS), jnp.float32),
+        scratch_shapes=[
+            pltpu.VMEM((model_size * blocks, sequences * ROWS, act_cols), bf16),
+            pltpu.VMEM(weighted.shape, bf16),
+            pltpu.VMEM((sequences * ROWS, queries * ROWS), jnp.float32),
+            pltpu.SemaphoreType.DMA,
+        ],
+        compiler_params=pltpu.CompilerParams(vmem_limit_bytes=60 * MIB),
+        name="score",
+    )(*grad_parts, all_acts, weighted)
     partial = scores.reshape(sequences, queries, ROWS).sum(axis=2)
 
     mine = lax.all_to_all(partial, "dp", split_axis=0, concat_axis=0, tiled=True).sum(axis=0)

time: 202 us -> 185 us (0.916)
  local copies, waits for them, and re-layouts: 14.3 us -> 2.63 us
  Pallas kernels: 45.6 us -> 38.5 us
    pallas_call x5 -> x2, Pallas kernels: 38.5 us -> 24.4 us  [the longest x1 22.1 us: per_device(): pl.pallas_call(score_kernel, grid=(sequences // CHUNK,), in_specs=[part_s...]
    unnamed x18 -> x6, local copies, waits for them, and re-layouts: 11.1 us -> 0.93 us
    pallas_call x1, Pallas kernels: 3.48 us -> 7.07 us  [per_device(): pl.pallas_call(weigh_kernel, grid_spec=pltpu.PrefetchScalarGridSpec(num_s...]
    pallas_call x1, Pallas kernels: 3.62 us -> 7 us  [per_device(): pl.pallas_call(turn_grads_kernel, grid=(steps,), in_specs=[pl.BlockSpec((...]
  transfers between devices with their start and end apart: 8 -> 8, of which waited for: 3 -> 3; matrix products, arithmetic and copies ran while one was open for 2% -> 1% of each run, Pallas kernels for 17% -> 8%
where the time goes in v2:
time: 185 us; the launch traced here: 184 us
  waiting for transfers between devices  73.1 us (40%)
  Pallas kernels  38.5 us (21%)
  blocking collectives  32.9 us (18%)
  starting transfers between devices  21 us (11%)
  between operations  13.6 us (7%)
  local copies, waits for them, and re-layouts  2.63 us (1%)
  other arithmetic  2.16 us (1%)
    all_to_all x1, waiting for transfers between devices, per_device(): lax.all_to_all(pieces, 'dp', split_axis=0, concat_axis=0, tiled=True)  42.2 us
    ppermute x3, waiting for transfers between devices, per_device(): lax.ppermute(own_query, 'mp', pairs)  30.9 us
    pallas_call x1, Pallas kernels, per_device(): pl.pallas_call(score_kernel, grid=(sequences // CHUNK,), in_specs=[part_s...  22.1 us
    all_to_all x1, blocking collectives, per_device(): lax.all_to_all(partial, 'dp', split_axis=0, concat_axis=0, tiled=True)  16.7 us
    all_to_all x1, blocking collectives, per_device(): lax.all_to_all(spread, ('section', 'mp'), split_axis=0, concat_axis=0, ti...  16.1 us
    all_to_all x1, starting transfers between devices, per_device(): lax.all_to_all(pieces, 'dp', split_axis=0, concat_axis=0, tiled=True)  10 us
    pallas_call x1, Pallas kernels, per_device(): pl.pallas_call(weigh_kernel, grid_spec=pltpu.PrefetchScalarGridSpec(num_s...  7.07 us
    pallas_call x1, Pallas kernels, per_device(): pl.pallas_call(turn_grads_kernel, grid=(steps,), in_specs=[pl.BlockSpec((...  7 us
  transfers between devices with their start and end apart: 8, of which 3 were waited for; matrix products, arithmetic and copies ran while one was open for 1% of the time, Pallas kernels for 8%

profile of v2, /device:TPU:1, one launch (start us, length us, event | category | flops | bytes accessed | tf_op | source)
XLA Modules:
  0.0 183.9 jit_solution(2514562624289129881)
XLA Ops:
  6.5 0.0 all-gather.3.cloned.1.call-start
  6.5 2.3 %turn_acts.1 = bf16[160,1024]{1,0:T(8,128)(2,1)} custom-call(bf16[128,1024]{1,0:T(8,128)(2,1)} %bitcast.42, bf16[32,1024]{1,0:T(8,128)(2,1)} %bitcast.47, bf16[1024,512]{1,0:T(8,128)(2,1)} %bitcast.39), custom_call_target="tpu_custom_call" | custom-call | tf_op jit(solution)/shard_map/turn_acts/pallas_call | solution.py:150
  8.9 0.0 all-gather.3.cloned.1.call-update
  8.9 0.0 copy-start.2
  8.9 7.0 %turn_grads.1 = bf16[32,144,128]{2,1,0:T(8,128)(2,1)} custom-call(bf16[128,3584]{1,0:T(8,128)(2,1)} %bitcast.40, bf16[32,3584]{1,0:T(8,128)(2,1)} %bitcast.43, bf16[3584,512]{1,0:T(8,128)(2,1)} %bitcast.37), custom_call_target="tpu_custom_call" | custom-call | tf_op jit(solution)/shard_map/turn_grads/pallas_call | solution.py:166
  15.9 10.0 %all-to-all-start = ((bf16[32,144,128]{2,1,0:T(8,128)(2,1)}), bf16[32,144,128]{2,1,0:T(8,128)(2,1)S(1)}, u32[]{:S(2)}, u32[]{:S(2)}) async-start(bf16[32,144,128]{2,1,0:T(8,128)(2,1)} %turn_grads.1), calls=%async_computation | async-start | bytes 2359296 | tf_op jit(solution)/shard_map/all_to_all | solution.py:183
  26.0 0.0 copy-done.2
  26.0 0.1 broadcast_in_dim.27
  26.1 0.1 broadcast_in_dim.28
  26.2 42.2 %all-to-all-done = bf16[32,144,128]{2,1,0:T(8,128)(2,1)S(1)} async-done(((bf16[32,144,128]{2,1,0:T(8,128)(2,1)}), bf16[32,144,128]{2,1,0:T(8,128)(2,1)S(1)}, u32[]{:S(2)}, u32[]{:S(2)}) %all-to-all-start) | async-done | bytes 1179680 | tf_op jit(solution)/shard_map/all_to_all | solution.py:183
  68.4 0.1 slice.10.refs_0_
  68.4 0.0 copy-start
  68.4 1.4 collective-permute-start
  69.8 1.6 collective-permute-start.1
  71.5 1.4 collective-permute-start.2
  73.0 0.6 gather_fusion
  73.5 0.1 bitcast_select_fusion
  73.6 0.6 collective-permute-start.3
  74.2 0.6 pad_add_fusion.order_ref
  74.8 2.2 %collective-permute-start.4 = (bf16[256,128]{1,0:T(8,128)(2,1)S(1)}, bf16[256,128]{1,0:T(8,128)(2,1)S(1)}, u32[]{:S(2)}, u32[]{:S(2)}) collective-permute-start(bf16[256,128]{1,0:T(8,128)(2,1)S(1)} %bitcast_select_fusion), channel_id=1, source_target_pairs={{0,3},{1,0},{2,1},{3,2},{4,7},{5,4},{6,5},{7,6},{8,11},{9,8},{10,9... | collective-permute-start | bytes 196616 | tf_op jit(solution)/shard_map/ppermute | solution.py:189
  77.0 29.3 %collective-permute-done.3 = bf16[256,128]{1,0:T(8,128)(2,1)S(1)} collective-permute-done((bf16[256,128]{1,0:T(8,128)(2,1)S(1)}, bf16[256,128]{1,0:T(8,128)(2,1)S(1)}, u32[]{:S(2)}, u32[]{:S(2)}) %collective-permute-start.3) | collective-permute-done | bytes 65568 | tf_op jit(solution)/shard_map/ppermute | solution.py:189
  106.3 3.8 %collective-permute-start.5 = (bf16[256,128]{1,0:T(8,128)(2,1)S(1)}, bf16[256,128]{1,0:T(8,128)(2,1)S(1)}, u32[]{:S(2)}, u32[]{:S(2)}) collective-permute-start(bf16[256,128]{1,0:T(8,128)(2,1)S(1)} %bitcast_select_fusion), channel_id=1, source_target_pairs={{0,2},{1,3},{2,0},{3,1},{4,6},{5,7},{6,4},{7,5},{8,10},{9,11},{10,... | collective-permute-start | bytes 196616 | tf_op jit(solution)/shard_map/ppermute | solution.py:189
  110.1 0.1 bitcast_select_fusion.1
  110.2 0.0 collective-permute-done.4
  110.2 1.5 collective-permute-done.5
  111.8 0.7 pad_maximum_fusion.grads_ref
  112.5 0.0 all-gather.3.cloned.1.call-done
  112.5 7.1 %weigh.1 = bf16[4,7,128,1024]{3,2,1,0:T(8,128)(2,1)} custom-call(s32[4]{0:T(128)} %pad_add_fusion.order_ref, s32[8]{0:T(128)} %owner_ref.1, bf16[4,256,128]{2,1,0:T(8,128)(2,1)} %pad_maximum_fusion.grads_ref, bf16[32,160,1024]{2,1,0:T(8,128)(2,1)} %bitcast.27, bf16[32,160,1024]{2,1,0:T(8,128)(2,1)} %bitcast.28, bf16[32,160,1024]{2,1,0:T(8,128)(2,1)} %bitcast.29, ...), custom_call_target="tpu_custom_call" | custom-call | tf_op jit(solution)/shard_map/weigh/pallas_call | solution.py:201
  119.6 0.0 copy-done
  119.6 0.0 collective-permute-done.refs_1_
  119.6 0.0 copy-start.1
  119.6 0.0 collective-permute-done.1.refs_2_
  119.6 0.0 collective-permute-done.2.refs_3_
  119.6 0.9 copy-done.1
  120.5 22.1 %score.1 = f32[32,128]{1,0:T(8,128)} custom-call(bf16[32,112,128]{2,1,0:T(8,128)(2,1)} %copy-done, bf16[32,112,128]{2,1,0:T(8,128)(2,1)} %copy-done.1, bf16[32,112,128]{2,1,0:T(8,128)(2,1)} %collective-permute-done.1.refs_2_, bf16[32,112,128]{2,1,0:T(8,128)(2,1)} %collective-permute-done.2.refs_3_, bf16[32,160,1024]{2,1,0:T(8,128)(2,1)} %bitcast.35, ...), custom_call_target="tpu_custom_call" | custom-call | tf_op jit(solution)/shard_map/score/pallas_call | solution.py:223
  142.6 0.8 copy.14
  143.5 0.1 copy.15
  143.6 16.7 %all_to_all.20 = f32[32,1,8]{2,1,0:T(1,128)S(1)} all-to-all(f32[32,1,8]{2,1,0:T(1,128)S(1)} %copy.15), channel_id=1, replica_groups=mesh['section'=2,'dp'=32,'mp'=4] {'dp'}, dimensions={0} | all-to-all | bytes 2048 | tf_op jit(solution)/shard_map/all_to_all | solution.py:244
  160.3 0.1 reduce_sum.28
  160.4 16.1 %all_to_all.21 = f32[8,1,8]{2,1,0:T(1,128)S(1)} all-to-all(f32[8,1,8]{2,1,0:T(1,128)S(1)} %broadcast_in_dim.34), channel_id=1, replica_groups=mesh['section'=2,'dp'=32,'mp'=4] {'section','mp'}, dimensions={0} | all-to-all | bytes 512 | tf_op jit(solution)/shard_map/all_to_all | solution.py:247
  176.5 0.5 multiply_bitcast_fusion
  (7 shorter events, 0.1 us)
Async XLA Ops:
  6.5 106.0 %all-gather.3.cloned.1.call-start = ((), (), s32[]{:S(2)}) async-start(), calls=%async_computation.3 | async-start | bytes 10813440 | tf_op jit(solution)/shard_map/all_gather | solution.py:163
  8.9 17.1 %copy-start.2 = (s32[8]{0:T(128)S(1)}, s32[8]{0:T(128)}, u32[]{:S(2)}) copy-start(s32[8]{0:T(128)} %owner_ref.1) | copy-start | bytes 100
  15.9 52.5 %all-to-all-start = ((bf16[32,144,128]{2,1,0:T(8,128)(2,1)}), bf16[32,144,128]{2,1,0:T(8,128)(2,1)S(1)}, u32[]{:S(2)}, u32[]{:S(2)}) async-start(bf16[32,144,128]{2,1,0:T(8,128)(2,1)} %turn_grads.1), calls=%async_computation | async-start | bytes 2359296 | tf_op jit(solution)/shard_map/all_to_all | solution.py:183
  68.4 51.1 %copy-start = (bf16[32,112,128]{2,1,0:T(8,128)(2,1)}, bf16[32,112,128]{2,1,0:T(8,128)(2,1)S(1)}, u32[]{:S(2)}) copy-start(bf16[32,112,128]{2,1,0:T(8,128)(2,1)S(1)} %slice.10.refs_0_) | copy-start | bytes 2752516
  68.4 51.1 %collective-permute-start = (bf16[32,112,128]{2,1,0:T(8,128)(2,1)S(1)}, bf16[32,112,128]{2,1,0:T(8,128)(2,1)S(1)}, u32[]{:S(2)}, u32[]{:S(2)}) collective-permute-start(bf16[32,112,128]{2,1,0:T(8,128)(2,1)S(1)} %slice.10.refs_0_), channel_id=1, source_target_pairs={{0,1},{1,2},{2,3},{3,0},{4,5},{5,6},{6,7},{7,4},{8,9},{9,10},{10,1... | collective-permute-start | bytes 2752520 | tf_op jit(solution)/shard_map/ppermute | solution.py:190
  69.8 49.8 %collective-permute-start.1 = (bf16[32,112,128]{2,1,0:T(8,128)(2,1)S(1)}, bf16[32,112,128]{2,1,0:T(8,128)(2,1)}, u32[]{:S(2)}, u32[]{:S(2)}) collective-permute-start(bf16[32,112,128]{2,1,0:T(8,128)(2,1)S(1)} %slice.10.refs_0_), channel_id=1, source_target_pairs={{0,3},{1,0},{2,1},{3,2},{4,7},{5,4},{6,5},{7,6},{8,11},{9,8},{10,9... | collective-permute-start | bytes 2752520 | tf_op jit(solution)/shard_map/ppermute | solution.py:190
  71.5 48.1 %collective-permute-start.2 = (bf16[32,112,128]{2,1,0:T(8,128)(2,1)S(1)}, bf16[32,112,128]{2,1,0:T(8,128)(2,1)}, u32[]{:S(2)}, u32[]{:S(2)}) collective-permute-start(bf16[32,112,128]{2,1,0:T(8,128)(2,1)S(1)} %slice.10.refs_0_), channel_id=1, source_target_pairs={{0,2},{1,3},{2,0},{3,1},{4,6},{5,7},{6,4},{7,5},{8,10},{9,11},{10,... | collective-permute-start | bytes 2752520 | tf_op jit(solution)/shard_map/ppermute | solution.py:190
  73.6 32.7 %collective-permute-start.3 = (bf16[256,128]{1,0:T(8,128)(2,1)S(1)}, bf16[256,128]{1,0:T(8,128)(2,1)S(1)}, u32[]{:S(2)}, u32[]{:S(2)}) collective-permute-start(bf16[256,128]{1,0:T(8,128)(2,1)S(1)} %bitcast_select_fusion), channel_id=1, source_target_pairs={{0,1},{1,2},{2,3},{3,0},{4,5},{5,6},{6,7},{7,4},{8,9},{9,10},{10,1... | collective-permute-start | bytes 196616 | tf_op jit(solution)/shard_map/ppermute | solution.py:189
  74.8 35.4 %collective-permute-start.4 = (bf16[256,128]{1,0:T(8,128)(2,1)S(1)}, bf16[256,128]{1,0:T(8,128)(2,1)S(1)}, u32[]{:S(2)}, u32[]{:S(2)}) collective-permute-start(bf16[256,128]{1,0:T(8,128)(2,1)S(1)} %bitcast_select_fusion), channel_id=1, source_target_pairs={{0,3},{1,0},{2,1},{3,2},{4,7},{5,4},{6,5},{7,6},{8,11},{9,8},{10,9... | collective-permute-start | bytes 196616 | tf_op jit(solution)/shard_map/ppermute | solution.py:189
  106.3 5.4 %collective-permute-start.5 = (bf16[256,128]{1,0:T(8,128)(2,1)S(1)}, bf16[256,128]{1,0:T(8,128)(2,1)S(1)}, u32[]{:S(2)}, u32[]{:S(2)}) collective-permute-start(bf16[256,128]{1,0:T(8,128)(2,1)S(1)} %bitcast_select_fusion), channel_id=1, source_target_pairs={{0,2},{1,3},{2,0},{3,1},{4,6},{5,7},{6,4},{7,5},{8,10},{9,11},{10,... | collective-permute-start | bytes 196616 | tf_op jit(solution)/shard_map/ppermute | solution.py:189
  119.6 0.9 copy-start.1
Sparse Core Ops, SparseCore 0:
  9.2 99.9 all-gather.2

commit v3 on v2

v3 whole, which is shorter than its diff:
```python
import functools
import math

import jax
import jax.numpy as jnp
from jax import lax
from jax.experimental import pallas as pl
from jax.experimental.pallas import tpu as pltpu
from jax.sharding import PartitionSpec as P

SEQLEN = 128
DAMPING = 0.1
ROWS = 16
CORES = 2
DEPTH = 4
MIB = 1 << 20


def tile_of(target, side):
    x, rest = divmod(target, DEPTH)
    z, core = divmod(rest, CORES)
    return (x * DEPTH + 2 * z + side) * CORES + core


def turn_acts_kernel(train_ref, query_ref, basis_ref, out_ref):
    rows = jnp.concatenate([train_ref[...], query_ref[...]], axis=0)
    out_ref[...] = jnp.dot(
        rows, basis_ref[...], preferred_element_type=jnp.float32
    ).astype(jnp.bfloat16)


def turn_grads_kernel(train_ref, query_ref, basis_ref, out_ref, turned, slots):
    step = pl.program_id(0)
    steps = pl.num_programs(0)
    size = basis_ref.shape[1]
    tokens = train_ref.shape[0]
    rows = jnp.concatenate([train_ref[...], query_ref[...]], axis=0)
    product = jnp.dot(rows, basis_ref[...], preferred_element_type=jnp.float32)
    turned[step] = product[:tokens].T.astype(jnp.bfloat16)
    slots[step] = product[tokens:]

    @pl.when(step == steps - 1)
    def _():
        targets, _, lanes = out_ref.shape
        total = turned.shape[0] * size
        piece = total // (2 * targets)
        length = slots.shape[1]
        for target in range(targets):
            for side in range(2):
                start = tile_of(target, side) * piece
                parts = []
                at = start
                while at < start + piece:
                    block = at // size
                    end = min(start + piece, (block + 1) * size)
                    parts.append(turned[block, at - block * size : end - block * size, :])
                    at = end
                rows = parts[0] if len(parts) == 1 else jnp.concatenate(parts, axis=0)
                out_ref[target, side * piece : (side + 1) * piece, :] = rows
                first = start // lanes
                tiles = []
                for tile in range(first, min(first + 2, total // lanes)):
                    col = tile * lanes
                    block = col // size
                    tiles.append(slots[block, :, col - block * size : col - block * size + lanes])
                window = jnp.concatenate(tiles, axis=1) if len(tiles) > 1 else tiles[0]
                shift = start - first * lanes
                if shift:
                    window = pltpu.roll(window, window.shape[1] - shift, 1)
                at = 2 * piece + side * length
                out_ref[target, at : at + length, :] = window[:, :lanes].astype(jnp.bfloat16)


def weigh_kernel(order_ref, place_ref, grads_ref, *refs):
    acts_refs = refs[:-4]
    own_ref, other_ref, out_ref, acts = refs[-4:]
    count = acts_refs[0].shape[2]
    tokens = len(acts_refs) * count
    queries = out_ref.shape[2] // ROWS

    @pl.when(pl.program_id(0) == 0)
    def _():
        for n, ref in enumerate(acts_refs):
            at = pl.multiple_of(place_ref[n] * count, count)
            acts[pl.ds(at, count), :] = ref[0, 0]

    turned = grads_ref[0].astype(jnp.float32).T
    shape = (queries * ROWS, tokens)
    own = lax.broadcasted_iota(jnp.int32, shape, 0) // ROWS == (
        lax.broadcasted_iota(jnp.int32, shape, 1) // (count // queries)
    ) % queries
    blocks = own_ref.shape[1] // ROWS
    lanes = grads_ref.shape[2] // 2
    side_of_own = place_ref[len(acts_refs)]
    for side in range(2):
        mine = side_of_own == side
        for b in range(blocks):
            rows = slice(b * ROWS, (b + 1) * ROWS)
            part = turned[side * lanes + b * ROWS : side * lanes + (b + 1) * ROWS]
            spread = jnp.concatenate([part] * queries, axis=0)
            spread = jnp.where(own, spread, 0.0).astype(jnp.bfloat16)
            moments = jnp.dot(spread, acts[...], preferred_element_type=jnp.float32)
            values = jnp.where(mine, own_ref[0, rows, :], other_ref[0, rows, :].astype(jnp.float32))
            inverse = 1.0 / (values + DAMPING)
            moments = moments.reshape(queries, ROWS, moments.shape[1]) * inverse[None]
            moments = moments.reshape(queries * ROWS, moments.shape[2])
            out_ref[0, side * blocks + b] = moments.astype(jnp.bfloat16)


def score_kernel(first, place_ref, *refs):
    parts = len(refs) - 8
    part_refs = refs[:parts]
    near_ref, far_ref, weighted_ref, out_ref, grams, weighted, totals, arrived = refs[parts:]
    step = pl.program_id(0)
    steps = pl.num_programs(0)
    blocks = weighted.shape[0]
    load = pltpu.make_async_copy(weighted_ref.at[pl.ds(first, blocks)], weighted, arrived)

    @pl.when(step == 0)
    def _():
        load.start()

    pairs = near_ref.shape[1]
    for far, acts_ref in enumerate((near_ref, far_ref)):
        for n in range(pairs):
            place = place_ref[(far * steps + step) * pairs + n]
            inner = lax.rem(place, CORES * pairs)
            grads = jnp.concatenate([part[0, inner] for part in part_refs], axis=0)
            gram = jnp.dot(grads, acts_ref[0, n], preferred_element_type=jnp.float32)
            gram = gram.astype(jnp.bfloat16)
            start = pl.multiple_of(place * ROWS, ROWS)
            for b in range(blocks):
                grams[b, pl.ds(start, ROWS), :] = gram[b * ROWS : (b + 1) * ROWS]

    @pl.when(step == steps - 1)
    def _():
        load.wait()
        totals[...] = jnp.zeros_like(totals)
        group = 7

        @pl.loop(0, blocks // group)
        def _(g):
            for b in range(group):
                totals[...] += lax.dot_general(
                    grams[g * group + b],
                    weighted[g * group + b],
                    (((1,), (1,)), ((), ())),
                    preferred_element_type=jnp.float32,
                )

        shape = totals.shape
        same = (
            lax.broadcasted_iota(jnp.int32, shape, 0) % ROWS
            == lax.broadcasted_iota(jnp.int32, shape, 1) % ROWS
        )
        kept = jnp.where(same, totals[...], 0.0)
        out_ref[...] = jnp.sum(kept.reshape(-1, ROWS, shape[1]), axis=1)


def per_device(
    train_acts, train_grads, basis_in, basis_out, eigen_values, query_acts, query_grads, query_owner
):
    block_size = basis_in.shape[2]
    tokens, act_cols = train_acts.shape[1:]
    grad_cols = train_grads.shape[2]
    length = query_acts.shape[2]
    queries = query_owner.shape[0]
    data_size = lax.axis_size("dp")
    model_size = lax.axis_size("mp")
    piece = grad_cols // data_size
    bf16 = jnp.bfloat16

    turned_acts = pl.pallas_call(
        turn_acts_kernel,
        grid=(act_cols // block_size,),
        in_specs=[
            pl.BlockSpec((tokens, block_size), lambda s: (0, s)),
            pl.BlockSpec((length, block_size), lambda s: (0, s)),
            pl.BlockSpec((block_size, block_size), lambda s: (s, 0)),
        ],
        out_specs=pl.BlockSpec((tokens + length, block_size), lambda s: (0, s)),
        out_shape=jax.ShapeDtypeStruct((tokens + length, act_cols), bf16),
        compiler_params=pltpu.CompilerParams(vmem_limit_bytes=60 * MIB),
        name="turn_acts",
    )(train_acts[0], query_acts[0, 0], basis_in[0])
    width = data_size // (DEPTH * CORES)
    targets = data_size // 2
    classes = [[tile_of(t, parity) for t in range(targets)] for parity in range(2)]
    where = [(x, z, c) for x in range(width) for z in range(DEPTH) for c in range(CORES)]

    def shifted(dx=0, dz=0, flip_z=0, flip_c=0):
        at = lambda x, z, c: (x % width * DEPTH + z % DEPTH) * CORES + c
        return [
            (at(x, z, c), at(x + dx, (z + dz) % DEPTH ^ flip_z, c ^ flip_c)) for x, z, c in where
        ]

    data_index = lax.axis_index("dp")
    my_x = data_index // (DEPTH * CORES)
    my_z = data_index // CORES % DEPTH
    my_core = data_index % CORES
    my_class = my_z % 2

    other_values = lax.ppermute(eigen_values[0].astype(bf16), "dp", shifted(flip_z=1))

    each = length // targets
    slot_acts = turned_acts[tokens:].reshape(width, DEPTH // 2, 1, CORES, -1, tokens)
    slot_acts = jnp.broadcast_to(slot_acts, (width, DEPTH // 2, 2, CORES) + slot_acts.shape[4:])
    slot_acts = slot_acts.reshape(data_size, -1, tokens)
    slot_acts = lax.all_to_all(slot_acts, "dp", split_axis=0, concat_axis=0, tiled=True)
    chosen_acts = jnp.take(slot_acts, query_owner, axis=0).reshape(queries * each, act_cols)
    sent = jnp.concatenate([turned_acts[:tokens], chosen_acts], axis=0)
    pair = jnp.stack([sent, lax.ppermute(sent, "dp", shifted(dz=2))])

    steps = grad_cols // block_size
    rows = 2 * (piece + length)
    pieces = pl.pallas_call(
        turn_grads_kernel,
        grid=(steps,),
        in_specs=[
            pl.BlockSpec((tokens, block_size), lambda s: (0, s)),
            pl.BlockSpec((length, block_size), lambda s: (0, s)),
            pl.BlockSpec((block_size, block_size), lambda s: (s, 0)),
        ],
        out_specs=pl.BlockSpec((targets, rows, tokens), lambda s: (0, 0, 0)),
        out_shape=jax.ShapeDtypeStruct((targets, rows, tokens), bf16),
        scratch_shapes=[
            pltpu.VMEM((steps, block_size, tokens), bf16),
            pltpu.VMEM((steps, length, block_size), jnp.float32),
        ],
        compiler_params=pltpu.CompilerParams(vmem_limit_bytes=60 * MIB),
        name="turn_grads",
    )(train_grads[0], query_grads[0, 0], basis_out[0])
    moved = lax.all_to_all(
        pieces, "dp", split_axis=0, concat_axis=0, tiled=True, axis_index_groups=classes
    )
    own_grads = moved[:, : 2 * piece].reshape(width, DEPTH // 2 * CORES, 2 * piece, tokens)

    owner_z = query_owner // CORES % DEPTH
    owner_place = query_owner // (DEPTH * CORES) * DEPTH + owner_z // 2 * CORES
    owner_place = owner_place + query_owner % CORES
    chosen = jnp.take(moved[:, 2 * piece :], owner_place, axis=0)
    chosen = jnp.where((owner_z % 2 == my_class)[:, None, None], chosen, 0).astype(bf16)
    chosen = chosen.reshape(queries, 2, targets, each, tokens).transpose(2, 0, 3, 1, 4)
    chosen = chosen.reshape(queries * length, 2 * tokens)
    own_query = chosen + lax.ppermute(chosen, "dp", shifted(flip_z=1))

    ring = range(model_size)
    shifts = [[(i, (i + s) % model_size) for i in ring] for s in (1, model_size - 1, 2)]
    grad_parts = [own_grads] + [lax.ppermute(own_grads, "mp", pairs) for pairs in shifts]
    query_parts = [own_query] + [lax.ppermute(own_query, "mp", pairs) for pairs in shifts]
    model_index = lax.axis_index("mp")
    order = jnp.stack([(model_index + s) % model_size for s in (0, model_size - 1, 1, 2)])
    order = order.astype(jnp.int32)

    near = jnp.stack([pair] + [lax.ppermute(pair, "dp", shifted(dx=s)) for s in range(1, width)])
    far = lax.ppermute(near, "dp", shifted(flip_c=1))
    places = [
        ((my_x + width - s) % width * (DEPTH // 2) + (my_z // 2 + n) % 2) * CORES
        + (my_core + flip) % CORES
        for flip in range(2)
        for s in range(width)
        for n in range(2)
    ]
    place = jnp.stack(places + [my_class]).astype(jnp.int32)

    blocks = piece // ROWS
    acts_specs = [
        pl.BlockSpec((1, 1, queries * each, act_cols), functools.partial(
            lambda x, n, s, order, place: (x, n, tokens // (queries * each), 0), x, n))
        for x in range(width)
        for n in range(2)
    ]
    weighted = pl.pallas_call(
        weigh_kernel,
        grid_spec=pltpu.PrefetchScalarGridSpec(
            num_scalar_prefetch=2,
            grid=(model_size,),
            in_specs=[
                pl.BlockSpec((1, queries * length, 2 * tokens), lambda s, order, place: (s, 0, 0)),
                *acts_specs,
                *acts_specs,
                pl.BlockSpec((1, piece, act_cols), lambda s, order, place: (order[s], 0, 0)),
                pl.BlockSpec((1, piece, act_cols), lambda s, order, place: (order[s], 0, 0)),
            ],
            out_specs=pl.BlockSpec(
                (1, 2 * blocks, queries * ROWS, act_cols), lambda s, order, place: (s, 0, 0, 0)
            ),
            scratch_shapes=[pltpu.VMEM((queries * length, act_cols), bf16)],
        ),
        out_shape=jax.ShapeDtypeStruct((model_size, 2 * blocks, queries * ROWS, act_cols), bf16),
        compiler_params=pltpu.CompilerParams(vmem_limit_bytes=60 * MIB),
        name="weigh",
    )(
        order, place, jnp.stack(query_parts), *([near] * (2 * width)), *([far] * (2 * width)),
        eigen_values[0], other_values,
    )
    weighted = weighted.reshape(model_size * 2 * blocks, queries * ROWS, act_cols)

    def score(first, parts):
        count = len(parts) * 2 * blocks
        part_spec = pl.BlockSpec(
            (1,) + own_grads.shape[1:],
            lambda s, place: (lax.div(place[2 * s], DEPTH // 2 * CORES), 0, 0, 0),
        )
        acts_spec = pl.BlockSpec((1, 2, tokens, act_cols), lambda s, place: (s, 0, 0, 0))
        return pl.pallas_call(
            functools.partial(score_kernel, first * 2 * blocks),
            grid_spec=pltpu.PrefetchScalarGridSpec(
                num_scalar_prefetch=1,
                grid=(width,),
                in_specs=[part_spec] * len(parts)
                + [acts_spec, acts_spec, pl.BlockSpec(memory_space=pl.ANY)],
                out_specs=pl.BlockSpec((targets, queries * ROWS), lambda s, place: (0, 0)),
                scratch_shapes=[
                    pltpu.VMEM((count, targets * ROWS, act_cols), bf16),
                    pltpu.VMEM((count,) + weighted.shape[1:], bf16),
                    pltpu.VMEM((targets * ROWS, queries * ROWS), jnp.float32),
                    pltpu.SemaphoreType.DMA,
                ],
            ),
            out_shape=jax.ShapeDtypeStruct((targets, queries * ROWS), jnp.float32),
            compiler_params=pltpu.CompilerParams(vmem_limit_bytes=60 * MIB),
            name="score",
        )(place, *parts, near, far, weighted)

    scores = score(0, grad_parts[:3]) + score(3, grad_parts[3:])
    partial = scores.reshape(targets, queries, ROWS).sum(axis=2)

    mine = lax.all_to_all(
        partial, "dp", split_axis=0, concat_axis=0, tiled=True, axis_index_groups=classes
    ).sum(axis=0)
    others = model_size * lax.axis_size("section")
    spread = jnp.broadcast_to(mine[None], (others, queries))
    gathered = lax.all_to_all(spread, ("section", "mp"), split_axis=0, concat_axis=0, tiled=True)
    layers = train_acts.shape[0] * lax.axis_size("section")
    normalizer = math.sqrt(
        layers * act_cols * model_size * grad_cols * model_size * SEQLEN * length
    )
    return gathered.sum(axis=0, keepdims=True) / normalizer


def solution(mesh):
    in_specs = (
        P("section", "dp", "mp"),
        P("section", "dp", "mp"),
        P("section", "mp", None),
        P("section", "mp", None),
        P("section", None, "dp", "mp"),
        P("section", "dp", None, "mp"),
        P("section", "dp", None, "mp"),
        P(),
    )
    return jax.shard_map(
        per_device, mesh=mesh, in_specs=in_specs, out_specs=P("dp", None), check_vma=False
    )
```

time: 185 us -> 211 us (1.14)
  between operations: 13.6 us -> 0.21 us
  waiting for transfers between devices: 73.1 us -> 85.4 us
  starting transfers between devices: 21 us -> 32.8 us
  Pallas kernels: 38.5 us -> 46.5 us
  local copies, waits for them, and re-layouts: 2.63 us -> 8.96 us
  other arithmetic: 2.16 us -> 8.16 us
  blocking collectives: 32.9 us -> 28 us
    ppermute x0 -> x7, waiting for transfers between devices: none -> 77.5 us  [the longest x1 38 us: per_device(): pair = jnp.stack([sent, lax.ppermute(sent, 'dp', shifted(dz=2))])]
    all_to_all x1 -> x2, waiting for transfers between devices: 42.2 us -> 1.65 us  [the longest x1 1.65 us: per_device(): lax.all_to_all(slot_acts, 'dp', split_axis=0, concat_axis=0, tiled=True)]
    ppermute x3, waiting for transfers between devices: 30.9 us -> 0.01 us  [per_device(): lax.ppermute(own_query, 'mp', pairs)]
    ppermute x0 -> x7, starting transfers between devices: none -> 9.49 us  [the longest x3 4.84 us: per_device(): lax.ppermute(pair, 'dp', shifted(dx=s))]
    ppermute x3, waiting for transfers between devices: 0.01 us -> 6.15 us  [per_device(): lax.ppermute(own_grads, 'mp', pairs)]
    all_to_all x1 -> x2, starting transfers between devices: 10 us -> 15.2 us  [the longest x1 10 us: per_device(): lax.all_to_all(slot_acts, 'dp', split_axis=0, concat_axis=0, tiled=True)]
    pallas_call x1 -> x2, Pallas kernels: 22.1 us -> 27.2 us  [score(): pl.pallas_call(functools.partial(score_kernel, first * 2 * blocks), grid_...]
    all_to_all x1, blocking collectives: 16.7 us -> 12.7 us  [per_device(): lax.all_to_all(partial, 'dp', split_axis=0, concat_axis=0, tiled=True, ax...]
  transfers between devices with their start and end apart: 8 -> 15, of which waited for: 3 -> 7; matrix products, arithmetic and copies ran while one was open for 1% -> 6% of each run, Pallas kernels for 8% -> 12%
where the time goes in v3:
time: 211 us; the launch traced here: 210 us
  waiting for transfers between devices  85.4 us (40%)
  Pallas kernels  46.5 us (22%)
  starting transfers between devices  32.8 us (16%)
  blocking collectives  28 us (13%)
  local copies, waits for them, and re-layouts  8.96 us (4%)
  other arithmetic  8.16 us (4%)
    ppermute x1, waiting for transfers between devices, per_device(): pair = jnp.stack([sent, lax.ppermute(sent, 'dp', shifted(dz=2))])  38 us
    pallas_call x2, Pallas kernels, score(): pl.pallas_call(functools.partial(score_kernel, first * 2 * blocks), grid_...  27.2 us
    ppermute x3, waiting for transfers between devices, per_device(): lax.ppermute(pair, 'dp', shifted(dx=s))  24 us
    all_to_all x1, blocking collectives, per_device(): lax.all_to_all(spread, ('section', 'mp'), split_axis=0, concat_axis=0, ti...  15.3 us
    all_to_all x1, blocking collectives, per_device(): lax.all_to_all(partial, 'dp', split_axis=0, concat_axis=0, tiled=True, ax...  12.7 us
    ppermute x1, waiting for transfers between devices, per_device(): lax.ppermute(eigen_values[0].astype(bf16), 'dp', shifted(flip_z=1))  10.8 us
    all_to_all x1, starting transfers between devices, per_device(): lax.all_to_all(slot_acts, 'dp', split_axis=0, concat_axis=0, tiled=True)  10 us
    pallas_call x1, Pallas kernels, per_device(): pl.pallas_call(weigh_kernel, grid_spec=pltpu.PrefetchScalarGridSpec(num_s...  9.88 us
  transfers between devices with their start and end apart: 15, of which 7 were waited for; matrix products, arithmetic and copies ran while one was open for 6% of the time, Pallas kernels for 12%

profile of v3, /device:TPU:1, one launch (start us, length us, event | category | flops | bytes accessed | tf_op | source)
XLA Modules:
  0.0 209.9 jit_solution(4440600838396662483)
XLA Ops:
  0.0 2.4 %turn_acts.1 = bf16[160,1024]{1,0:T(8,128)(2,1)} custom-call(bf16[128,1024]{1,0:T(8,128)(2,1)} %bitcast.73, bf16[32,1024]{1,0:T(8,128)(2,1)} %bitcast.79, bf16[1024,512]{1,0:T(8,128)(2,1)} %bitcast.65), custom_call_target="tpu_custom_call" | custom-call | tf_op jit(solution)/shard_map/turn_acts/pallas_call | solution.py:173
  2.4 0.8 slice.22
  3.2 0.7 broadcast_in_dim.53
  3.9 10.0 %all-to-all-start.1 = ((bf16[32,16,128]{2,1,0:T(8,128)(2,1)}), bf16[32,16,128]{2,1,0:T(8,128)(2,1)S(1)}, u32[]{:S(2)}, u32[]{:S(2)}) async-start(bf16[32,16,128]{2,1,0:T(8,128)(2,1)} %bitcast.24), calls=%async_computation.1 | async-start | bytes 262144 | tf_op jit(solution)/shard_map/all_to_all | solution.py:209
  13.9 0.0 copy-done.7
  14.0 7.0 %turn_grads.1 = bf16[16,288,128]{2,1,0:T(8,128)(2,1)} custom-call(bf16[128,3584]{1,0:T(8,128)(2,1)} %bitcast.66, bf16[32,3584]{1,0:T(8,128)(2,1)} %bitcast.74, bf16[3584,512]{1,0:T(8,128)(2,1)} %bitcast.62), custom_call_target="tpu_custom_call" | custom-call | tf_op jit(solution)/shard_map/turn_grads/pallas_call | solution.py:216
  21.0 1.6 all-to-all-done.1
  22.7 5.1 %all-to-all-start = ((bf16[16,288,128]{2,1,0:T(8,128)(2,1)}), bf16[16,288,128]{2,1,0:T(8,128)(2,1)S(1)}, u32[]{:S(2)}, u32[]{:S(2)}) async-start(bf16[16,288,128]{2,1,0:T(8,128)(2,1)} %turn_grads.1), calls=%async_computation | async-start | bytes 2359296 | tf_op jit(solution)/shard_map/all_to_all | solution.py:233
  27.8 0.6 gather_fusion
  28.4 0.1 broadcast_select_fusion.2
  28.5 0.0 slice-done
  28.5 0.1 fusion.4
  28.6 2.4 %collective-permute-start.2 = (bf16[144,1024]{1,0:T(8,128)(2,1)S(1)}, bf16[144,1024]{1,0:T(8,128)(2,1)S(1)}, u32[]{:S(2)}, u32[]{:S(2)}) collective-permute-start(bf16[144,1024]{1,0:T(8,128)(2,1)S(1)} %get-tuple-element.11), channel_id=1, source_target_pairs={{0,16},{4,20},{8,24},{12,28},{16,0},{20,4},{24,8},{28,12},{32,48},... | collective-permute-start | bytes 884744 | tf_op jit(solution)/shard_map/ppermute | solution.py:212
  30.9 38.0 %collective-permute-done.2 = bf16[144,1024]{1,0:T(8,128)(2,1)S(1)} collective-permute-done((bf16[144,1024]{1,0:T(8,128)(2,1)S(1)}, bf16[144,1024]{1,0:T(8,128)(2,1)S(1)}, u32[]{:S(2)}, u32[]{:S(2)}) %collective-permute-start.2) | collective-permute-done | bytes 294944 | tf_op jit(solution)/shard_map/ppermute | solution.py:212
  69.0 0.1 fusion.5
  69.0 1.3 collective-permute-start.3
  70.3 2.4 %collective-permute-start.4 = (bf16[2,144,1024]{2,1,0:T(8,128)(2,1)S(1)}, bf16[2,144,1024]{2,1,0:T(8,128)(2,1)S(1)}, u32[]{:S(2)}, u32[]{:S(2)}) collective-permute-start(bf16[2,144,1024]{2,1,0:T(8,128)(2,1)S(1)} %get-tuple-element.9), channel_id=1, source_target_pairs={{0,64},{4,68},{8,72},{12,76},{16,80},{20,84},{24,88},{28,92},{32,9... | collective-permute-start | bytes 1769480 | tf_op jit(solution)/shard_map/ppermute | solution.py:255
  72.7 1.2 collective-permute-start.5
  73.9 10.4 %collective-permute-done.3 = bf16[2,144,1024]{2,1,0:T(8,128)(2,1)S(1)} collective-permute-done((bf16[2,144,1024]{2,1,0:T(8,128)(2,1)S(1)}, bf16[2,144,1024]{2,1,0:T(8,128)(2,1)S(1)}, u32[]{:S(2)}, u32[]{:S(2)}) %collective-permute-start.3) | collective-permute-done | bytes 589856 | tf_op jit(solution)/shard_map/ppermute | solution.py:255
  84.3 13.5 %collective-permute-done.4 = bf16[2,144,1024]{2,1,0:T(8,128)(2,1)S(1)} collective-permute-done((bf16[2,144,1024]{2,1,0:T(8,128)(2,1)S(1)}, bf16[2,144,1024]{2,1,0:T(8,128)(2,1)S(1)}, u32[]{:S(2)}, u32[]{:S(2)}) %collective-permute-start.4) | collective-permute-done | bytes 589856 | tf_op jit(solution)/shard_map/ppermute | solution.py:255
  97.9 0.0 collective-permute-done.5
  97.9 0.3 pad_maximum_fusion.refs_0_.refs_1_.refs_2_.refs_3_.refs_4_.refs_5_.refs_6_.refs_7_
  98.2 0.0 copy-start
  98.2 1.9 collective-permute-start.6
  100.0 0.0 all-to-all-done
  100.1 0.7 slice.23
  100.8 2.2 %gather_fusion.1 = bf16[8,64,128]{2,1,0:T(8,128)(2,1)} fusion(bf16[16,64,128]{2,1,0:T(8,128)(2,1)} %slice.23, s32[1024]{0:T(1024)S(1)} %pad_clamp_fusion), kind=kCustom, calls=%fused_computation.1 | custom fusion | bytes 262176 | tf_op jit(solution)/shard_map/jit(_take)/gather | solution.py:241
  102.9 1.1 broadcast_select_fusion.1
  104.1 0.1 collective-permute-start.7
  104.2 4.8 %collective-permute-done.7 = bf16[256,256]{1,0:T(8,128)(2,1)S(1)} collective-permute-done((bf16[256,256]{1,0:T(8,128)(2,1)S(1)}, bf16[256,256]{1,0:T(8,128)(2,1)S(1)}, u32[]{:S(2)}, u32[]{:S(2)}) %collective-permute-start.7) | collective-permute-done | bytes 131104 | tf_op jit(solution)/shard_map/ppermute | solution.py:245
  109.0 1.4 collective-permute-start.8
  110.4 1.5 collective-permute-start.9
  111.9 1.6 collective-permute-start.10
  113.4 2.6 %bitcast_convert_fusion = bf16[4,112,1024]{2,1,0:T(8,128)(2,1)} fusion(f32[1,4,112,1024]{3,2,1,0:T(8,128)} %param.12), kind=kLoop, calls=%fused_computation.37 | loop fusion | flops 458752 | bytes 2752512 | tf_op jit(solution)/shard_map/convert_element_type | solution.py:203
  116.0 0.3 collective-permute-start.11
  116.3 1.0 slice.20
  117.3 0.0 copy-done
  117.3 0.0 collective-permute-done.8
  117.3 1.5 collective-permute-start.12
  118.8 0.0 copy-done.2
  118.8 0.0 collective-permute-done.9
  118.8 0.1 collective-permute-start
  118.9 0.0 collective-permute-done.10
  119.0 0.5 copy-done.4
  119.5 0.6 copy-done.5
  120.1 2.1 %collective-permute-start.1 = (bf16[4,4,224,128]{3,2,1,0:T(8,128)(2,1)}, bf16[4,4,224,128]{3,2,1,0:T(8,128)(2,1)}, u32[]{:S(2)}, u32[]{:S(2)}) collective-permute-start(bf16[4,4,224,128]{3,2,1,0:T(8,128)(2,1)} %bitcast.20.refs_0_), channel_id=1, source_target_pairs={{0,3},{1,0},{2,1},{3,2},{4,7},{5,4},{6,5},{7,6},{8,11},{9,8},{10,9... | collective-permute-start | bytes 2752520 | tf_op jit(solution)/shard_map/ppermute | solution.py:249
  122.3 0.7 stack.125.place_ref
  122.9 0.6 pad_add_fusion.order_ref
  123.5 2.0 pad_maximum_fusion.2.grads_ref
  125.5 10.8 %collective-permute-done.11.refs_17_ = bf16[4,112,1024]{2,1,0:T(8,128)(2,1)} collective-permute-done((bf16[4,112,1024]{2,1,0:T(8,128)(2,1)}, bf16[4,112,1024]{2,1,0:T(8,128)(2,1)}, u32[]{:S(2)}, u32[]{:S(2)}) %collective-permute-start.11) | collective-permute-done | bytes 917536 | tf_op jit(solution)/shard_map/ppermute | solution.py:203
  136.2 0.0 collective-permute-done.6.refs_8_.refs_9_.refs_10_.refs_11_.refs_12_.refs_13_.refs_14_.refs_15_.refs_4_.refs_2_
  136.2 9.9 %weigh.1 = bf16[4,14,128,1024]{3,2,1,0:T(8,128)(2,1)} custom-call(s32[4]{0:T(128)} %pad_add_fusion.order_ref, s32[17]{0:T(128)} %stack.125.place_ref, bf16[4,256,256]{2,1,0:T(8,128)(2,1)} %pad_maximum_fusion.2.grads_ref, bf16[4,2,144,1024]{3,2,1,0:T(8,128)(2,1)} %copy-done, bf16[4,2,144,1024]{3,2,1,0:T(8,128)(2,1)} %copy-done, ...), custom_call_target="tpu_custom_call" | custom-call | tf_op jit(solution)/shard_map/weigh/pallas_call | solution.py:273
  146.1 0.0 collective-permute-done.12.refs_0_
  146.1 8.8 %score.3 = f32[16,128]{1,0:T(8,128)} custom-call(s32[17]{0:T(128)} %stack.125.place_ref, bf16[4,4,224,128]{3,2,1,0:T(8,128)(2,1)} %collective-permute-done.12.refs_0_, bf16[4,2,144,1024]{3,2,1,0:T(8,128)(2,1)} %copy-done, bf16[4,2,144,1024]{3,2,1,0:T(8,128)(2,1)} %collective-permute-done.6.refs_8_.refs_9_.refs_10_.refs_11_.refs_12_.refs_13_.refs_14_.refs_15_.refs_4_.refs_2_, ...), custom_call_target="tpu_custom_call" | custom-call | tf_op jit(solution)/shard_map/score/pallas_call | solution.py:306
  154.9 6.1 %collective-permute-done.refs_1_ = bf16[4,4,224,128]{3,2,1,0:T(8,128)(2,1)S(1)} collective-permute-done((bf16[4,4,224,128]{3,2,1,0:T(8,128)(2,1)}, bf16[4,4,224,128]{3,2,1,0:T(8,128)(2,1)S(1)}, u32[]{:S(2)}, u32[]{:S(2)}) %collective-permute-start) | collective-permute-done | bytes 917536 | tf_op jit(solution)/shard_map/ppermute | solution.py:249
  161.1 0.0 collective-permute-done.1.refs_2_
  161.1 1.0 copy-done.1
  162.0 18.4 %score.2 = f32[16,128]{1,0:T(8,128)} custom-call(s32[17]{0:T(128)} %stack.125.place_ref, bf16[4,4,224,128]{3,2,1,0:T(8,128)(2,1)} %bitcast.20.refs_0_, bf16[4,4,224,128]{3,2,1,0:T(8,128)(2,1)} %copy-done.1, bf16[4,4,224,128]{3,2,1,0:T(8,128)(2,1)} %collective-permute-done.1.refs_2_, bf16[4,2,144,1024]{3,2,1,0:T(8,128)(2,1)} %copy-done, ...), custom_call_target="tpu_custom_call" | custom-call | tf_op jit(solution)/shard_map/score/pallas_call | solution.py:306
  180.5 0.7 add.315
  181.2 0.1 reshape.57
  181.3 0.1 reduce_sum.27
  181.4 12.7 %all_to_all.25 = f32[16,1,8]{2,1,0:T(1,128)S(1)} all-to-all(f32[16,1,8]{2,1,0:T(1,128)S(1)} %bitcast.80), channel_id=1, replica_groups={{0,4,16,20,32,36,48,52,64,68,80,84,96,100,112,116},{8,12,24,28,40,44,56..., dimensions={0} | all-to-all | bytes 1024 | tf_op jit(solution)/shard_map/all_to_all | solution.py:329
  194.1 15.3 %all_to_all.26 = f32[8,1,8]{2,1,0:T(1,128)S(1)} all-to-all(f32[8,1,8]{2,1,0:T(1,128)S(1)} %broadcast_in_dim.61), channel_id=1, replica_groups=mesh['section'=2,'dp'=32,'mp'=4] {'section','mp'}, dimensions={0} | all-to-all | bytes 512 | tf_op jit(solution)/shard_map/all_to_all | solution.py:334
  209.4 0.5 multiply_bitcast_fusion
  (22 shorter events, 0.2 us)
Async XLA Ops:
  0.0 13.9 %copy-start.7 = (s32[8]{0:T(128)S(1)}, s32[8]{0:T(128)}, u32[]{:S(2)}) copy-start(s32[8]{0:T(128)} %param.15) | copy-start | bytes 100
  3.9 18.7 %all-to-all-start.1 = ((bf16[32,16,128]{2,1,0:T(8,128)(2,1)}), bf16[32,16,128]{2,1,0:T(8,128)(2,1)S(1)}, u32[]{:S(2)}, u32[]{:S(2)}) async-start(bf16[32,16,128]{2,1,0:T(8,128)(2,1)} %bitcast.24), calls=%async_computation.1 | async-start | bytes 262144 | tf_op jit(solution)/shard_map/all_to_all | solution.py:209
  21.0 7.5 %slice-start = ((bf16[160,1024]{1,0:T(8,128)(2,1)}), bf16[128,1024]{1,0:T(8,128)(2,1)S(1)}, s32[]{:S(2)}) async-start(bf16[160,1024]{1,0:T(8,128)(2,1)} %turn_acts.1), calls=%async_computation.4 | async-start | bytes 524288 | tf_op jit(solution)/shard_map/slice | solution.py:211
  22.7 77.4 %all-to-all-start = ((bf16[16,288,128]{2,1,0:T(8,128)(2,1)}), bf16[16,288,128]{2,1,0:T(8,128)(2,1)S(1)}, u32[]{:S(2)}, u32[]{:S(2)}) async-start(bf16[16,288,128]{2,1,0:T(8,128)(2,1)} %turn_grads.1), calls=%async_computation | async-start | bytes 2359296 | tf_op jit(solution)/shard_map/all_to_all | solution.py:233
  28.6 40.4 %collective-permute-start.2 = (bf16[144,1024]{1,0:T(8,128)(2,1)S(1)}, bf16[144,1024]{1,0:T(8,128)(2,1)S(1)}, u32[]{:S(2)}, u32[]{:S(2)}) collective-permute-start(bf16[144,1024]{1,0:T(8,128)(2,1)S(1)} %get-tuple-element.11), channel_id=1, source_target_pairs={{0,16},{4,20},{8,24},{12,28},{16,0},{20,4},{24,8},{28,12},{32,48},... | collective-permute-start | bytes 884744 | tf_op jit(solution)/shard_map/ppermute | solution.py:212
  69.0 15.3 %collective-permute-start.3 = (bf16[2,144,1024]{2,1,0:T(8,128)(2,1)S(1)}, bf16[2,144,1024]{2,1,0:T(8,128)(2,1)S(1)}, u32[]{:S(2)}, u32[]{:S(2)}) collective-permute-start(bf16[2,144,1024]{2,1,0:T(8,128)(2,1)S(1)} %get-tuple-element.9), channel_id=1, source_target_pairs={{0,32},{4,36},{8,40},{12,44},{16,48},{20,52},{24,56},{28,60},{32,6... | collective-permute-start | bytes 1769480 | tf_op jit(solution)/shard_map/ppermute | solution.py:255
  70.3 27.5 %collective-permute-start.4 = (bf16[2,144,1024]{2,1,0:T(8,128)(2,1)S(1)}, bf16[2,144,1024]{2,1,0:T(8,128)(2,1)S(1)}, u32[]{:S(2)}, u32[]{:S(2)}) collective-permute-start(bf16[2,144,1024]{2,1,0:T(8,128)(2,1)S(1)} %get-tuple-element.9), channel_id=1, source_target_pairs={{0,64},{4,68},{8,72},{12,76},{16,80},{20,84},{24,88},{28,92},{32,9... | collective-permute-start | bytes 1769480 | tf_op jit(solution)/shard_map/ppermute | solution.py:255
  72.7 25.1 %collective-permute-start.5 = (bf16[2,144,1024]{2,1,0:T(8,128)(2,1)S(1)}, bf16[2,144,1024]{2,1,0:T(8,128)(2,1)S(1)}, u32[]{:S(2)}, u32[]{:S(2)}) collective-permute-start(bf16[2,144,1024]{2,1,0:T(8,128)(2,1)S(1)} %get-tuple-element.9), channel_id=1, source_target_pairs={{0,96},{4,100},{8,104},{12,108},{16,112},{20,116},{24,120},{28,124... | collective-permute-start | bytes 1769480 | tf_op jit(solution)/shard_map/ppermute | solution.py:255
  98.2 19.2 %copy-start = (bf16[4,2,144,1024]{3,2,1,0:T(8,128)(2,1)}, bf16[4,2,144,1024]{3,2,1,0:T(8,128)(2,1)S(1)}, u32[]{:S(2)}) copy-start(bf16[4,2,144,1024]{3,2,1,0:T(8,128)(2,1)S(1)} %pad_maximum_fusion.refs_0_.refs_1_.refs_2_.refs_3_.refs_4_.refs_5_.refs_6_.refs_7_) | copy-start | bytes 7077892
  98.2 38.1 %collective-permute-start.6 = (bf16[4,2,144,1024]{3,2,1,0:T(8,128)(2,1)S(1)}, bf16[4,2,144,1024]{3,2,1,0:T(8,128)(2,1)}, u32[]{:S(2)}, u32[]{:S(2)}) collective-permute-start(bf16[4,2,144,1024]{3,2,1,0:T(8,128)(2,1)S(1)} %pad_maximum_fusion.refs_0_.refs_1_.refs_2_.refs_3_.refs_4_.refs_5_.refs_6_.refs_7_), channel_id=1, source_target_pairs={{0,4},{4,0},{8,12},{12,8},{16,20},{20,16},{24,28},{28,24},{32,36},... | collective-permute-start | bytes 7077896 | tf_op jit(solution)/shard_map/ppermute | solution.py:256
  104.1 4.9 %collective-permute-start.7 = (bf16[256,256]{1,0:T(8,128)(2,1)S(1)}, bf16[256,256]{1,0:T(8,128)(2,1)S(1)}, u32[]{:S(2)}, u32[]{:S(2)}) collective-permute-start(bf16[256,256]{1,0:T(8,128)(2,1)S(1)} %bitcast.75), channel_id=1, source_target_pairs={{0,8},{4,12},{8,0},{12,4},{16,24},{20,28},{24,16},{28,20},{32,40},... | collective-permute-start | bytes 393224 | tf_op jit(solution)/shard_map/ppermute | solution.py:245
  109.0 9.9 %copy-start.2 = (bf16[256,256]{1,0:T(8,128)(2,1)}, bf16[256,256]{1,0:T(8,128)(2,1)S(1)}, u32[]{:S(2)}) copy-start(bf16[256,256]{1,0:T(8,128)(2,1)S(1)} %fusion.3) | copy-start | bytes 393220
  109.0 8.4 %collective-permute-start.8 = (bf16[256,256]{1,0:T(8,128)(2,1)S(1)}, bf16[256,256]{1,0:T(8,128)(2,1)S(1)}, u32[]{:S(2)}, u32[]{:S(2)}) collective-permute-start(bf16[256,256]{1,0:T(8,128)(2,1)S(1)} %fusion.3), channel_id=1, source_target_pairs={{0,1},{1,2},{2,3},{3,0},{4,5},{5,6},{6,7},{7,4},{8,9},{9,10},{10,1... | collective-permute-start | bytes 393224 | tf_op jit(solution)/shard_map/ppermute | solution.py:250
  110.4 8.5 %collective-permute-start.9 = (bf16[256,256]{1,0:T(8,128)(2,1)S(1)}, bf16[256,256]{1,0:T(8,128)(2,1)S(1)}, u32[]{:S(2)}, u32[]{:S(2)}) collective-permute-start(bf16[256,256]{1,0:T(8,128)(2,1)S(1)} %fusion.3), channel_id=1, source_target_pairs={{0,3},{1,0},{2,1},{3,2},{4,7},{5,4},{6,5},{7,6},{8,11},{9,8},{10,9... | collective-permute-start | bytes 393224 | tf_op jit(solution)/shard_map/ppermute | solution.py:250
  111.9 7.0 %collective-permute-start.10 = (bf16[256,256]{1,0:T(8,128)(2,1)S(1)}, bf16[256,256]{1,0:T(8,128)(2,1)S(1)}, u32[]{:S(2)}, u32[]{:S(2)}) collective-permute-start(bf16[256,256]{1,0:T(8,128)(2,1)S(1)} %fusion.3), channel_id=1, source_target_pairs={{0,2},{1,3},{2,0},{3,1},{4,6},{5,7},{6,4},{7,5},{8,10},{9,11},{10,... | collective-permute-start | bytes 393224 | tf_op jit(solution)/shard_map/ppermute | solution.py:250
  116.0 20.2 %collective-permute-start.11 = (bf16[4,112,1024]{2,1,0:T(8,128)(2,1)}, bf16[4,112,1024]{2,1,0:T(8,128)(2,1)}, u32[]{:S(2)}, u32[]{:S(2)}) collective-permute-start(bf16[4,112,1024]{2,1,0:T(8,128)(2,1)} %bitcast_convert_fusion), channel_id=1, source_target_pairs={{0,8},{4,12},{8,0},{12,4},{16,24},{20,28},{24,16},{28,20},{32,40},... | collective-permute-start | bytes 2752520 | tf_op jit(solution)/shard_map/ppermute | solution.py:203
  117.3 1.6 copy-start.3
  117.3 28.8 %collective-permute-start.12 = (bf16[4,4,224,128]{3,2,1,0:T(8,128)(2,1)}, bf16[4,4,224,128]{3,2,1,0:T(8,128)(2,1)}, u32[]{:S(2)}, u32[]{:S(2)}) collective-permute-start(bf16[4,4,224,128]{3,2,1,0:T(8,128)(2,1)} %bitcast.20.refs_0_), channel_id=1, source_target_pairs={{0,2},{1,3},{2,0},{3,1},{4,6},{5,7},{6,4},{7,5},{8,10},{9,11},{10,... | collective-permute-start | bytes 2752520 | tf_op jit(solution)/shard_map/ppermute | solution.py:249
  118.8 0.7 copy-start.4
  118.8 42.2 %collective-permute-start = (bf16[4,4,224,128]{3,2,1,0:T(8,128)(2,1)}, bf16[4,4,224,128]{3,2,1,0:T(8,128)(2,1)S(1)}, u32[]{:S(2)}, u32[]{:S(2)}) collective-permute-start(bf16[4,4,224,128]{3,2,1,0:T(8,128)(2,1)} %bitcast.20.refs_0_), channel_id=1, source_target_pairs={{0,1},{1,2},{2,3},{3,0},{4,5},{5,6},{6,7},{7,4},{8,9},{9,10},{10,1... | collective-permute-start | bytes 2752520 | tf_op jit(solution)/shard_map/ppermute | solution.py:249
  119.5 0.6 copy-start.5
  120.1 40.9 %collective-permute-start.1 = (bf16[4,4,224,128]{3,2,1,0:T(8,128)(2,1)}, bf16[4,4,224,128]{3,2,1,0:T(8,128)(2,1)}, u32[]{:S(2)}, u32[]{:S(2)}) collective-permute-start(bf16[4,4,224,128]{3,2,1,0:T(8,128)(2,1)} %bitcast.20.refs_0_), channel_id=1, source_target_pairs={{0,3},{1,0},{2,1},{3,2},{4,7},{5,4},{6,5},{7,6},{8,11},{9,8},{10,9... | collective-permute-start | bytes 2752520 | tf_op jit(solution)/shard_map/ppermute | solution.py:249
  154.9 25.6 %copy-start.6 = (f32[16,128]{1,0:T(8,128)S(1)}, f32[16,128]{1,0:T(8,128)}, u32[]{:S(2)}) copy-start(f32[16,128]{1,0:T(8,128)} %score.3) | copy-start | bytes 24580
  161.1 1.0 copy-start.1

commit v4 on v3

v4 whole, which is shorter than its diff:
```python
import functools
import math

import jax
import jax.numpy as jnp
from jax import lax
from jax.experimental import pallas as pl
from jax.experimental.pallas import tpu as pltpu
from jax.sharding import PartitionSpec as P

SEQLEN = 128
DAMPING = 0.1
ROWS = 16
CORES = 2
DEPTH = 4
MIB = 1 << 20


def tile_of(target, side):
    x, rest = divmod(target, DEPTH)
    z, core = divmod(rest, CORES)
    return (x * DEPTH + 2 * z + side) * CORES + core


def turn_acts_kernel(train_ref, query_ref, basis_ref, out_ref):
    rows = jnp.concatenate([train_ref[...], query_ref[...]], axis=0)
    out_ref[...] = jnp.dot(
        rows, basis_ref[...], preferred_element_type=jnp.float32
    ).astype(jnp.bfloat16)


def turn_grads_kernel(train_ref, query_ref, basis_ref, out_ref, turned, slots):
    step = pl.program_id(0)
    steps = pl.num_programs(0)
    size = basis_ref.shape[1]
    tokens = train_ref.shape[0]
    rows = jnp.concatenate([train_ref[...], query_ref[...]], axis=0)
    product = jnp.dot(rows, basis_ref[...], preferred_element_type=jnp.float32)
    turned[step] = product[:tokens].T.astype(jnp.bfloat16)
    slots[step] = product[tokens:]

    @pl.when(step == steps - 1)
    def _():
        targets, _, lanes = out_ref.shape
        total = turned.shape[0] * size
        piece = total // (2 * targets)
        length = slots.shape[1]
        for target in range(targets):
            for side in range(2):
                start = tile_of(target, side) * piece
                parts = []
                at = start
                while at < start + piece:
                    block = at // size
                    end = min(start + piece, (block + 1) * size)
                    parts.append(turned[block, at - block * size : end - block * size, :])
                    at = end
                rows = parts[0] if len(parts) == 1 else jnp.concatenate(parts, axis=0)
                out_ref[target, side * piece : (side + 1) * piece, :] = rows
                first = start // lanes
                tiles = []
                for tile in range(first, min(first + 2, total // lanes)):
                    col = tile * lanes
                    block = col // size
                    tiles.append(slots[block, :, col - block * size : col - block * size + lanes])
                window = jnp.concatenate(tiles, axis=1) if len(tiles) > 1 else tiles[0]
                shift = start - first * lanes
                if shift:
                    window = pltpu.roll(window, window.shape[1] - shift, 1)
                at = 2 * piece + side * length
                out_ref[target, at : at + length, :] = window[:, :lanes].astype(jnp.bfloat16)


def grams_of(step, steps, place_ref, part_refs, near_ref, far_ref, grams):
    blocks = grams.shape[0]
    pairs = near_ref.shape[1]
    for far, acts_ref in enumerate((near_ref, far_ref)):
        for n in range(pairs):
            place = place_ref[(far * steps + step) * pairs + n]
            inner = lax.rem(place, CORES * pairs)
            grads = jnp.concatenate([part[0, inner] for part in part_refs], axis=0)
            gram = jnp.dot(grads, acts_ref[0, n], preferred_element_type=jnp.float32)
            gram = gram.astype(jnp.bfloat16)
            start = pl.multiple_of(place * ROWS, ROWS)
            for b in range(blocks):
                grams[b, pl.ds(start, ROWS), :] = gram[b * ROWS : (b + 1) * ROWS]


def scores_of(grams, weighted, totals, out_ref):
    totals[...] = jnp.zeros_like(totals)
    group = 7

    @pl.loop(0, grams.shape[0] // group)
    def _(g):
        for b in range(group):
            totals[...] += lax.dot_general(
                grams[g * group + b],
                weighted[g * group + b],
                (((1,), (1,)), ((), ())),
                preferred_element_type=jnp.float32,
            )

    shape = totals.shape
    same = (
        lax.broadcasted_iota(jnp.int32, shape, 0) % ROWS
        == lax.broadcasted_iota(jnp.int32, shape, 1) % ROWS
    )
    kept = jnp.where(same, totals[...], 0.0)
    out_ref[...] = jnp.sum(kept.reshape(-1, ROWS, shape[1]), axis=1)


def first_kernel(length, order_ref, place_ref, *refs):
    (query_ref, query_acts_ref, own_ref, other_ref), refs = refs[:4], refs[4:]
    part_refs, refs = refs[:-7], refs[-7:]
    near_ref, far_ref, out_ref, last_ref, grams, weighted, totals = refs
    step = pl.program_id(0)
    steps = pl.num_programs(0)
    queries = query_acts_ref.shape[0] // length
    turned = query_ref[0].astype(jnp.float32).T
    shape = (queries * ROWS, queries * length)
    own = (
        lax.broadcasted_iota(jnp.int32, shape, 0) // ROWS
        == lax.broadcasted_iota(jnp.int32, shape, 1) // length
    )
    blocks = own_ref.shape[1] // ROWS
    lanes = query_ref.shape[2] // 2
    side_of_own = place_ref[4 * steps]
    for side in range(2):
        mine = side_of_own == side
        for b in range(blocks):
            rows = slice(b * ROWS, (b + 1) * ROWS)
            part = turned[side * lanes + b * ROWS : side * lanes + (b + 1) * ROWS]
            spread = jnp.concatenate([part] * queries, axis=0)
            spread = jnp.where(own, spread, 0.0).astype(jnp.bfloat16)
            moments = jnp.dot(spread, query_acts_ref[...], preferred_element_type=jnp.float32)
            values = jnp.where(mine, own_ref[0, rows, :], other_ref[0, rows, :].astype(jnp.float32))
            inverse = 1.0 / (values + DAMPING)
            moments = moments.reshape(queries, ROWS, moments.shape[1]) * inverse[None]
            moments = moments.reshape(queries * ROWS, moments.shape[2]).astype(jnp.bfloat16)
            weighted[step * (2 * blocks) + side * blocks + b] = moments

    grams_of(step, steps, place_ref, part_refs, near_ref, far_ref, grams)

    @pl.when(step == steps - 1)
    def _():
        last_ref[...] = weighted[(steps - 1) * 2 * blocks :]
        scores_of(grams, weighted, totals, out_ref)


def last_kernel(place_ref, low_ref, high_ref, near_ref, far_ref, weighted_ref, out_ref, grams, totals):
    step = pl.program_id(0)
    steps = pl.num_programs(0)
    grams_of(step, steps, place_ref, [low_ref, high_ref], near_ref, far_ref, grams)

    @pl.when(step == steps - 1)
    def _():
        scores_of(grams, weighted_ref, totals, out_ref)


def per_device(
    train_acts, train_grads, basis_in, basis_out, eigen_values, query_acts, query_grads, query_owner
):
    block_size = basis_in.shape[2]
    tokens, act_cols = train_acts.shape[1:]
    grad_cols = train_grads.shape[2]
    length = query_acts.shape[2]
    queries = query_owner.shape[0]
    data_size = lax.axis_size("dp")
    model_size = lax.axis_size("mp")
    piece = grad_cols // data_size
    bf16 = jnp.bfloat16

    turned_acts = pl.pallas_call(
        turn_acts_kernel,
        grid=(act_cols // block_size,),
        in_specs=[
            pl.BlockSpec((tokens, block_size), lambda s: (0, s)),
            pl.BlockSpec((length, block_size), lambda s: (0, s)),
            pl.BlockSpec((block_size, block_size), lambda s: (s, 0)),
        ],
        out_specs=pl.BlockSpec((tokens + length, block_size), lambda s: (0, s)),
        out_shape=jax.ShapeDtypeStruct((tokens + length, act_cols), bf16),
        compiler_params=pltpu.CompilerParams(vmem_limit_bytes=60 * MIB),
        name="turn_acts",
    )(train_acts[0], query_acts[0, 0], basis_in[0])
    width = data_size // (DEPTH * CORES)
    targets = data_size // 2
    classes = [[tile_of(t, parity) for t in range(targets)] for parity in range(2)]
    where = [(x, z, c) for x in range(width) for z in range(DEPTH) for c in range(CORES)]

    def shifted(dx=0, dz=0, flip_z=0, flip_c=0):
        at = lambda x, z, c: (x % width * DEPTH + z % DEPTH) * CORES + c
        return [
            (at(x, z, c), at(x + dx, (z + dz) % DEPTH ^ flip_z, c ^ flip_c)) for x, z, c in where
        ]

    data_index = lax.axis_index("dp")
    my_x = data_index // (DEPTH * CORES)
    my_z = data_index // CORES % DEPTH
    my_core = data_index % CORES
    my_class = my_z % 2

    other_values = lax.ppermute(eigen_values[0].astype(bf16), "dp", shifted(flip_z=1))

    other_acts = lax.ppermute(turned_acts, "dp", shifted(dz=2))

    steps = grad_cols // block_size
    rows = 2 * (piece + length)
    pieces = pl.pallas_call(
        turn_grads_kernel,
        grid=(steps,),
        in_specs=[
            pl.BlockSpec((tokens, block_size), lambda s: (0, s)),
            pl.BlockSpec((length, block_size), lambda s: (0, s)),
            pl.BlockSpec((block_size, block_size), lambda s: (s, 0)),
        ],
        out_specs=pl.BlockSpec((targets, rows, tokens), lambda s: (0, 0, 0)),
        out_shape=jax.ShapeDtypeStruct((targets, rows, tokens), bf16),
        scratch_shapes=[
            pltpu.VMEM((steps, block_size, tokens), bf16),
            pltpu.VMEM((steps, length, block_size), jnp.float32),
        ],
        compiler_params=pltpu.CompilerParams(vmem_limit_bytes=60 * MIB),
        name="turn_grads",
    )(train_grads[0], query_grads[0, 0], basis_out[0])
    turned_acts, other_acts, pieces = lax.optimization_barrier((turned_acts, other_acts, pieces))
    pair = jnp.stack([turned_acts, other_acts])
    moved = lax.all_to_all(
        pieces, "dp", split_axis=0, concat_axis=0, tiled=True, axis_index_groups=classes
    )
    others_x = [lax.ppermute(pair, "dp", shifted(dx=s)) for s in range(1, width)]
    moved, other_values, pair, *others_x = lax.optimization_barrier(
        (moved, other_values, pair, *others_x)
    )
    near = jnp.stack([pair] + others_x)
    own_grads = moved[:, : 2 * piece].reshape(width, DEPTH // 2 * CORES, 2 * piece, tokens)

    owner_x = query_owner // (DEPTH * CORES)
    owner_z = query_owner // CORES % DEPTH
    owner_core = query_owner % CORES
    in_class = (owner_z % 2 == my_class)[:, None, None]
    owner_place = (owner_x * (DEPTH // 2) + owner_z // 2) * CORES + owner_core
    chosen = jnp.take(moved[:, 2 * piece :], owner_place, axis=0)
    chosen = jnp.where(in_class, chosen, 0).astype(bf16)
    chosen = chosen.reshape(queries, 2, length, tokens).transpose(0, 2, 1, 3)
    chosen = chosen.reshape(queries * length, 2 * tokens)
    own_query = chosen + lax.ppermute(chosen, "dp", shifted(flip_z=1))

    ring = range(model_size)
    shifts = [[(i, (i + s) % model_size) for i in ring] for s in (1, model_size - 1, 2)]
    grad_parts = [own_grads] + [lax.ppermute(own_grads, "mp", pairs) for pairs in shifts[:2]]
    opposite = [
        lax.ppermute(grad_parts[1][:, :, :piece], "mp", shifts[0]),
        lax.ppermute(grad_parts[2][:, :, piece:], "mp", shifts[1]),
    ]
    own_query = jnp.broadcast_to(own_query[None], (model_size,) + own_query.shape)
    query_parts = lax.all_to_all(own_query, "mp", split_axis=0, concat_axis=0, tiled=True)
    model_index = lax.axis_index("mp")
    order = jnp.stack([(model_index + s) % model_size for s in (0, model_size - 1, 1, 2)])
    order = order.astype(jnp.int32)

    far = lax.ppermute(near, "dp", shifted(flip_c=1))
    places = [
        ((my_x + width - s) % width * (DEPTH // 2) + (my_z // 2 + n) % 2) * CORES
        + (my_core + flip) % CORES
        for flip in range(2)
        for s in range(width)
        for n in range(2)
    ]
    place = jnp.stack(places + [my_class]).astype(jnp.int32)

    slots = jnp.concatenate([near[:, :, tokens:], far[:, :, tokens:]], axis=0)
    slots = slots.reshape(CORES * width * 2, length, act_cols)
    relative = (owner_core ^ my_core) * width + (my_x + width - owner_x) % width
    relative = relative * 2 + (owner_z // 2 ^ my_z // 2)
    chosen_acts = jnp.where(in_class, jnp.take(slots, relative, axis=0), 0).astype(bf16)
    _, chosen_acts = lax.optimization_barrier((own_query, chosen_acts))
    chosen_acts = chosen_acts.reshape(queries * length, act_cols)
    chosen_acts = chosen_acts + lax.ppermute(chosen_acts, "dp", shifted(flip_z=1))

    blocks = piece // ROWS
    early = model_size - 1
    part_block = (1,) + own_grads.shape[1:]
    half_block = (1,) + opposite[0].shape[1:]
    acts_block = (1, 2, tokens, act_cols)
    weighted_shape = (2 * blocks, queries * ROWS, act_cols)
    total_shape = (targets * ROWS, queries * ROWS)
    score_shape = jax.ShapeDtypeStruct((targets, queries * ROWS), jnp.float32)

    def x_of(place, s):
        return lax.div(place[2 * s], DEPTH // 2 * CORES)

    work = 4 * targets * tokens * 2 * piece * act_cols
    early_scores, last_weighted = pl.pallas_call(
        functools.partial(first_kernel, length),
        grid_spec=pltpu.PrefetchScalarGridSpec(
            num_scalar_prefetch=2,
            grid=(width,),
            in_specs=[
                pl.BlockSpec(
                    (1, queries * length, 2 * tokens), lambda s, order, place: (order[s], 0, 0)
                ),
                pl.BlockSpec((queries * length, act_cols), lambda s, order, place: (0, 0)),
                pl.BlockSpec((1, piece, act_cols), lambda s, order, place: (order[s], 0, 0)),
                pl.BlockSpec((1, piece, act_cols), lambda s, order, place: (order[s], 0, 0)),
            ]
            + [pl.BlockSpec(part_block, lambda s, order, place: (x_of(place, s), 0, 0, 0))] * early
            + [pl.BlockSpec(acts_block, lambda s, order, place: (s, 0, 0, 0))] * 2,
            out_specs=[
                pl.BlockSpec(score_shape.shape, lambda s, order, place: (0, 0)),
                pl.BlockSpec(weighted_shape, lambda s, order, place: (0, 0, 0)),
            ],
            scratch_shapes=[
                pltpu.VMEM((early * 2 * blocks, targets * ROWS, act_cols), bf16),
                pltpu.VMEM((model_size * 2 * blocks,) + weighted_shape[1:], bf16),
                pltpu.VMEM(total_shape, jnp.float32),
            ],
        ),
        out_shape=[score_shape, jax.ShapeDtypeStruct(weighted_shape, bf16)],
        compiler_params=pltpu.CompilerParams(vmem_limit_bytes=60 * MIB),
        cost_estimate=pl.CostEstimate(flops=early * work, bytes_accessed=16 * MIB, transcendentals=0),
        name="first_scores",
    )(order, place, query_parts, chosen_acts, eigen_values[0], other_values,
      *grad_parts[:early], near, far)
    last_scores = pl.pallas_call(
        last_kernel,
        grid_spec=pltpu.PrefetchScalarGridSpec(
            num_scalar_prefetch=1,
            grid=(width,),
            in_specs=[
                *[pl.BlockSpec(half_block, lambda s, place: (x_of(place, s), 0, 0, 0))] * 2,
                pl.BlockSpec(acts_block, lambda s, place: (s, 0, 0, 0)),
                pl.BlockSpec(acts_block, lambda s, place: (s, 0, 0, 0)),
                pl.BlockSpec(weighted_shape, lambda s, place: (0, 0, 0)),
            ],
            out_specs=pl.BlockSpec(score_shape.shape, lambda s, place: (0, 0)),
            scratch_shapes=[
                pltpu.VMEM((2 * blocks, targets * ROWS, act_cols), bf16),
                pltpu.VMEM(total_shape, jnp.float32),
            ],
        ),
        out_shape=score_shape,
        compiler_params=pltpu.CompilerParams(vmem_limit_bytes=60 * MIB),
        cost_estimate=pl.CostEstimate(flops=work, bytes_accessed=9 * MIB, transcendentals=0),
        name="last_scores",
    )(place, *opposite, near, far, last_weighted)
    scores = early_scores + last_scores
    partial = scores.reshape(targets, queries, ROWS).sum(axis=2)

    mine = lax.all_to_all(
        partial, "dp", split_axis=0, concat_axis=0, tiled=True, axis_index_groups=classes
    ).sum(axis=0)
    others = model_size * lax.axis_size("section")
    spread = jnp.broadcast_to(mine[None], (others, queries))
    gathered = lax.all_to_all(spread, ("section", "mp"), split_axis=0, concat_axis=0, tiled=True)
    layers = train_acts.shape[0] * lax.axis_size("section")
    normalizer = math.sqrt(
        layers * act_cols * model_size * grad_cols * model_size * SEQLEN * length
    )
    return gathered.sum(axis=0, keepdims=True) / normalizer


def solution(mesh):
    in_specs = (
        P("section", "dp", "mp"),
        P("section", "dp", "mp"),
        P("section", "mp", None),
        P("section", "mp", None),
        P("section", None, "dp", "mp"),
        P("section", "dp", None, "mp"),
        P("section", "dp", None, "mp"),
        P(),
    )
    return jax.shard_map(
        per_device, mesh=mesh, in_specs=in_specs, out_specs=P("dp", None), check_vma=False
    )
```

time: 211 us -> 174 us (0.82)
  waiting for transfers between devices: 85.4 us -> 49.7 us
  Pallas kernels: 46.5 us -> 41.1 us
  local copies, waits for them, and re-layouts: 8.96 us -> 12.3 us
    ppermute x4, waiting for transfers between devices: 38 us -> 7.01 us  [the longest x1 7 us: per_device(): other_acts = lax.ppermute(turned_acts, 'dp', shifted(dz=2))]
    ppermute x1, waiting for transfers between devices: 10.8 us -> 26.4 us  [per_device(): lax.ppermute(eigen_values[0].astype(bf16), 'dp', shifted(flip_z=1))]
    ppermute x3, waiting for transfers between devices: 24 us -> 8.51 us  [per_device(): lax.ppermute(pair, 'dp', shifted(dx=s))]
    all_to_all x1, starting transfers between devices: 10 us -> 4.29 us  [per_device(): lax.all_to_all(own_query, 'mp', split_axis=0, concat_axis=0, tiled=True)]
    pallas_call x3 -> x2, Pallas kernels: 37.1 us -> 31.8 us  [the longest x1 22.3 us: per_device(): pl.pallas_call(functools.partial(first_kernel, length), grid_spec=pltpu.P...]
    ppermute x1, waiting for transfers between devices: 4.79 us -> 0.01 us  [per_device(): own_query = chosen + lax.ppermute(chosen, 'dp', shifted(flip_z=1))]
    ppermute x1, starting transfers between devices: 0.09 us -> 3.36 us  [per_device(): own_query = chosen + lax.ppermute(chosen, 'dp', shifted(flip_z=1))]
    ppermute x1, starting transfers between devices: 0.32 us -> 3.37 us  [per_device(): lax.ppermute(eigen_values[0].astype(bf16), 'dp', shifted(flip_z=1))]
  transfers between devices with their start and end apart: 15 -> 14, of which waited for: 7 -> 5; matrix products, arithmetic and copies ran while one was open for 6% -> 8% of each run, Pallas kernels for 12% -> 17%
where the time goes in v4:
time: 174 us; the launch traced here: 173 us
  waiting for transfers between devices  49.7 us (29%)
  Pallas kernels  41.1 us (24%)
  starting transfers between devices  33.8 us (19%)
  blocking collectives  28.2 us (16%)
  local copies, waits for them, and re-layouts  12.3 us (7%)
  other arithmetic  8.12 us (5%)
    ppermute x1, waiting for transfers between devices, per_device(): lax.ppermute(eigen_values[0].astype(bf16), 'dp', shifted(flip_z=1))  26.4 us
    pallas_call x1, Pallas kernels, per_device(): pl.pallas_call(functools.partial(first_kernel, length), grid_spec=pltpu.P...  22.3 us
    all_to_all x1, blocking collectives, per_device(): lax.all_to_all(spread, ('section', 'mp'), split_axis=0, concat_axis=0, ti...  15.8 us
    all_to_all x1, blocking collectives, per_device(): lax.all_to_all(partial, 'dp', split_axis=0, concat_axis=0, tiled=True, ax...  12.4 us
    pallas_call x1, Pallas kernels, per_device(): pl.pallas_call(last_kernel, grid_spec=pltpu.PrefetchScalarGridSpec(num_sc...  9.52 us
    ppermute x3, waiting for transfers between devices, per_device(): lax.ppermute(pair, 'dp', shifted(dx=s))  8.51 us
    ppermute x2, waiting for transfers between devices, per_device(): lax.ppermute(own_grads, 'mp', pairs)  7.18 us
    ppermute x1, waiting for transfers between devices, per_device(): other_acts = lax.ppermute(turned_acts, 'dp', shifted(dz=2))  7 us
  transfers between devices with their start and end apart: 14, of which 5 were waited for; matrix products, arithmetic and copies ran while one was open for 8% of the time, Pallas kernels for 17%

profile of v4, /device:TPU:1, one launch (start us, length us, event | category | flops | bytes accessed | tf_op | source)
XLA Modules:
  0.0 173.4 jit_solution(16840057332612702085)
XLA Ops:
  0.0 2.3 %turn_acts.1 = bf16[160,1024]{1,0:T(8,128)(2,1)} custom-call(bf16[128,1024]{1,0:T(8,128)(2,1)} %bitcast.72, bf16[32,1024]{1,0:T(8,128)(2,1)} %bitcast.75, bf16[1024,512]{1,0:T(8,128)(2,1)} %bitcast.63), custom_call_target="tpu_custom_call" | custom-call | tf_op jit(solution)/shard_map/turn_acts/pallas_call | solution.py:173
  2.3 3.8 %collective-permute-start = (bf16[160,1024]{1,0:T(8,128)(2,1)}, bf16[160,1024]{1,0:T(8,128)(2,1)S(1)}, u32[]{:S(2)}, u32[]{:S(2)}) collective-permute-start(bf16[160,1024]{1,0:T(8,128)(2,1)} %turn_acts.1), channel_id=1, source_target_pairs={{0,16},{4,20},{8,24},{12,28},{16,0},{20,4},{24,8},{28,12},{32,48},... | collective-permute-start | bytes 983048 | tf_op jit(solution)/shard_map/ppermute | solution.py:205
  6.2 7.0 %turn_grads.1 = bf16[16,288,128]{2,1,0:T(8,128)(2,1)} custom-call(bf16[128,3584]{1,0:T(8,128)(2,1)} %bitcast.67, bf16[32,3584]{1,0:T(8,128)(2,1)} %bitcast.73, bf16[3584,512]{1,0:T(8,128)(2,1)} %bitcast.55), custom_call_target="tpu_custom_call" | custom-call | tf_op jit(solution)/shard_map/turn_grads/pallas_call | solution.py:209
  13.1 7.0 %collective-permute-done = bf16[160,1024]{1,0:T(8,128)(2,1)S(1)} collective-permute-done((bf16[160,1024]{1,0:T(8,128)(2,1)}, bf16[160,1024]{1,0:T(8,128)(2,1)S(1)}, u32[]{:S(2)}, u32[]{:S(2)}) %collective-permute-start) | collective-permute-done | bytes 327712 | tf_op jit(solution)/shard_map/ppermute | solution.py:205
  20.1 6.2 %all-to-all-start = ((bf16[16,288,128]{2,1,0:T(8,128)(2,1)}), bf16[16,288,128]{2,1,0:T(8,128)(2,1)S(1)}, u32[]{:S(2)}, u32[]{:S(2)}) async-start(bf16[16,288,128]{2,1,0:T(8,128)(2,1)} %turn_grads.1), calls=%async_computation | async-start | bytes 2359296 | tf_op jit(solution)/shard_map/all_to_all | solution.py:228
  26.4 0.1 bitcast_convert_fusion
  26.5 3.4 %collective-permute-start.1 = (bf16[4,112,1024]{2,1,0:T(8,128)(2,1)S(1)}, bf16[4,112,1024]{2,1,0:T(8,128)(2,1)S(1)}, u32[]{:S(2)}, u32[]{:S(2)}) collective-permute-start(bf16[4,112,1024]{2,1,0:T(8,128)(2,1)S(1)} %bitcast_convert_fusion), channel_id=1, source_target_pairs={{0,8},{4,12},{8,0},{12,4},{16,24},{20,28},{24,16},{28,20},{32,40},... | collective-permute-start | bytes 2752520 | tf_op jit(solution)/shard_map/ppermute | solution.py:203
  29.9 0.0 copy-done.8
  29.9 1.1 pad_maximum_fusion.2
  31.0 1.4 collective-permute-start.2
  32.5 2.4 %collective-permute-start.3 = (bf16[2,160,1024]{2,1,0:T(8,128)(2,1)S(1)}, bf16[2,160,1024]{2,1,0:T(8,128)(2,1)S(1)}, u32[]{:S(2)}, u32[]{:S(2)}) collective-permute-start(bf16[2,160,1024]{2,1,0:T(8,128)(2,1)S(1)} %pad_maximum_fusion.2), channel_id=1, source_target_pairs={{0,64},{4,68},{8,72},{12,76},{16,80},{20,84},{24,88},{28,92},{32,9... | collective-permute-start | bytes 1966088 | tf_op jit(solution)/shard_map/ppermute | solution.py:231
  34.9 1.2 collective-permute-start.4
  36.0 26.4 %collective-permute-done.1.refs_3_ = bf16[4,112,1024]{2,1,0:T(8,128)(2,1)S(1)} collective-permute-done((bf16[4,112,1024]{2,1,0:T(8,128)(2,1)S(1)}, bf16[4,112,1024]{2,1,0:T(8,128)(2,1)S(1)}, u32[]{:S(2)}, u32[]{:S(2)}) %collective-permute-start.1) | collective-permute-done | bytes 917536 | tf_op jit(solution)/shard_map/ppermute | solution.py:203
  62.4 0.0 collective-permute-done.2
  62.4 8.5 %collective-permute-done.3 = bf16[2,160,1024]{2,1,0:T(8,128)(2,1)S(1)} collective-permute-done((bf16[2,160,1024]{2,1,0:T(8,128)(2,1)S(1)}, bf16[2,160,1024]{2,1,0:T(8,128)(2,1)S(1)}, u32[]{:S(2)}, u32[]{:S(2)}) %collective-permute-start.3) | collective-permute-done | bytes 655392 | tf_op jit(solution)/shard_map/ppermute | solution.py:231
  71.0 0.0 collective-permute-done.4
  71.0 0.0 all-to-all-done
  71.0 0.0 copy-start.1
  71.0 0.0 copy-done.4
  71.0 0.8 copy-done.5
  71.8 0.4 copy-done.1
  72.2 1.9 %pad_maximum_fusion.refs_7_.near_ref = bf16[4,2,160,1024]{3,2,1,0:T(8,128)(2,1)S(1)} fusion(bf16[1,2,160,1024]{3,2,1,0:T(8,128)(2,1)} %bitcast.35, bf16[1,2,160,1024]{3,2,1,0:T(8,128)(2,1)} %bitcast.69, bf16[1,2,160,1024]{3,2,1,0:T(8,128)(2,1)} %bitcast.68, bf16[1,2,160,1024]{3,2,1,0:T(8,128)(2,1)S(1)} %bitcast.56), kind=kLoop, calls=%fused_computation.2 | loop fusion | flops 3932160 | bytes 5242880 | tf_op jit(solution)/shard_map/stack | solution.py:235
  74.1 1.0 collective-permute-start.6
  75.1 0.6 gather_fusion
  75.7 0.1 select_bitcast_fusion
  75.8 0.1 copy.16
  75.9 3.4 %collective-permute-start.5 = (bf16[256,256]{1,0:T(8,128)(2,1)S(1)}, bf16[256,256]{1,0:T(8,128)(2,1)S(1)}, u32[]{:S(2)}, u32[]{:S(2)}) collective-permute-start(bf16[256,256]{1,0:T(8,128)(2,1)S(1)} %bitcast.74), channel_id=1, source_target_pairs={{0,8},{4,12},{8,0},{12,4},{16,24},{20,28},{24,16},{28,20},{32,40},... | collective-permute-start | bytes 393224 | tf_op jit(solution)/shard_map/ppermute | solution.py:247
  79.4 1.2 slice.21
  80.6 1.4 collective-permute-start.8
  82.0 1.5 collective-permute-start.9
  83.5 0.0 collective-permute-done.5
  83.5 0.7 fusion.4
  84.2 0.0 collective-permute-done.6.refs_8_.far_ref
  84.2 1.1 slice.29
  85.3 0.0 copy-done
  85.3 1.1 pad_maximum_fusion.1
  86.4 1.8 %gather_fusion.1 = bf16[8,32,1024]{2,1,0:T(8,128)(2,1)S(1)} fusion(bf16[16,32,1024]{2,1,0:T(8,128)(2,1)} %bitcast.57, s32[1024]{0:T(1024)S(1)} %pad_clamp_fusion), kind=kCustom, calls=%fused_computation.1 | custom fusion | bytes 1048608 | tf_op jit(solution)/shard_map/jit(_take)/gather | solution.py:276
  88.2 0.1 select_select_fusion
  88.4 1.7 %broadcast_in_dim.67 = bf16[4,256,256]{2,1,0:T(8,128)(2,1)} broadcast(bf16[256,256]{1,0:T(8,128)(2,1)} %fusion.4), dimensions={1,2} | broadcast | bytes 655360 | tf_op jit(solution)/shard_map/broadcast_in_dim | solution.py:256
  90.1 0.8 collective-permute-start.7
  90.9 4.3 %all-to-all-start.1 = ((bf16[4,256,256]{2,1,0:T(8,128)(2,1)}), bf16[4,256,256]{2,1,0:T(8,128)(2,1)S(1)}, u32[]{:S(2)}, u32[]{:S(2)}) async-start(bf16[4,256,256]{2,1,0:T(8,128)(2,1)} %broadcast_in_dim.67), calls=%async_computation.1 | async-start | bytes 1048576 | tf_op jit(solution)/shard_map/all_to_all | solution.py:257
  95.2 0.7 stack.115.place_ref
  95.9 0.7 pad_add_fusion.order_ref
  96.6 7.2 %collective-permute-done.8.refs_5_ = bf16[4,4,224,128]{3,2,1,0:T(8,128)(2,1)} collective-permute-done((bf16[4,4,224,128]{3,2,1,0:T(8,128)(2,1)S(1)}, bf16[4,4,224,128]{3,2,1,0:T(8,128)(2,1)}, u32[]{:S(2)}, u32[]{:S(2)}) %collective-permute-start.8) | collective-permute-done | bytes 917536 | tf_op jit(solution)/shard_map/ppermute | solution.py:251
  103.7 1.1 slice.30
  104.8 0.1 collective-permute-start.10
  104.9 0.0 collective-permute-done.9.refs_6_
  104.9 1.1 slice.31
  106.0 2.9 %collective-permute-start.11 = (bf16[4,4,112,128]{3,2,1,0:T(8,128)(2,1)S(1)}, bf16[4,4,112,128]{3,2,1,0:T(8,128)(2,1)S(1)}, u32[]{:S(2)}, u32[]{:S(2)}) collective-permute-start(bf16[4,4,112,128]{3,2,1,0:T(8,128)(2,1)S(1)} %slice.31), channel_id=1, source_target_pairs={{0,3},{1,0},{2,1},{3,2},{4,7},{5,4},{6,5},{7,6},{8,11},{9,8},{10,9... | collective-permute-start | bytes 1376264 | tf_op jit(solution)/shard_map/ppermute | solution.py:254
  108.9 0.0 collective-permute-done.7
  108.9 0.9 bitcast_add_fusion.refs_1_
  109.8 0.6 all-to-all-done.1.refs_0_
  110.4 0.8 copy-done.6
  111.2 22.3 %first_scores.1 = (f32[16,128]{1,0:T(8,128)}, bf16[14,128,1024]{2,1,0:T(8,128)(2,1)}) custom-call(s32[4]{0:T(128)} %pad_add_fusion.order_ref, s32[17]{0:T(128)} %stack.115.place_ref, bf16[4,256,256]{2,1,0:T(8,128)(2,1)} %copy-done.6, bf16[256,1024]{1,0:T(8,128)(2,1)} %bitcast_add_fusion.refs_1_, f32[4,112,1024]{2,1,0:T(8,128)} %bitcast.59, ...), custom_call_target="tpu_custom_call" | custom-call | flops 5637144576 | bytes 16777216 | tf_op jit(solution)/shard_map/first_scores/pallas_call | solution.py:294
  133.4 0.0 collective-permute-done.10.low_ref
  133.4 0.0 collective-permute-done.11.high_ref
  133.5 0.8 copy-done.7
  134.2 9.5 %last_scores.1 = f32[16,128]{1,0:T(8,128)} custom-call(s32[17]{0:T(128)} %stack.115.place_ref, bf16[4,4,112,128]{3,2,1,0:T(8,128)(2,1)} %collective-permute-done.10.low_ref, bf16[4,4,112,128]{3,2,1,0:T(8,128)(2,1)} %copy-done.7, bf16[4,2,160,1024]{3,2,1,0:T(8,128)(2,1)} %copy-done, bf16[4,2,160,1024]{3,2,1,0:T(8,128)(2,1)} %collective-permute-done.6.refs_8_.far_ref, ...), custom_call_target="tpu_custom_call" | custom-call | flops 1879048192 | bytes 9437184 | tf_op jit(solution)/shard_map/last_scores/pallas_call | solution.py:325
  143.8 0.7 add.333
  144.5 0.1 reshape.51
  144.5 0.1 reduce_sum.27
  144.6 12.4 %all_to_all.25 = f32[16,1,8]{2,1,0:T(1,128)S(1)} all-to-all(f32[16,1,8]{2,1,0:T(1,128)S(1)} %bitcast.76), channel_id=1, replica_groups={{0,4,16,20,32,36,48,52,64,68,80,84,96,100,112,116},{8,12,24,28,40,44,56..., dimensions={0} | all-to-all | bytes 1024 | tf_op jit(solution)/shard_map/all_to_all | solution.py:350
  157.1 15.8 %all_to_all.26 = f32[8,1,8]{2,1,0:T(1,128)S(1)} all-to-all(f32[8,1,8]{2,1,0:T(1,128)S(1)} %broadcast_in_dim.73), channel_id=1, replica_groups=mesh['section'=2,'dp'=32,'mp'=4] {'section','mp'}, dimensions={0} | all-to-all | bytes 512 | tf_op jit(solution)/shard_map/all_to_all | solution.py:355
  172.9 0.5 multiply_bitcast_fusion
  (27 shorter events, 0.2 us)
Async XLA Ops:
  2.3 17.8 %collective-permute-start = (bf16[160,1024]{1,0:T(8,128)(2,1)}, bf16[160,1024]{1,0:T(8,128)(2,1)S(1)}, u32[]{:S(2)}, u32[]{:S(2)}) collective-permute-start(bf16[160,1024]{1,0:T(8,128)(2,1)} %turn_acts.1), channel_id=1, source_target_pairs={{0,16},{4,20},{8,24},{12,28},{16,0},{20,4},{24,8},{28,12},{32,48},... | collective-permute-start | bytes 983048 | tf_op jit(solution)/shard_map/ppermute | solution.py:205
  13.1 13.2 %copy-start.2 = (f32[1,4,112,1024]{3,2,1,0:T(8,128)S(1)}, f32[1,4,112,1024]{3,2,1,0:T(8,128)}, u32[]{:S(2)}) copy-start(f32[1,4,112,1024]{3,2,1,0:T(8,128)} %param.12) | copy-start | bytes 5505028
  20.1 9.7 %copy-start.8 = (bf16[160,1024]{1,0:T(8,128)(2,1)}, bf16[160,1024]{1,0:T(8,128)(2,1)S(1)}, u32[]{:S(2)}) copy-start(bf16[160,1024]{1,0:T(8,128)(2,1)S(1)} %collective-permute-done) | copy-start | bytes 983044
  20.1 50.8 %all-to-all-start = ((bf16[16,288,128]{2,1,0:T(8,128)(2,1)}), bf16[16,288,128]{2,1,0:T(8,128)(2,1)S(1)}, u32[]{:S(2)}, u32[]{:S(2)}) async-start(bf16[16,288,128]{2,1,0:T(8,128)(2,1)} %turn_grads.1), calls=%async_computation | async-start | bytes 2359296 | tf_op jit(solution)/shard_map/all_to_all | solution.py:228
  26.5 35.9 %collective-permute-start.1 = (bf16[4,112,1024]{2,1,0:T(8,128)(2,1)S(1)}, bf16[4,112,1024]{2,1,0:T(8,128)(2,1)S(1)}, u32[]{:S(2)}, u32[]{:S(2)}) collective-permute-start(bf16[4,112,1024]{2,1,0:T(8,128)(2,1)S(1)} %bitcast_convert_fusion), channel_id=1, source_target_pairs={{0,8},{4,12},{8,0},{12,4},{16,24},{20,28},{24,16},{28,20},{32,40},... | collective-permute-start | bytes 2752520 | tf_op jit(solution)/shard_map/ppermute | solution.py:203
  31.0 31.4 %collective-permute-start.2 = (bf16[2,160,1024]{2,1,0:T(8,128)(2,1)S(1)}, bf16[2,160,1024]{2,1,0:T(8,128)(2,1)S(1)}, u32[]{:S(2)}, u32[]{:S(2)}) collective-permute-start(bf16[2,160,1024]{2,1,0:T(8,128)(2,1)S(1)} %pad_maximum_fusion.2), channel_id=1, source_target_pairs={{0,32},{4,36},{8,40},{12,44},{16,48},{20,52},{24,56},{28,60},{32,6... | collective-permute-start | bytes 1966088 | tf_op jit(solution)/shard_map/ppermute | solution.py:231
  32.5 38.5 %collective-permute-start.3 = (bf16[2,160,1024]{2,1,0:T(8,128)(2,1)S(1)}, bf16[2,160,1024]{2,1,0:T(8,128)(2,1)S(1)}, u32[]{:S(2)}, u32[]{:S(2)}) collective-permute-start(bf16[2,160,1024]{2,1,0:T(8,128)(2,1)S(1)} %pad_maximum_fusion.2), channel_id=1, source_target_pairs={{0,64},{4,68},{8,72},{12,76},{16,80},{20,84},{24,88},{28,92},{32,9... | collective-permute-start | bytes 1966088 | tf_op jit(solution)/shard_map/ppermute | solution.py:231
  34.9 36.1 %collective-permute-start.4 = (bf16[2,160,1024]{2,1,0:T(8,128)(2,1)S(1)}, bf16[2,160,1024]{2,1,0:T(8,128)(2,1)}, u32[]{:S(2)}, u32[]{:S(2)}) collective-permute-start(bf16[2,160,1024]{2,1,0:T(8,128)(2,1)S(1)} %pad_maximum_fusion.2), channel_id=1, source_target_pairs={{0,96},{4,100},{8,104},{12,108},{16,112},{20,116},{24,120},{28,124... | collective-permute-start | bytes 1966088 | tf_op jit(solution)/shard_map/ppermute | solution.py:231
  62.4 8.5 %copy-start.11 = (bf16[4,112,1024]{2,1,0:T(8,128)(2,1)}, bf16[4,112,1024]{2,1,0:T(8,128)(2,1)S(1)}, u32[]{:S(2)}) copy-start(bf16[4,112,1024]{2,1,0:T(8,128)(2,1)S(1)} %collective-permute-done.1.refs_3_) | copy-start | bytes 2752516
  62.4 8.5 %copy-start.4 = (bf16[2,160,1024]{2,1,0:T(8,128)(2,1)}, bf16[2,160,1024]{2,1,0:T(8,128)(2,1)S(1)}, u32[]{:S(2)}) copy-start(bf16[2,160,1024]{2,1,0:T(8,128)(2,1)S(1)} %collective-permute-done.2) | copy-start | bytes 1966084
  71.0 0.9 copy-start.5
  71.0 1.3 copy-start.1
  72.2 2.8 %copy-start.10 = (s32[8]{0:T(128)S(1)}, s32[8]{0:T(128)}, u32[]{:S(2)}) copy-start(s32[8]{0:T(128)} %param.15) | copy-start | bytes 100
  72.2 2.9 %slice-start = ((bf16[16,288,128]{2,1,0:T(8,128)(2,1)}), bf16[16,64,128]{2,1,0:T(8,128)(2,1)S(1)}, s32[]{:S(2)}) async-start(bf16[16,288,128]{2,1,0:T(8,128)(2,1)} %copy-done.1), calls=%async_computation.4 | async-start | bytes 524288 | tf_op jit(solution)/shard_map/slice | solution.py:243
  74.1 11.2 %copy-start = (bf16[4,2,160,1024]{3,2,1,0:T(8,128)(2,1)}, bf16[4,2,160,1024]{3,2,1,0:T(8,128)(2,1)S(1)}, u32[]{:S(2)}) copy-start(bf16[4,2,160,1024]{3,2,1,0:T(8,128)(2,1)S(1)} %pad_maximum_fusion.refs_7_.near_ref) | copy-start | bytes 7864324
  74.1 10.1 %collective-permute-start.6 = (bf16[4,2,160,1024]{3,2,1,0:T(8,128)(2,1)S(1)}, bf16[4,2,160,1024]{3,2,1,0:T(8,128)(2,1)}, u32[]{:S(2)}, u32[]{:S(2)}) collective-permute-start(bf16[4,2,160,1024]{3,2,1,0:T(8,128)(2,1)S(1)} %pad_maximum_fusion.refs_7_.near_ref), channel_id=1, source_target_pairs={{0,4},{4,0},{8,12},{12,8},{16,20},{20,16},{24,28},{28,24},{32,36},... | collective-permute-start | bytes 7864328 | tf_op jit(solution)/shard_map/ppermute | solution.py:262
  75.9 7.6 %collective-permute-start.5 = (bf16[256,256]{1,0:T(8,128)(2,1)S(1)}, bf16[256,256]{1,0:T(8,128)(2,1)S(1)}, u32[]{:S(2)}, u32[]{:S(2)}) collective-permute-start(bf16[256,256]{1,0:T(8,128)(2,1)S(1)} %bitcast.74), channel_id=1, source_target_pairs={{0,8},{4,12},{8,0},{12,4},{16,24},{20,28},{24,16},{28,20},{32,40},... | collective-permute-start | bytes 393224 | tf_op jit(solution)/shard_map/ppermute | solution.py:247
  80.6 7.7 %copy-start.3 = (bf16[16,224,128]{2,1,0:T(8,128)(2,1)}, bf16[16,224,128]{2,1,0:T(8,128)(2,1)S(1)}, u32[]{:S(2)}) copy-start(bf16[16,224,128]{2,1,0:T(8,128)(2,1)S(1)} %slice.21) | copy-start | bytes 2752516
  80.6 23.1 %collective-permute-start.8 = (bf16[4,4,224,128]{3,2,1,0:T(8,128)(2,1)S(1)}, bf16[4,4,224,128]{3,2,1,0:T(8,128)(2,1)}, u32[]{:S(2)}, u32[]{:S(2)}) collective-permute-start(bf16[4,4,224,128]{3,2,1,0:T(8,128)(2,1)S(1)} %bitcast.64), channel_id=1, source_target_pairs={{0,1},{1,2},{2,3},{3,0},{4,5},{5,6},{6,7},{7,4},{8,9},{9,10},{10,1... | collective-permute-start | bytes 2752520 | tf_op jit(solution)/shard_map/ppermute | solution.py:251
  82.0 22.9 %collective-permute-start.9 = (bf16[4,4,224,128]{3,2,1,0:T(8,128)(2,1)S(1)}, bf16[4,4,224,128]{3,2,1,0:T(8,128)(2,1)}, u32[]{:S(2)}, u32[]{:S(2)}) collective-permute-start(bf16[4,4,224,128]{3,2,1,0:T(8,128)(2,1)S(1)} %bitcast.65), channel_id=1, source_target_pairs={{0,3},{1,0},{2,1},{3,2},{4,7},{5,4},{6,5},{7,6},{8,11},{9,8},{10,9... | collective-permute-start | bytes 2752520 | tf_op jit(solution)/shard_map/ppermute | solution.py:251
  90.1 18.7 %collective-permute-start.7 = (bf16[256,1024]{1,0:T(8,128)(2,1)S(1)}, bf16[256,1024]{1,0:T(8,128)(2,1)S(1)}, u32[]{:S(2)}, u32[]{:S(2)}) collective-permute-start(bf16[256,1024]{1,0:T(8,128)(2,1)S(1)} %bitcast.58), channel_id=1, source_target_pairs={{0,8},{4,12},{8,0},{12,4},{16,24},{20,28},{24,16},{28,20},{32,40},... | collective-permute-start | bytes 1572872 | tf_op jit(solution)/shard_map/ppermute | solution.py:279
  90.9 19.5 %all-to-all-start.1 = ((bf16[4,256,256]{2,1,0:T(8,128)(2,1)}), bf16[4,256,256]{2,1,0:T(8,128)(2,1)S(1)}, u32[]{:S(2)}, u32[]{:S(2)}) async-start(bf16[4,256,256]{2,1,0:T(8,128)(2,1)} %broadcast_in_dim.67), calls=%async_computation.1 | async-start | bytes 1048576 | tf_op jit(solution)/shard_map/all_to_all | solution.py:257
  104.8 28.6 %collective-permute-start.10 = (bf16[4,4,112,128]{3,2,1,0:T(8,128)(2,1)S(1)}, bf16[4,4,112,128]{3,2,1,0:T(8,128)(2,1)}, u32[]{:S(2)}, u32[]{:S(2)}) collective-permute-start(bf16[4,4,112,128]{3,2,1,0:T(8,128)(2,1)S(1)} %slice.30), channel_id=1, source_target_pairs={{0,1},{1,2},{2,3},{3,0},{4,5},{5,6},{6,7},{7,4},{8,9},{9,10},{10,1... | collective-permute-start | bytes 1376264 | tf_op jit(solution)/shard_map/ppermute | solution.py:253
  106.0 27.5 %collective-permute-start.11 = (bf16[4,4,112,128]{3,2,1,0:T(8,128)(2,1)S(1)}, bf16[4,4,112,128]{3,2,1,0:T(8,128)(2,1)S(1)}, u32[]{:S(2)}, u32[]{:S(2)}) collective-permute-start(bf16[4,4,112,128]{3,2,1,0:T(8,128)(2,1)S(1)} %slice.31), channel_id=1, source_target_pairs={{0,3},{1,0},{2,1},{3,2},{4,7},{5,4},{6,5},{7,6},{8,11},{9,8},{10,9... | collective-permute-start | bytes 1376264 | tf_op jit(solution)/shard_map/ppermute | solution.py:254
  110.4 0.8 copy-start.6
  133.4 0.8 copy-start.7
  134.2 9.5 %copy-start.9 = (f32[16,128]{1,0:T(8,128)S(1)}, f32[16,128]{1,0:T(8,128)}, u32[]{:S(2)}) copy-start(f32[16,128]{1,0:T(8,128)} %get-tuple-element.27) | copy-start | bytes 24580

commit v5 on v4

--- a/solution.py
+++ b/solution.py
@@ -347,17 +347,21 @@
     scores = early_scores + last_scores
     partial = scores.reshape(targets, queries, ROWS).sum(axis=2)
 
-    mine = lax.all_to_all(
-        partial, "dp", split_axis=0, concat_axis=0, tiled=True, axis_index_groups=classes
-    ).sum(axis=0)
-    others = model_size * lax.axis_size("section")
-    spread = jnp.broadcast_to(mine[None], (others, queries))
-    gathered = lax.all_to_all(spread, ("section", "mp"), split_axis=0, concat_axis=0, tiled=True)
+    rows = partial.reshape(width, DEPTH // 2, 1, CORES, queries)
+    parities = jnp.arange(2).reshape(1, 1, 2, 1, 1)
+    rows = jnp.where(parities == my_class, rows, 0.0).reshape(data_size, 1, queries)
+    rows = jnp.broadcast_to(rows, (data_size, model_size, queries))
+    rows = rows.reshape(data_size * model_size, queries)
+    rows = lax.all_to_all(rows, ("dp", "mp"), split_axis=0, concat_axis=0, tiled=True)
+    mine = rows.sum(axis=0, keepdims=True)
+    sections = lax.axis_size("section")
+    swapped = [(i, (i + 1) % sections) for i in range(sections)]
+    mine = mine + lax.ppermute(mine, "section", swapped)
     layers = train_acts.shape[0] * lax.axis_size("section")
     normalizer = math.sqrt(
         layers * act_cols * model_size * grad_cols * model_size * SEQLEN * length
     )
-    return gathered.sum(axis=0, keepdims=True) / normalizer
+    return mine / normalizer
 
 
 def solution(mesh):

time: 174 us -> 171 us (0.983)
  blocking collectives: 28.2 us -> 18.6 us
  starting transfers between devices: 33.8 us -> 38.5 us
    all_to_all x2 -> x1, blocking collectives: 28.2 us -> 18.6 us  [per_device(): lax.all_to_all(rows, ('dp', 'mp'), split_axis=0, concat_axis=0, tiled=True)]
    ppermute x0 -> x1, starting transfers between devices: none -> 4.75 us  [per_device(): mine = mine + lax.ppermute(mine, 'section', swapped)]
  transfers between devices with their start and end apart: 14 -> 15, of which waited for: 5 -> 6; matrix products, arithmetic and copies ran while one was open for 8% -> 8% of each run, Pallas kernels for 17% -> 17%
where the time goes in v5:
time: 171 us; the launch traced here: 170 us
  waiting for transfers between devices  51.2 us (30%)
  Pallas kernels  41.1 us (24%)
  starting transfers between devices  38.5 us (23%)
  blocking collectives  18.6 us (11%)
  local copies, waits for them, and re-layouts  12.5 us (7%)
  other arithmetic  8.25 us (5%)
    ppermute x1, waiting for transfers between devices, per_device(): lax.ppermute(eigen_values[0].astype(bf16), 'dp', shifted(flip_z=1))  26.4 us
    pallas_call x1, Pallas kernels, per_device(): pl.pallas_call(functools.partial(first_kernel, length), grid_spec=pltpu.P...  22.3 us
    all_to_all x1, blocking collectives, per_device(): lax.all_to_all(rows, ('dp', 'mp'), split_axis=0, concat_axis=0, tiled=True)  18.6 us
    pallas_call x1, Pallas kernels, per_device(): pl.pallas_call(last_kernel, grid_spec=pltpu.PrefetchScalarGridSpec(num_sc...  9.54 us
    ppermute x3, waiting for transfers between devices, per_device(): lax.ppermute(pair, 'dp', shifted(dx=s))  8.51 us
    ppermute x2, waiting for transfers between devices, per_device(): lax.ppermute(own_grads, 'mp', pairs)  7.05 us
    pallas_call x1, Pallas kernels, per_device(): pl.pallas_call(turn_grads_kernel, grid=(steps,), in_specs=[pl.BlockSpec((...  7 us
    ppermute x1, waiting for transfers between devices, per_device(): other_acts = lax.ppermute(turned_acts, 'dp', shifted(dz=2))  6.98 us
  transfers between devices with their start and end apart: 15, of which 6 were waited for; matrix products, arithmetic and copies ran while one was open for 8% of the time, Pallas kernels for 17%

profile of v5, /device:TPU:1, one launch (start us, length us, event | category | flops | bytes accessed | tf_op | source)
XLA Modules:
  0.0 170.4 jit_solution(9764050018780002761)
XLA Ops:
  0.0 2.3 %turn_acts.1 = bf16[160,1024]{1,0:T(8,128)(2,1)} custom-call(bf16[128,1024]{1,0:T(8,128)(2,1)} %bitcast.72, bf16[32,1024]{1,0:T(8,128)(2,1)} %bitcast.76, bf16[1024,512]{1,0:T(8,128)(2,1)} %bitcast.62), custom_call_target="tpu_custom_call" | custom-call | tf_op jit(solution)/shard_map/turn_acts/pallas_call | solution.py:173
  2.3 3.8 %collective-permute-start = (bf16[160,1024]{1,0:T(8,128)(2,1)}, bf16[160,1024]{1,0:T(8,128)(2,1)S(1)}, u32[]{:S(2)}, u32[]{:S(2)}) collective-permute-start(bf16[160,1024]{1,0:T(8,128)(2,1)} %turn_acts.1), channel_id=1, source_target_pairs={{0,16},{4,20},{8,24},{12,28},{16,0},{20,4},{24,8},{28,12},{32,48},... | collective-permute-start | bytes 983048 | tf_op jit(solution)/shard_map/ppermute | solution.py:205
  6.2 7.0 %turn_grads.1 = bf16[16,288,128]{2,1,0:T(8,128)(2,1)} custom-call(bf16[128,3584]{1,0:T(8,128)(2,1)} %bitcast.66, bf16[32,3584]{1,0:T(8,128)(2,1)} %bitcast.73, bf16[3584,512]{1,0:T(8,128)(2,1)} %bitcast.54), custom_call_target="tpu_custom_call" | custom-call | tf_op jit(solution)/shard_map/turn_grads/pallas_call | solution.py:209
  13.2 7.0 %collective-permute-done = bf16[160,1024]{1,0:T(8,128)(2,1)S(1)} collective-permute-done((bf16[160,1024]{1,0:T(8,128)(2,1)}, bf16[160,1024]{1,0:T(8,128)(2,1)S(1)}, u32[]{:S(2)}, u32[]{:S(2)}) %collective-permute-start) | collective-permute-done | bytes 327712 | tf_op jit(solution)/shard_map/ppermute | solution.py:205
  20.1 6.2 %all-to-all-start = ((bf16[16,288,128]{2,1,0:T(8,128)(2,1)}), bf16[16,288,128]{2,1,0:T(8,128)(2,1)S(1)}, u32[]{:S(2)}, u32[]{:S(2)}) async-start(bf16[16,288,128]{2,1,0:T(8,128)(2,1)} %turn_grads.1), calls=%async_computation | async-start | bytes 2359296 | tf_op jit(solution)/shard_map/all_to_all | solution.py:228
  26.4 0.1 bitcast_convert_fusion
  26.5 3.4 %collective-permute-start.1 = (bf16[4,112,1024]{2,1,0:T(8,128)(2,1)S(1)}, bf16[4,112,1024]{2,1,0:T(8,128)(2,1)S(1)}, u32[]{:S(2)}, u32[]{:S(2)}) collective-permute-start(bf16[4,112,1024]{2,1,0:T(8,128)(2,1)S(1)} %bitcast_convert_fusion), channel_id=1, source_target_pairs={{0,8},{4,12},{8,0},{12,4},{16,24},{20,28},{24,16},{28,20},{32,40},... | collective-permute-start | bytes 2752520 | tf_op jit(solution)/shard_map/ppermute | solution.py:203
  29.9 1.1 pad_maximum_fusion.2
  31.0 1.4 collective-permute-start.2
  32.5 2.4 %collective-permute-start.3 = (bf16[2,160,1024]{2,1,0:T(8,128)(2,1)S(1)}, bf16[2,160,1024]{2,1,0:T(8,128)(2,1)S(1)}, u32[]{:S(2)}, u32[]{:S(2)}) collective-permute-start(bf16[2,160,1024]{2,1,0:T(8,128)(2,1)S(1)} %pad_maximum_fusion.2), channel_id=1, source_target_pairs={{0,64},{4,68},{8,72},{12,76},{16,80},{20,84},{24,88},{28,92},{32,9... | collective-permute-start | bytes 1966088 | tf_op jit(solution)/shard_map/ppermute | solution.py:231
  34.9 1.2 collective-permute-start.4
  36.0 26.4 %collective-permute-done.1.refs_3_ = bf16[4,112,1024]{2,1,0:T(8,128)(2,1)S(1)} collective-permute-done((bf16[4,112,1024]{2,1,0:T(8,128)(2,1)S(1)}, bf16[4,112,1024]{2,1,0:T(8,128)(2,1)S(1)}, u32[]{:S(2)}, u32[]{:S(2)}) %collective-permute-start.1) | collective-permute-done | bytes 917536 | tf_op jit(solution)/shard_map/ppermute | solution.py:203
  62.4 0.0 collective-permute-done.2
  62.4 8.5 %collective-permute-done.3 = bf16[2,160,1024]{2,1,0:T(8,128)(2,1)S(1)} collective-permute-done((bf16[2,160,1024]{2,1,0:T(8,128)(2,1)S(1)}, bf16[2,160,1024]{2,1,0:T(8,128)(2,1)S(1)}, u32[]{:S(2)}, u32[]{:S(2)}) %collective-permute-start.3) | collective-permute-done | bytes 655392 | tf_op jit(solution)/shard_map/ppermute | solution.py:231
  71.0 0.0 collective-permute-done.4
  71.0 0.0 all-to-all-done
  71.0 0.8 copy-done.5
  71.8 0.4 copy-done.1
  72.2 1.9 %pad_maximum_fusion.refs_7_.near_ref = bf16[4,2,160,1024]{3,2,1,0:T(8,128)(2,1)S(1)} fusion(bf16[1,2,160,1024]{3,2,1,0:T(8,128)(2,1)} %bitcast.35, bf16[1,2,160,1024]{3,2,1,0:T(8,128)(2,1)} %bitcast.68, bf16[1,2,160,1024]{3,2,1,0:T(8,128)(2,1)} %bitcast.67, bf16[1,2,160,1024]{3,2,1,0:T(8,128)(2,1)S(1)} %bitcast.55), kind=kLoop, calls=%fused_computation.2 | loop fusion | flops 3932160 | bytes 5242880 | tf_op jit(solution)/shard_map/stack | solution.py:235
  74.1 1.0 collective-permute-start.6
  75.1 0.6 gather_fusion
  75.7 0.1 select_bitcast_fusion
  75.8 0.1 copy.11
  76.0 3.4 %collective-permute-start.5 = (bf16[256,256]{1,0:T(8,128)(2,1)S(1)}, bf16[256,256]{1,0:T(8,128)(2,1)S(1)}, u32[]{:S(2)}, u32[]{:S(2)}) collective-permute-start(bf16[256,256]{1,0:T(8,128)(2,1)S(1)} %bitcast.74), channel_id=1, source_target_pairs={{0,8},{4,12},{8,0},{12,4},{16,24},{20,28},{24,16},{28,20},{32,40},... | collective-permute-start | bytes 393224 | tf_op jit(solution)/shard_map/ppermute | solution.py:247
  79.4 1.2 slice.21
  80.6 1.4 collective-permute-start.8
  82.0 1.5 collective-permute-start.9
  83.5 0.0 collective-permute-done.5
  83.6 0.7 fusion.4
  84.2 0.0 collective-permute-done.6.refs_8_.far_ref
  84.2 1.1 slice.29
  85.3 1.1 pad_maximum_fusion.1
  86.4 1.8 %gather_fusion.1 = bf16[8,32,1024]{2,1,0:T(8,128)(2,1)S(1)} fusion(bf16[16,32,1024]{2,1,0:T(8,128)(2,1)} %bitcast.56, s32[1024]{0:T(1024)S(1)} %pad_clamp_fusion), kind=kCustom, calls=%fused_computation.1 | custom fusion | bytes 1048608 | tf_op jit(solution)/shard_map/jit(_take)/gather | solution.py:276
  88.2 0.1 select_select_fusion
  88.4 1.7 %broadcast_in_dim.99 = bf16[4,256,256]{2,1,0:T(8,128)(2,1)} broadcast(bf16[256,256]{1,0:T(8,128)(2,1)} %fusion.4), dimensions={1,2} | broadcast | bytes 655360 | tf_op jit(solution)/shard_map/broadcast_in_dim | solution.py:256
  90.1 0.8 collective-permute-start.7
  91.0 4.3 %all-to-all-start.1 = ((bf16[4,256,256]{2,1,0:T(8,128)(2,1)}), bf16[4,256,256]{2,1,0:T(8,128)(2,1)S(1)}, u32[]{:S(2)}, u32[]{:S(2)}) async-start(bf16[4,256,256]{2,1,0:T(8,128)(2,1)} %broadcast_in_dim.99), calls=%async_computation.1 | async-start | bytes 1048576 | tf_op jit(solution)/shard_map/all_to_all | solution.py:257
  95.2 0.1 broadcast_in_dim.91
  95.3 0.1 broadcast_in_dim.92
  95.5 0.6 stack.115.place_ref
  96.1 0.6 pad_add_fusion.order_ref
  96.7 7.0 %collective-permute-done.8.refs_5_ = bf16[4,4,224,128]{3,2,1,0:T(8,128)(2,1)} collective-permute-done((bf16[4,4,224,128]{3,2,1,0:T(8,128)(2,1)S(1)}, bf16[4,4,224,128]{3,2,1,0:T(8,128)(2,1)}, u32[]{:S(2)}, u32[]{:S(2)}) %collective-permute-start.8) | collective-permute-done | bytes 917536 | tf_op jit(solution)/shard_map/ppermute | solution.py:251
  103.8 1.1 slice.30
  104.8 0.1 collective-permute-start.10
  104.9 0.0 collective-permute-done.9.refs_6_
  104.9 1.1 slice.31
  106.0 2.9 %collective-permute-start.11 = (bf16[4,4,112,128]{3,2,1,0:T(8,128)(2,1)S(1)}, bf16[4,4,112,128]{3,2,1,0:T(8,128)(2,1)S(1)}, u32[]{:S(2)}, u32[]{:S(2)}) collective-permute-start(bf16[4,4,112,128]{3,2,1,0:T(8,128)(2,1)S(1)} %slice.31), channel_id=1, source_target_pairs={{0,3},{1,0},{2,1},{3,2},{4,7},{5,4},{6,5},{7,6},{8,11},{9,8},{10,9... | collective-permute-start | bytes 1376264 | tf_op jit(solution)/shard_map/ppermute | solution.py:254
  108.9 0.0 collective-permute-done.7
  108.9 0.9 bitcast_add_fusion.refs_1_
  109.8 0.6 all-to-all-done.1.refs_0_
  110.4 0.8 copy-done.6
  111.2 22.3 %first_scores.1 = (f32[16,128]{1,0:T(8,128)}, bf16[14,128,1024]{2,1,0:T(8,128)(2,1)}) custom-call(s32[4]{0:T(128)} %pad_add_fusion.order_ref, s32[17]{0:T(128)} %stack.115.place_ref, bf16[4,256,256]{2,1,0:T(8,128)(2,1)} %copy-done.6, bf16[256,1024]{1,0:T(8,128)(2,1)} %bitcast_add_fusion.refs_1_, f32[4,112,1024]{2,1,0:T(8,128)} %bitcast.58, ...), custom_call_target="tpu_custom_call" | custom-call | flops 5637144576 | bytes 16777216 | tf_op jit(solution)/shard_map/first_scores/pallas_call | solution.py:294
  133.5 0.0 collective-permute-done.10.low_ref
  133.5 0.8 copy-done.7
  134.3 9.5 %last_scores.1 = f32[16,128]{1,0:T(8,128)} custom-call(s32[17]{0:T(128)} %stack.115.place_ref, bf16[4,4,112,128]{3,2,1,0:T(8,128)(2,1)} %collective-permute-done.10.low_ref, bf16[4,4,112,128]{3,2,1,0:T(8,128)(2,1)} %copy-done.7, bf16[4,2,160,1024]{3,2,1,0:T(8,128)(2,1)} %copy-done, bf16[4,2,160,1024]{3,2,1,0:T(8,128)(2,1)} %collective-permute-done.6.refs_8_.far_ref, ...), custom_call_target="tpu_custom_call" | custom-call | flops 1879048192 | bytes 9437184 | tf_op jit(solution)/shard_map/last_scores/pallas_call | solution.py:325
  143.8 0.7 add.336
  144.5 0.1 reshape.60
  144.6 0.1 reduce_sum.18
  144.7 0.1 broadcast_select_fusion
  144.8 18.6 %all_to_all.19 = f32[128,1,8]{2,1,0:T(1,128)S(1)} all-to-all(f32[128,1,8]{2,1,0:T(1,128)S(1)} %bitcast.71), channel_id=1, replica_groups=mesh['section'=2,'dp'=32,'mp'=4] {'dp','mp'}, dimensions={0} | all-to-all | bytes 8192 | tf_op jit(solution)/shard_map/all_to_all | solution.py:355
  163.4 0.2 reduce_sum.19
  163.6 4.8 %collective-permute-start.12 = (f32[1,8]{1,0:T(1,128)S(1)}, f32[1,8]{1,0:T(1,128)S(1)}, u32[]{:S(2)}, u32[]{:S(2)}) collective-permute-start(f32[1,8]{1,0:T(1,128)S(1)} %bitcast.78), channel_id=1, source_target_pairs={{0,128},{128,0},{1,129},{129,1},{2,130},{130,2},{3,131},{131,3},{4... | collective-permute-start | bytes 104 | tf_op jit(solution)/shard_map/ppermute | solution.py:359
  168.3 1.6 collective-permute-done.12
  169.9 0.5 add_multiply_fusion
  (32 shorter events, 0.2 us)
Async XLA Ops:
  2.3 17.8 %collective-permute-start = (bf16[160,1024]{1,0:T(8,128)(2,1)}, bf16[160,1024]{1,0:T(8,128)(2,1)S(1)}, u32[]{:S(2)}, u32[]{:S(2)}) collective-permute-start(bf16[160,1024]{1,0:T(8,128)(2,1)} %turn_acts.1), channel_id=1, source_target_pairs={{0,16},{4,20},{8,24},{12,28},{16,0},{20,4},{24,8},{28,12},{32,48},... | collective-permute-start | bytes 983048 | tf_op jit(solution)/shard_map/ppermute | solution.py:205
  13.2 13.2 %copy-start.2 = (f32[1,4,112,1024]{3,2,1,0:T(8,128)S(1)}, f32[1,4,112,1024]{3,2,1,0:T(8,128)}, u32[]{:S(2)}) copy-start(f32[1,4,112,1024]{3,2,1,0:T(8,128)} %param.12) | copy-start | bytes 5505028
  20.1 9.7 %copy-start.8 = (bf16[160,1024]{1,0:T(8,128)(2,1)}, bf16[160,1024]{1,0:T(8,128)(2,1)S(1)}, u32[]{:S(2)}) copy-start(bf16[160,1024]{1,0:T(8,128)(2,1)S(1)} %collective-permute-done) | copy-start | bytes 983044
  20.1 50.8 %all-to-all-start = ((bf16[16,288,128]{2,1,0:T(8,128)(2,1)}), bf16[16,288,128]{2,1,0:T(8,128)(2,1)S(1)}, u32[]{:S(2)}, u32[]{:S(2)}) async-start(bf16[16,288,128]{2,1,0:T(8,128)(2,1)} %turn_grads.1), calls=%async_computation | async-start | bytes 2359296 | tf_op jit(solution)/shard_map/all_to_all | solution.py:228
  26.5 35.9 %collective-permute-start.1 = (bf16[4,112,1024]{2,1,0:T(8,128)(2,1)S(1)}, bf16[4,112,1024]{2,1,0:T(8,128)(2,1)S(1)}, u32[]{:S(2)}, u32[]{:S(2)}) collective-permute-start(bf16[4,112,1024]{2,1,0:T(8,128)(2,1)S(1)} %bitcast_convert_fusion), channel_id=1, source_target_pairs={{0,8},{4,12},{8,0},{12,4},{16,24},{20,28},{24,16},{28,20},{32,40},... | collective-permute-start | bytes 2752520 | tf_op jit(solution)/shard_map/ppermute | solution.py:203
  31.0 31.4 %collective-permute-start.2 = (bf16[2,160,1024]{2,1,0:T(8,128)(2,1)S(1)}, bf16[2,160,1024]{2,1,0:T(8,128)(2,1)S(1)}, u32[]{:S(2)}, u32[]{:S(2)}) collective-permute-start(bf16[2,160,1024]{2,1,0:T(8,128)(2,1)S(1)} %pad_maximum_fusion.2), channel_id=1, source_target_pairs={{0,32},{4,36},{8,40},{12,44},{16,48},{20,52},{24,56},{28,60},{32,6... | collective-permute-start | bytes 1966088 | tf_op jit(solution)/shard_map/ppermute | solution.py:231
  32.5 38.5 %collective-permute-start.3 = (bf16[2,160,1024]{2,1,0:T(8,128)(2,1)S(1)}, bf16[2,160,1024]{2,1,0:T(8,128)(2,1)S(1)}, u32[]{:S(2)}, u32[]{:S(2)}) collective-permute-start(bf16[2,160,1024]{2,1,0:T(8,128)(2,1)S(1)} %pad_maximum_fusion.2), channel_id=1, source_target_pairs={{0,64},{4,68},{8,72},{12,76},{16,80},{20,84},{24,88},{28,92},{32,9... | collective-permute-start | bytes 1966088 | tf_op jit(solution)/shard_map/ppermute | solution.py:231
  34.9 36.1 %collective-permute-start.4 = (bf16[2,160,1024]{2,1,0:T(8,128)(2,1)S(1)}, bf16[2,160,1024]{2,1,0:T(8,128)(2,1)}, u32[]{:S(2)}, u32[]{:S(2)}) collective-permute-start(bf16[2,160,1024]{2,1,0:T(8,128)(2,1)S(1)} %pad_maximum_fusion.2), channel_id=1, source_target_pairs={{0,96},{4,100},{8,104},{12,108},{16,112},{20,116},{24,120},{28,124... | collective-permute-start | bytes 1966088 | tf_op jit(solution)/shard_map/ppermute | solution.py:231
  62.4 8.5 %copy-start.11 = (bf16[4,112,1024]{2,1,0:T(8,128)(2,1)}, bf16[4,112,1024]{2,1,0:T(8,128)(2,1)S(1)}, u32[]{:S(2)}) copy-start(bf16[4,112,1024]{2,1,0:T(8,128)(2,1)S(1)} %collective-permute-done.1.refs_3_) | copy-start | bytes 2752516
  62.4 8.5 %copy-start.4 = (bf16[2,160,1024]{2,1,0:T(8,128)(2,1)}, bf16[2,160,1024]{2,1,0:T(8,128)(2,1)S(1)}, u32[]{:S(2)}) copy-start(bf16[2,160,1024]{2,1,0:T(8,128)(2,1)S(1)} %collective-permute-done.2) | copy-start | bytes 1966084
  71.0 0.8 copy-start.5
  71.0 1.3 copy-start.1
  72.2 2.8 %copy-start.10 = (s32[8]{0:T(128)S(1)}, s32[8]{0:T(128)}, u32[]{:S(2)}) copy-start(s32[8]{0:T(128)} %param.15) | copy-start | bytes 100
  72.2 2.9 %slice-start = ((bf16[16,288,128]{2,1,0:T(8,128)(2,1)}), bf16[16,64,128]{2,1,0:T(8,128)(2,1)S(1)}, s32[]{:S(2)}) async-start(bf16[16,288,128]{2,1,0:T(8,128)(2,1)} %copy-done.1), calls=%async_computation.3 | async-start | bytes 524288 | tf_op jit(solution)/shard_map/slice | solution.py:243
  74.1 11.2 %copy-start = (bf16[4,2,160,1024]{3,2,1,0:T(8,128)(2,1)}, bf16[4,2,160,1024]{3,2,1,0:T(8,128)(2,1)S(1)}, u32[]{:S(2)}) copy-start(bf16[4,2,160,1024]{3,2,1,0:T(8,128)(2,1)S(1)} %pad_maximum_fusion.refs_7_.near_ref) | copy-start | bytes 7864324
  74.1 10.1 %collective-permute-start.6 = (bf16[4,2,160,1024]{3,2,1,0:T(8,128)(2,1)S(1)}, bf16[4,2,160,1024]{3,2,1,0:T(8,128)(2,1)}, u32[]{:S(2)}, u32[]{:S(2)}) collective-permute-start(bf16[4,2,160,1024]{3,2,1,0:T(8,128)(2,1)S(1)} %pad_maximum_fusion.refs_7_.near_ref), channel_id=1, source_target_pairs={{0,4},{4,0},{8,12},{12,8},{16,20},{20,16},{24,28},{28,24},{32,36},... | collective-permute-start | bytes 7864328 | tf_op jit(solution)/shard_map/ppermute | solution.py:262
  76.0 7.6 %collective-permute-start.5 = (bf16[256,256]{1,0:T(8,128)(2,1)S(1)}, bf16[256,256]{1,0:T(8,128)(2,1)S(1)}, u32[]{:S(2)}, u32[]{:S(2)}) collective-permute-start(bf16[256,256]{1,0:T(8,128)(2,1)S(1)} %bitcast.74), channel_id=1, source_target_pairs={{0,8},{4,12},{8,0},{12,4},{16,24},{20,28},{24,16},{28,20},{32,40},... | collective-permute-start | bytes 393224 | tf_op jit(solution)/shard_map/ppermute | solution.py:247
  80.6 7.7 %copy-start.3 = (bf16[16,224,128]{2,1,0:T(8,128)(2,1)}, bf16[16,224,128]{2,1,0:T(8,128)(2,1)S(1)}, u32[]{:S(2)}) copy-start(bf16[16,224,128]{2,1,0:T(8,128)(2,1)S(1)} %slice.21) | copy-start | bytes 2752516
  80.6 23.1 %collective-permute-start.8 = (bf16[4,4,224,128]{3,2,1,0:T(8,128)(2,1)S(1)}, bf16[4,4,224,128]{3,2,1,0:T(8,128)(2,1)}, u32[]{:S(2)}, u32[]{:S(2)}) collective-permute-start(bf16[4,4,224,128]{3,2,1,0:T(8,128)(2,1)S(1)} %bitcast.63), channel_id=1, source_target_pairs={{0,1},{1,2},{2,3},{3,0},{4,5},{5,6},{6,7},{7,4},{8,9},{9,10},{10,1... | collective-permute-start | bytes 2752520 | tf_op jit(solution)/shard_map/ppermute | solution.py:251
  82.0 22.9 %collective-permute-start.9 = (bf16[4,4,224,128]{3,2,1,0:T(8,128)(2,1)S(1)}, bf16[4,4,224,128]{3,2,1,0:T(8,128)(2,1)}, u32[]{:S(2)}, u32[]{:S(2)}) collective-permute-start(bf16[4,4,224,128]{3,2,1,0:T(8,128)(2,1)S(1)} %bitcast.64), channel_id=1, source_target_pairs={{0,3},{1,0},{2,1},{3,2},{4,7},{5,4},{6,5},{7,6},{8,11},{9,8},{10,9... | collective-permute-start | bytes 2752520 | tf_op jit(solution)/shard_map/ppermute | solution.py:251
  90.1 18.7 %collective-permute-start.7 = (bf16[256,1024]{1,0:T(8,128)(2,1)S(1)}, bf16[256,1024]{1,0:T(8,128)(2,1)S(1)}, u32[]{:S(2)}, u32[]{:S(2)}) collective-permute-start(bf16[256,1024]{1,0:T(8,128)(2,1)S(1)} %bitcast.57), channel_id=1, source_target_pairs={{0,8},{4,12},{8,0},{12,4},{16,24},{20,28},{24,16},{28,20},{32,40},... | collective-permute-start | bytes 1572872 | tf_op jit(solution)/shard_map/ppermute | solution.py:279
  91.0 19.5 %all-to-all-start.1 = ((bf16[4,256,256]{2,1,0:T(8,128)(2,1)}), bf16[4,256,256]{2,1,0:T(8,128)(2,1)S(1)}, u32[]{:S(2)}, u32[]{:S(2)}) async-start(bf16[4,256,256]{2,1,0:T(8,128)(2,1)} %broadcast_in_dim.99), calls=%async_computation.1 | async-start | bytes 1048576 | tf_op jit(solution)/shard_map/all_to_all | solution.py:257
  104.8 28.7 %collective-permute-start.10 = (bf16[4,4,112,128]{3,2,1,0:T(8,128)(2,1)S(1)}, bf16[4,4,112,128]{3,2,1,0:T(8,128)(2,1)}, u32[]{:S(2)}, u32[]{:S(2)}) collective-permute-start(bf16[4,4,112,128]{3,2,1,0:T(8,128)(2,1)S(1)} %slice.30), channel_id=1, source_target_pairs={{0,1},{1,2},{2,3},{3,0},{4,5},{5,6},{6,7},{7,4},{8,9},{9,10},{10,1... | collective-permute-start | bytes 1376264 | tf_op jit(solution)/shard_map/ppermute | solution.py:253
  106.0 27.5 %collective-permute-start.11 = (bf16[4,4,112,128]{3,2,1,0:T(8,128)(2,1)S(1)}, bf16[4,4,112,128]{3,2,1,0:T(8,128)(2,1)S(1)}, u32[]{:S(2)}, u32[]{:S(2)}) collective-permute-start(bf16[4,4,112,128]{3,2,1,0:T(8,128)(2,1)S(1)} %slice.31), channel_id=1, source_target_pairs={{0,3},{1,0},{2,1},{3,2},{4,7},{5,4},{6,5},{7,6},{8,11},{9,8},{10,9... | collective-permute-start | bytes 1376264 | tf_op jit(solution)/shard_map/ppermute | solution.py:254
  110.4 0.8 copy-start.6
  133.5 0.8 copy-start.7
  134.3 9.5 %copy-start.9 = (f32[16,128]{1,0:T(8,128)S(1)}, f32[16,128]{1,0:T(8,128)}, u32[]{:S(2)}) copy-start(f32[16,128]{1,0:T(8,128)} %get-tuple-element.27) | copy-start | bytes 24580
  163.6 6.4 %collective-permute-start.12 = (f32[1,8]{1,0:T(1,128)S(1)}, f32[1,8]{1,0:T(1,128)S(1)}, u32[]{:S(2)}, u32[]{:S(2)}) collective-permute-start(f32[1,8]{1,0:T(1,128)S(1)} %bitcast.78), channel_id=1, source_target_pairs={{0,128},{128,0},{1,129},{129,1},{2,130},{130,2},{3,131},{131,3},{4... | collective-permute-start | bytes 104 | tf_op jit(solution)/shard_map/ppermute | solution.py:359

commit v6 on v5

--- a/solution.py
+++ b/solution.py
@@ -147,14 +147,23 @@
         scores_of(grams, weighted, totals, out_ref)
 
 
-def last_kernel(place_ref, low_ref, high_ref, near_ref, far_ref, weighted_ref, out_ref, grams, totals):
+def last_kernel(
+    place_ref, part_ref, near_ref, far_ref, weighted_ref, out_ref, grams, weighted, totals, arrived
+):
     step = pl.program_id(0)
     steps = pl.num_programs(0)
-    grams_of(step, steps, place_ref, [low_ref, high_ref], near_ref, far_ref, grams)
+    load = pltpu.make_async_copy(weighted_ref, weighted, arrived)
+
+    @pl.when(step == 0)
+    def _():
+        load.start()
+
+    grams_of(step, steps, place_ref, [part_ref], near_ref, far_ref, grams)
 
     @pl.when(step == steps - 1)
     def _():
-        scores_of(grams, weighted_ref, totals, out_ref)
+        load.wait()
+        scores_of(grams, weighted, totals, out_ref)
 
 
 def per_device(
@@ -247,12 +256,9 @@
     own_query = chosen + lax.ppermute(chosen, "dp", shifted(flip_z=1))
 
     ring = range(model_size)
-    shifts = [[(i, (i + s) % model_size) for i in ring] for s in (1, model_size - 1, 2)]
-    grad_parts = [own_grads] + [lax.ppermute(own_grads, "mp", pairs) for pairs in shifts[:2]]
-    opposite = [
-        lax.ppermute(grad_parts[1][:, :, :piece], "mp", shifts[0]),
-        lax.ppermute(grad_parts[2][:, :, piece:], "mp", shifts[1]),
-    ]
+    shifts = [[(i, (i + s) % model_size) for i in ring] for s in (1, model_size - 1)]
+    grad_parts = [own_grads] + [lax.ppermute(own_grads, "mp", pairs) for pairs in shifts]
+    opposite = lax.ppermute(grad_parts[1], "mp", shifts[0])
     own_query = jnp.broadcast_to(own_query[None], (model_size,) + own_query.shape)
     query_parts = lax.all_to_all(own_query, "mp", split_axis=0, concat_axis=0, tiled=True)
     model_index = lax.axis_index("mp")
@@ -281,7 +287,6 @@
     blocks = piece // ROWS
     early = model_size - 1
     part_block = (1,) + own_grads.shape[1:]
-    half_block = (1,) + opposite[0].shape[1:]
     acts_block = (1, 2, tokens, act_cols)
     weighted_shape = (2 * blocks, queries * ROWS, act_cols)
     total_shape = (targets * ROWS, queries * ROWS)
@@ -328,22 +333,24 @@
             num_scalar_prefetch=1,
             grid=(width,),
             in_specs=[
-                *[pl.BlockSpec(half_block, lambda s, place: (x_of(place, s), 0, 0, 0))] * 2,
+                pl.BlockSpec(part_block, lambda s, place: (x_of(place, s), 0, 0, 0)),
                 pl.BlockSpec(acts_block, lambda s, place: (s, 0, 0, 0)),
                 pl.BlockSpec(acts_block, lambda s, place: (s, 0, 0, 0)),
-                pl.BlockSpec(weighted_shape, lambda s, place: (0, 0, 0)),
+                pl.BlockSpec(memory_space=pl.ANY),
             ],
             out_specs=pl.BlockSpec(score_shape.shape, lambda s, place: (0, 0)),
             scratch_shapes=[
                 pltpu.VMEM((2 * blocks, targets * ROWS, act_cols), bf16),
+                pltpu.VMEM(weighted_shape, bf16),
                 pltpu.VMEM(total_shape, jnp.float32),
+                pltpu.SemaphoreType.DMA,
             ],
         ),
         out_shape=score_shape,
         compiler_params=pltpu.CompilerParams(vmem_limit_bytes=60 * MIB),
         cost_estimate=pl.CostEstimate(flops=work, bytes_accessed=9 * MIB, transcendentals=0),
         name="last_scores",
-    )(place, *opposite, near, far, last_weighted)
+    )(place, opposite, near, far, last_weighted)
     scores = early_scores + last_scores
     partial = scores.reshape(targets, queries, ROWS).sum(axis=2)
 

time: 171 us -> 170 us (level)
  waiting for transfers between devices: 51.2 us -> 56 us
  starting transfers between devices: 38.5 us -> 35.5 us
  local copies, waits for them, and re-layouts: 12.5 us -> 10.5 us
    all_to_all x1, waiting for transfers between devices: 0.58 us -> 4.02 us  [per_device(): lax.all_to_all(own_query, 'mp', split_axis=0, concat_axis=0, tiled=True)]
    ppermute x2 -> x1, starting transfers between devices: 2.99 us -> 0.01 us  [per_device(): opposite = lax.ppermute(grad_parts[1], 'mp', shifts[0])]
    slice x2 -> x0, local copies, waits for them, and re-layouts: 2.11 us -> none  [the longest x1 1.06 us: per_device(): grad_parts[2][:, :, piece:]]
  transfers between devices with their start and end apart: 15 -> 14, of which waited for: 6 -> 6; matrix products, arithmetic and copies ran while one was open for 8% -> 7% of each run, Pallas kernels for 17% -> 17%
where the time goes in v6:
time: 170 us; the launch traced here: 169 us
  waiting for transfers between devices  56 us (33%)
  Pallas kernels  40.5 us (24%)
  starting transfers between devices  35.5 us (21%)
  blocking collectives  18 us (11%)
  local copies, waits for them, and re-layouts  10.5 us (6%)
  other arithmetic  8.3 us (5%)
    ppermute x1, waiting for transfers between devices, per_device(): lax.ppermute(eigen_values[0].astype(bf16), 'dp', shifted(flip_z=1))  26.4 us
    pallas_call x1, Pallas kernels, per_device(): pl.pallas_call(functools.partial(first_kernel, length), grid_spec=pltpu.P...  22.3 us
    all_to_all x1, blocking collectives, per_device(): lax.all_to_all(rows, ('dp', 'mp'), split_axis=0, concat_axis=0, tiled=True)  18 us
    pallas_call x1, Pallas kernels, per_device(): pl.pallas_call(last_kernel, grid_spec=pltpu.PrefetchScalarGridSpec(num_sc...  8.92 us
    ppermute x3, waiting for transfers between devices, per_device(): lax.ppermute(pair, 'dp', shifted(dx=s))  8.51 us
    ppermute x2, waiting for transfers between devices, per_device(): lax.ppermute(own_grads, 'mp', pairs)  8.45 us
    pallas_call x1, Pallas kernels, per_device(): pl.pallas_call(turn_grads_kernel, grid=(steps,), in_specs=[pl.BlockSpec((...  7 us
    ppermute x1, waiting for transfers between devices, per_device(): other_acts = lax.ppermute(turned_acts, 'dp', shifted(dz=2))  6.98 us
  transfers between devices with their start and end apart: 14, of which 6 were waited for; matrix products, arithmetic and copies ran while one was open for 7% of the time, Pallas kernels for 17%

profile of v6, /device:TPU:1, one launch (start us, length us, event | category | flops | bytes accessed | tf_op | source)
XLA Modules:
  0.0 169.3 jit_solution(16927981348564583408)
XLA Ops:
  0.0 2.3 %turn_acts.1 = bf16[160,1024]{1,0:T(8,128)(2,1)} custom-call(bf16[128,1024]{1,0:T(8,128)(2,1)} %bitcast.72, bf16[32,1024]{1,0:T(8,128)(2,1)} %bitcast.76, bf16[1024,512]{1,0:T(8,128)(2,1)} %bitcast.62), custom_call_target="tpu_custom_call" | custom-call | tf_op jit(solution)/shard_map/turn_acts/pallas_call | solution.py:182
  2.3 3.8 %collective-permute-start = (bf16[160,1024]{1,0:T(8,128)(2,1)}, bf16[160,1024]{1,0:T(8,128)(2,1)S(1)}, u32[]{:S(2)}, u32[]{:S(2)}) collective-permute-start(bf16[160,1024]{1,0:T(8,128)(2,1)} %turn_acts.1), channel_id=1, source_target_pairs={{0,16},{4,20},{8,24},{12,28},{16,0},{20,4},{24,8},{28,12},{32,48},... | collective-permute-start | bytes 983048 | tf_op jit(solution)/shard_map/ppermute | solution.py:214
  6.2 7.0 %turn_grads.1 = bf16[16,288,128]{2,1,0:T(8,128)(2,1)} custom-call(bf16[128,3584]{1,0:T(8,128)(2,1)} %bitcast.66, bf16[32,3584]{1,0:T(8,128)(2,1)} %bitcast.73, bf16[3584,512]{1,0:T(8,128)(2,1)} %bitcast.54), custom_call_target="tpu_custom_call" | custom-call | tf_op jit(solution)/shard_map/turn_grads/pallas_call | solution.py:218
  13.2 7.0 %collective-permute-done = bf16[160,1024]{1,0:T(8,128)(2,1)S(1)} collective-permute-done((bf16[160,1024]{1,0:T(8,128)(2,1)}, bf16[160,1024]{1,0:T(8,128)(2,1)S(1)}, u32[]{:S(2)}, u32[]{:S(2)}) %collective-permute-start) | collective-permute-done | bytes 327712 | tf_op jit(solution)/shard_map/ppermute | solution.py:214
  20.1 6.2 %all-to-all-start = ((bf16[16,288,128]{2,1,0:T(8,128)(2,1)}), bf16[16,288,128]{2,1,0:T(8,128)(2,1)S(1)}, u32[]{:S(2)}, u32[]{:S(2)}) async-start(bf16[16,288,128]{2,1,0:T(8,128)(2,1)} %turn_grads.1), calls=%async_computation | async-start | bytes 2359296 | tf_op jit(solution)/shard_map/all_to_all | solution.py:237
  26.4 0.0 copy-done.2
  26.4 0.1 bitcast_convert_fusion
  26.5 3.4 %collective-permute-start.1 = (bf16[4,112,1024]{2,1,0:T(8,128)(2,1)S(1)}, bf16[4,112,1024]{2,1,0:T(8,128)(2,1)S(1)}, u32[]{:S(2)}, u32[]{:S(2)}) collective-permute-start(bf16[4,112,1024]{2,1,0:T(8,128)(2,1)S(1)} %bitcast_convert_fusion), channel_id=1, source_target_pairs={{0,8},{4,12},{8,0},{12,4},{16,24},{20,28},{24,16},{28,20},{32,40},... | collective-permute-start | bytes 2752520 | tf_op jit(solution)/shard_map/ppermute | solution.py:212
  29.9 1.1 pad_maximum_fusion.2
  31.0 1.4 collective-permute-start.2
  32.5 2.4 %collective-permute-start.3 = (bf16[2,160,1024]{2,1,0:T(8,128)(2,1)S(1)}, bf16[2,160,1024]{2,1,0:T(8,128)(2,1)S(1)}, u32[]{:S(2)}, u32[]{:S(2)}) collective-permute-start(bf16[2,160,1024]{2,1,0:T(8,128)(2,1)S(1)} %pad_maximum_fusion.2), channel_id=1, source_target_pairs={{0,64},{4,68},{8,72},{12,76},{16,80},{20,84},{24,88},{28,92},{32,9... | collective-permute-start | bytes 1966088 | tf_op jit(solution)/shard_map/ppermute | solution.py:240
  34.9 1.2 collective-permute-start.4
  36.0 26.4 %collective-permute-done.1.refs_3_ = bf16[4,112,1024]{2,1,0:T(8,128)(2,1)S(1)} collective-permute-done((bf16[4,112,1024]{2,1,0:T(8,128)(2,1)S(1)}, bf16[4,112,1024]{2,1,0:T(8,128)(2,1)S(1)}, u32[]{:S(2)}, u32[]{:S(2)}) %collective-permute-start.1) | collective-permute-done | bytes 917536 | tf_op jit(solution)/shard_map/ppermute | solution.py:212
  62.4 0.0 collective-permute-done.2
  62.4 8.5 %collective-permute-done.3 = bf16[2,160,1024]{2,1,0:T(8,128)(2,1)S(1)} collective-permute-done((bf16[2,160,1024]{2,1,0:T(8,128)(2,1)S(1)}, bf16[2,160,1024]{2,1,0:T(8,128)(2,1)S(1)}, u32[]{:S(2)}, u32[]{:S(2)}) %collective-permute-start.3) | collective-permute-done | bytes 655392 | tf_op jit(solution)/shard_map/ppermute | solution.py:240
  71.0 0.0 collective-permute-done.4
  71.0 0.0 all-to-all-done
  71.0 0.8 copy-done.6
  71.8 0.4 copy-done.1
  72.2 1.9 %pad_maximum_fusion.refs_7_.near_ref = bf16[4,2,160,1024]{3,2,1,0:T(8,128)(2,1)S(1)} fusion(bf16[1,2,160,1024]{3,2,1,0:T(8,128)(2,1)} %bitcast.35, bf16[1,2,160,1024]{3,2,1,0:T(8,128)(2,1)} %bitcast.68, bf16[1,2,160,1024]{3,2,1,0:T(8,128)(2,1)} %bitcast.67, bf16[1,2,160,1024]{3,2,1,0:T(8,128)(2,1)S(1)} %bitcast.55), kind=kLoop, calls=%fused_computation.2 | loop fusion | flops 3932160 | bytes 5242880 | tf_op jit(solution)/shard_map/stack | solution.py:244
  74.1 0.0 copy-start
  74.1 1.0 collective-permute-start.6
  75.1 0.0 slice-done
  75.2 0.6 gather_fusion
  75.7 0.1 select_bitcast_fusion
  75.8 0.1 copy.11
  76.0 3.4 %collective-permute-start.5 = (bf16[256,256]{1,0:T(8,128)(2,1)S(1)}, bf16[256,256]{1,0:T(8,128)(2,1)S(1)}, u32[]{:S(2)}, u32[]{:S(2)}) collective-permute-start(bf16[256,256]{1,0:T(8,128)(2,1)S(1)} %bitcast.74), channel_id=1, source_target_pairs={{0,8},{4,12},{8,0},{12,4},{16,24},{20,28},{24,16},{28,20},{32,40},... | collective-permute-start | bytes 393224 | tf_op jit(solution)/shard_map/ppermute | solution.py:256
  79.3 1.2 slice.15
  80.6 1.4 collective-permute-start.8
  82.0 1.5 collective-permute-start.9
  83.6 0.0 collective-permute-done.5
  83.6 0.7 fusion.4
  84.2 0.0 collective-permute-done.6.refs_8_.far_ref
  84.2 1.1 slice.21
  85.3 1.1 pad_maximum_fusion.1
  86.4 1.8 %gather_fusion.1 = bf16[8,32,1024]{2,1,0:T(8,128)(2,1)S(1)} fusion(bf16[16,32,1024]{2,1,0:T(8,128)(2,1)} %bitcast.56, s32[1024]{0:T(1024)S(1)} %pad_clamp_fusion), kind=kCustom, calls=%fused_computation.1 | custom fusion | bytes 1048608 | tf_op jit(solution)/shard_map/jit(_take)/gather | solution.py:282
  88.3 0.1 select_select_fusion
  88.4 1.8 %broadcast_in_dim.99 = bf16[4,256,256]{2,1,0:T(8,128)(2,1)} broadcast(bf16[256,256]{1,0:T(8,128)(2,1)} %fusion.4), dimensions={1,2} | broadcast | bytes 655360 | tf_op jit(solution)/shard_map/broadcast_in_dim | solution.py:262
  90.2 0.8 collective-permute-start.7
  91.0 4.3 %all-to-all-start.1 = ((bf16[4,256,256]{2,1,0:T(8,128)(2,1)}), bf16[4,256,256]{2,1,0:T(8,128)(2,1)S(1)}, u32[]{:S(2)}, u32[]{:S(2)}) async-start(bf16[4,256,256]{2,1,0:T(8,128)(2,1)} %broadcast_in_dim.99), calls=%async_computation.1 | async-start | bytes 1048576 | tf_op jit(solution)/shard_map/all_to_all | solution.py:263
  95.3 8.4 %collective-permute-done.8.refs_5_ = bf16[4,4,224,128]{3,2,1,0:T(8,128)(2,1)} collective-permute-done((bf16[4,4,224,128]{3,2,1,0:T(8,128)(2,1)S(1)}, bf16[4,4,224,128]{3,2,1,0:T(8,128)(2,1)}, u32[]{:S(2)}, u32[]{:S(2)}) %collective-permute-start.8) | collective-permute-done | bytes 917536 | tf_op jit(solution)/shard_map/ppermute | solution.py:260
  103.7 0.0 collective-permute-start.10
  103.9 0.1 broadcast_in_dim.91
  104.0 0.1 broadcast_in_dim.92
  104.1 0.6 stack.115.place_ref
  104.7 0.7 pad_add_fusion.order_ref
  105.4 0.0 collective-permute-done.7
  105.4 0.9 bitcast_add_fusion.refs_1_
  106.3 4.0 %all-to-all-done.1.refs_0_ = bf16[4,256,256]{2,1,0:T(8,128)(2,1)S(1)} async-done(((bf16[4,256,256]{2,1,0:T(8,128)(2,1)}), bf16[4,256,256]{2,1,0:T(8,128)(2,1)S(1)}, u32[]{:S(2)}, u32[]{:S(2)}) %all-to-all-start.1) | async-done | bytes 524320 | tf_op jit(solution)/shard_map/all_to_all | solution.py:263
  110.4 0.0 collective-permute-done.9.refs_6_
  110.4 0.8 copy-done.7
  111.2 22.3 %first_scores.1 = (f32[16,128]{1,0:T(8,128)}, bf16[14,128,1024]{2,1,0:T(8,128)(2,1)}) custom-call(s32[4]{0:T(128)} %pad_add_fusion.order_ref, s32[17]{0:T(128)} %stack.115.place_ref, bf16[4,256,256]{2,1,0:T(8,128)(2,1)} %copy-done.7, bf16[256,1024]{1,0:T(8,128)(2,1)} %bitcast_add_fusion.refs_1_, f32[4,112,1024]{2,1,0:T(8,128)} %bitcast.58, ...), custom_call_target="tpu_custom_call" | custom-call | flops 5637144576 | bytes 16777216 | tf_op jit(solution)/shard_map/first_scores/pallas_call | solution.py:299
  133.4 0.0 collective-permute-done.10.part_ref
  133.4 0.9 copy-done.3
  134.4 8.9 %last_scores.1 = f32[16,128]{1,0:T(8,128)} custom-call(s32[17]{0:T(128)} %stack.115.place_ref, bf16[4,4,224,128]{3,2,1,0:T(8,128)(2,1)} %copy-done.3, bf16[4,2,160,1024]{3,2,1,0:T(8,128)(2,1)} %copy-done, bf16[4,2,160,1024]{3,2,1,0:T(8,128)(2,1)} %collective-permute-done.6.refs_8_.far_ref, bf16[14,128,1024]{2,1,0:T(8,128)(2,1)} %get-tuple-element.28.weighted_ref), custom_call_target="tpu_custom_call" | custom-call | flops 1879048192 | bytes 9437184 | tf_op jit(solution)/shard_map/last_scores/pallas_call | solution.py:330
  143.3 0.7 add.336
  144.0 0.1 reshape.60
  144.1 0.1 reduce_sum.18
  144.2 0.1 broadcast_select_fusion
  144.3 18.0 %all_to_all.19 = f32[128,1,8]{2,1,0:T(1,128)S(1)} all-to-all(f32[128,1,8]{2,1,0:T(1,128)S(1)} %bitcast.71), channel_id=1, replica_groups=mesh['section'=2,'dp'=32,'mp'=4] {'dp','mp'}, dimensions={0} | all-to-all | bytes 8192 | tf_op jit(solution)/shard_map/all_to_all | solution.py:362
  162.3 0.2 reduce_sum.19
  162.4 4.8 %collective-permute-start.11 = (f32[1,8]{1,0:T(1,128)S(1)}, f32[1,8]{1,0:T(1,128)S(1)}, u32[]{:S(2)}, u32[]{:S(2)}) collective-permute-start(f32[1,8]{1,0:T(1,128)S(1)} %bitcast.78), channel_id=1, source_target_pairs={{0,128},{128,0},{1,129},{129,1},{2,130},{130,2},{3,131},{131,3},{4... | collective-permute-start | bytes 104 | tf_op jit(solution)/shard_map/ppermute | solution.py:366
  167.2 1.6 collective-permute-done.11
  168.8 0.5 add_multiply_fusion
  (28 shorter events, 0.2 us)
Async XLA Ops:
  2.3 17.8 %collective-permute-start = (bf16[160,1024]{1,0:T(8,128)(2,1)}, bf16[160,1024]{1,0:T(8,128)(2,1)S(1)}, u32[]{:S(2)}, u32[]{:S(2)}) collective-permute-start(bf16[160,1024]{1,0:T(8,128)(2,1)} %turn_acts.1), channel_id=1, source_target_pairs={{0,16},{4,20},{8,24},{12,28},{16,0},{20,4},{24,8},{28,12},{32,48},... | collective-permute-start | bytes 983048 | tf_op jit(solution)/shard_map/ppermute | solution.py:214
  13.2 13.2 %copy-start.2 = (f32[1,4,112,1024]{3,2,1,0:T(8,128)S(1)}, f32[1,4,112,1024]{3,2,1,0:T(8,128)}, u32[]{:S(2)}) copy-start(f32[1,4,112,1024]{3,2,1,0:T(8,128)} %param.12) | copy-start | bytes 5505028
  20.1 9.7 %copy-start.8 = (bf16[160,1024]{1,0:T(8,128)(2,1)}, bf16[160,1024]{1,0:T(8,128)(2,1)S(1)}, u32[]{:S(2)}) copy-start(bf16[160,1024]{1,0:T(8,128)(2,1)S(1)} %collective-permute-done) | copy-start | bytes 983044
  20.1 50.8 %all-to-all-start = ((bf16[16,288,128]{2,1,0:T(8,128)(2,1)}), bf16[16,288,128]{2,1,0:T(8,128)(2,1)S(1)}, u32[]{:S(2)}, u32[]{:S(2)}) async-start(bf16[16,288,128]{2,1,0:T(8,128)(2,1)} %turn_grads.1), calls=%async_computation | async-start | bytes 2359296 | tf_op jit(solution)/shard_map/all_to_all | solution.py:237
  26.5 35.9 %collective-permute-start.1 = (bf16[4,112,1024]{2,1,0:T(8,128)(2,1)S(1)}, bf16[4,112,1024]{2,1,0:T(8,128)(2,1)S(1)}, u32[]{:S(2)}, u32[]{:S(2)}) collective-permute-start(bf16[4,112,1024]{2,1,0:T(8,128)(2,1)S(1)} %bitcast_convert_fusion), channel_id=1, source_target_pairs={{0,8},{4,12},{8,0},{12,4},{16,24},{20,28},{24,16},{28,20},{32,40},... | collective-permute-start | bytes 2752520 | tf_op jit(solution)/shard_map/ppermute | solution.py:212
  31.0 31.4 %collective-permute-start.2 = (bf16[2,160,1024]{2,1,0:T(8,128)(2,1)S(1)}, bf16[2,160,1024]{2,1,0:T(8,128)(2,1)S(1)}, u32[]{:S(2)}, u32[]{:S(2)}) collective-permute-start(bf16[2,160,1024]{2,1,0:T(8,128)(2,1)S(1)} %pad_maximum_fusion.2), channel_id=1, source_target_pairs={{0,32},{4,36},{8,40},{12,44},{16,48},{20,52},{24,56},{28,60},{32,6... | collective-permute-start | bytes 1966088 | tf_op jit(solution)/shard_map/ppermute | solution.py:240
  32.5 38.5 %collective-permute-start.3 = (bf16[2,160,1024]{2,1,0:T(8,128)(2,1)S(1)}, bf16[2,160,1024]{2,1,0:T(8,128)(2,1)S(1)}, u32[]{:S(2)}, u32[]{:S(2)}) collective-permute-start(bf16[2,160,1024]{2,1,0:T(8,128)(2,1)S(1)} %pad_maximum_fusion.2), channel_id=1, source_target_pairs={{0,64},{4,68},{8,72},{12,76},{16,80},{20,84},{24,88},{28,92},{32,9... | collective-permute-start | bytes 1966088 | tf_op jit(solution)/shard_map/ppermute | solution.py:240
  34.9 36.1 %collective-permute-start.4 = (bf16[2,160,1024]{2,1,0:T(8,128)(2,1)S(1)}, bf16[2,160,1024]{2,1,0:T(8,128)(2,1)}, u32[]{:S(2)}, u32[]{:S(2)}) collective-permute-start(bf16[2,160,1024]{2,1,0:T(8,128)(2,1)S(1)} %pad_maximum_fusion.2), channel_id=1, source_target_pairs={{0,96},{4,100},{8,104},{12,108},{16,112},{20,116},{24,120},{28,124... | collective-permute-start | bytes 1966088 | tf_op jit(solution)/shard_map/ppermute | solution.py:240
  62.4 8.5 %copy-start.11 = (bf16[4,112,1024]{2,1,0:T(8,128)(2,1)}, bf16[4,112,1024]{2,1,0:T(8,128)(2,1)S(1)}, u32[]{:S(2)}) copy-start(bf16[4,112,1024]{2,1,0:T(8,128)(2,1)S(1)} %collective-permute-done.1.refs_3_) | copy-start | bytes 2752516
  62.4 8.5 %copy-start.5 = (bf16[2,160,1024]{2,1,0:T(8,128)(2,1)}, bf16[2,160,1024]{2,1,0:T(8,128)(2,1)S(1)}, u32[]{:S(2)}) copy-start(bf16[2,160,1024]{2,1,0:T(8,128)(2,1)S(1)} %collective-permute-done.2) | copy-start | bytes 1966084
  71.0 0.8 copy-start.6
  71.0 1.3 copy-start.1
  72.2 2.8 %copy-start.10 = (s32[8]{0:T(128)S(1)}, s32[8]{0:T(128)}, u32[]{:S(2)}) copy-start(s32[8]{0:T(128)} %param.15) | copy-start | bytes 100
  72.2 2.9 %slice-start = ((bf16[16,288,128]{2,1,0:T(8,128)(2,1)}), bf16[16,64,128]{2,1,0:T(8,128)(2,1)S(1)}, s32[]{:S(2)}) async-start(bf16[16,288,128]{2,1,0:T(8,128)(2,1)} %copy-done.1), calls=%async_computation.3 | async-start | bytes 524288 | tf_op jit(solution)/shard_map/slice | solution.py:252
  74.1 11.2 %copy-start = (bf16[4,2,160,1024]{3,2,1,0:T(8,128)(2,1)}, bf16[4,2,160,1024]{3,2,1,0:T(8,128)(2,1)S(1)}, u32[]{:S(2)}) copy-start(bf16[4,2,160,1024]{3,2,1,0:T(8,128)(2,1)S(1)} %pad_maximum_fusion.refs_7_.near_ref) | copy-start | bytes 7864324
  74.1 10.1 %collective-permute-start.6 = (bf16[4,2,160,1024]{3,2,1,0:T(8,128)(2,1)S(1)}, bf16[4,2,160,1024]{3,2,1,0:T(8,128)(2,1)}, u32[]{:S(2)}, u32[]{:S(2)}) collective-permute-start(bf16[4,2,160,1024]{3,2,1,0:T(8,128)(2,1)S(1)} %pad_maximum_fusion.refs_7_.near_ref), channel_id=1, source_target_pairs={{0,4},{4,0},{8,12},{12,8},{16,20},{20,16},{24,28},{28,24},{32,36},... | collective-permute-start | bytes 7864328 | tf_op jit(solution)/shard_map/ppermute | solution.py:268
  76.0 7.6 %collective-permute-start.5 = (bf16[256,256]{1,0:T(8,128)(2,1)S(1)}, bf16[256,256]{1,0:T(8,128)(2,1)S(1)}, u32[]{:S(2)}, u32[]{:S(2)}) collective-permute-start(bf16[256,256]{1,0:T(8,128)(2,1)S(1)} %bitcast.74), channel_id=1, source_target_pairs={{0,8},{4,12},{8,0},{12,4},{16,24},{20,28},{24,16},{28,20},{32,40},... | collective-permute-start | bytes 393224 | tf_op jit(solution)/shard_map/ppermute | solution.py:256
  80.6 7.7 %copy-start.4 = (bf16[16,224,128]{2,1,0:T(8,128)(2,1)}, bf16[16,224,128]{2,1,0:T(8,128)(2,1)S(1)}, u32[]{:S(2)}) copy-start(bf16[16,224,128]{2,1,0:T(8,128)(2,1)S(1)} %slice.15) | copy-start | bytes 2752516
  80.6 23.1 %collective-permute-start.8 = (bf16[4,4,224,128]{3,2,1,0:T(8,128)(2,1)S(1)}, bf16[4,4,224,128]{3,2,1,0:T(8,128)(2,1)}, u32[]{:S(2)}, u32[]{:S(2)}) collective-permute-start(bf16[4,4,224,128]{3,2,1,0:T(8,128)(2,1)S(1)} %bitcast.63), channel_id=1, source_target_pairs={{0,1},{1,2},{2,3},{3,0},{4,5},{5,6},{6,7},{7,4},{8,9},{9,10},{10,1... | collective-permute-start | bytes 2752520 | tf_op jit(solution)/shard_map/ppermute | solution.py:260
  82.0 28.3 %collective-permute-start.9 = (bf16[4,4,224,128]{3,2,1,0:T(8,128)(2,1)S(1)}, bf16[4,4,224,128]{3,2,1,0:T(8,128)(2,1)}, u32[]{:S(2)}, u32[]{:S(2)}) collective-permute-start(bf16[4,4,224,128]{3,2,1,0:T(8,128)(2,1)S(1)} %bitcast.64), channel_id=1, source_target_pairs={{0,3},{1,0},{2,1},{3,2},{4,7},{5,4},{6,5},{7,6},{8,11},{9,8},{10,9... | collective-permute-start | bytes 2752520 | tf_op jit(solution)/shard_map/ppermute | solution.py:260
  90.2 15.2 %collective-permute-start.7 = (bf16[256,1024]{1,0:T(8,128)(2,1)S(1)}, bf16[256,1024]{1,0:T(8,128)(2,1)S(1)}, u32[]{:S(2)}, u32[]{:S(2)}) collective-permute-start(bf16[256,1024]{1,0:T(8,128)(2,1)S(1)} %bitcast.57), channel_id=1, source_target_pairs={{0,8},{4,12},{8,0},{12,4},{16,24},{20,28},{24,16},{28,20},{32,40},... | collective-permute-start | bytes 1572872 | tf_op jit(solution)/shard_map/ppermute | solution.py:285
  91.0 19.4 %all-to-all-start.1 = ((bf16[4,256,256]{2,1,0:T(8,128)(2,1)}), bf16[4,256,256]{2,1,0:T(8,128)(2,1)S(1)}, u32[]{:S(2)}, u32[]{:S(2)}) async-start(bf16[4,256,256]{2,1,0:T(8,128)(2,1)} %broadcast_in_dim.99), calls=%async_computation.1 | async-start | bytes 1048576 | tf_op jit(solution)/shard_map/all_to_all | solution.py:263
  103.7 29.7 %collective-permute-start.10 = (bf16[4,4,224,128]{3,2,1,0:T(8,128)(2,1)}, bf16[4,4,224,128]{3,2,1,0:T(8,128)(2,1)S(1)}, u32[]{:S(2)}, u32[]{:S(2)}) collective-permute-start(bf16[4,4,224,128]{3,2,1,0:T(8,128)(2,1)} %collective-permute-done.8.refs_5_), channel_id=1, source_target_pairs={{0,1},{1,2},{2,3},{3,0},{4,5},{5,6},{6,7},{7,4},{8,9},{9,10},{10,1... | collective-permute-start | bytes 2752520 | tf_op jit(solution)/shard_map/ppermute | solution.py:261
  110.4 0.8 copy-start.7
  133.4 0.9 copy-start.3
  134.4 8.9 %copy-start.9 = (f32[16,128]{1,0:T(8,128)S(1)}, f32[16,128]{1,0:T(8,128)}, u32[]{:S(2)}) copy-start(f32[16,128]{1,0:T(8,128)} %get-tuple-element.27) | copy-start | bytes 24580
  162.4 6.4 %collective-permute-start.11 = (f32[1,8]{1,0:T(1,128)S(1)}, f32[1,8]{1,0:T(1,128)S(1)}, u32[]{:S(2)}, u32[]{:S(2)}) collective-permute-start(f32[1,8]{1,0:T(1,128)S(1)} %bitcast.78), channel_id=1, source_target_pairs={{0,128},{128,0},{1,129},{129,1},{2,130},{130,2},{3,131},{131,3},{4... | collective-permute-start | bytes 104 | tf_op jit(solution)/shard_map/ppermute | solution.py:366
